TPU v7x, 32 devices: a whole 2x2x4 slice. The times are simulated.
32 devices in a mesh: blk: 16 (over z, y, core), rep: 2 (over x).
Axes of the slice: x: 2, y: 2, z: 4, core: 2. Of those that a mesh axis runs over, the one named last changes fastest.
Arguments:
- features: bfloat16 [8192, 128], P('blk'), may hold values from -6 to 6
- weight: bfloat16 [128, 256], replicated, may hold values from -0.5 to 0.5
- tile_vals: bfloat16 [16, 2, 8, 12, 128, 128], P('blk', 'rep'), may hold values from -0.078125 to 0.078125
- tile_pos: int32 [16, 2, 8, 12], P('blk', 'rep'), may hold values from 0 to 15, as said below
- tile_count: int32 [16, 2, 8], P('blk', 'rep'), may hold values from 1 to 12, as said below
- cotangent: bfloat16 [8192, 256], P(('blk', 'rep')), may hold values from -6 to 6
Outputs:
- activations: bfloat16 [8192, 256], P(('blk', 'rep'))
- feat_grad: bfloat16 [8192, 128], P(('blk', 'rep'))
- weight_grad: float32 [128, 256], replicated
Inputs may be any that keep to these rules, and one draw needn't show every extreme that they name: `tile_pos`: within one row group, copy and section the entries are distinct. `tile_count`: row group 0 has all 12 slots live in every copy and section.
All inputs are finite; a program needn't handle non-finite values.
Results may differ from a plain program's by a relative error of at most 0.014.
Values may be sent and summed in bfloat16 or wider, within the bound.
No kernel may reach another device: no remote copies, remote signals or barrier semaphores. Data moves between devices by JAX's collectives and lax.ppermute only.
A program may use at most 128 MiB of HBM per device.

v0:
```python
import jax
import jax.numpy as jnp
from jax import lax
from jax.sharding import PartitionSpec as P


def passed_along(block, axis, distance):
    devices = range(lax.axis_size(axis))
    route = [((i - distance) % len(devices), i) for i in devices]
    return lax.ppermute(block, axis, route)


def gelu_tanh(value):
    return jax.nn.gelu(value, approximate=True)


def section_forward(tile_block, positions, live_count, current, blocks):
    tile_size = tile_block.shape[-1]
    columns = current.reshape(blocks, tile_size, current.shape[-1])
    picked = columns[positions % blocks]
    live_mask = (jnp.arange(tile_block.shape[0], dtype=jnp.int32) < live_count).astype(jnp.float32)
    product = jnp.einsum("tik,tkf->tif", tile_block, picked, preferred_element_type=jnp.float32)
    product = product * live_mask[:, None, None]
    placing = (
        (positions // blocks)[:, None] == jnp.arange(blocks, dtype=jnp.int32)[None, :]
    ).astype(jnp.float32)
    return jnp.einsum("tn,tif->nif", placing, product).reshape(
        blocks * tile_size, current.shape[-1]
    )


def section_backward(tile_block, positions, live_count, grad_rows, blocks):
    tile_size = tile_block.shape[-1]
    rows_view = grad_rows.reshape(blocks, tile_size, grad_rows.shape[-1])
    picked = rows_view[positions // blocks]
    live_mask = (jnp.arange(tile_block.shape[0], dtype=jnp.int32) < live_count).astype(jnp.float32)
    product = jnp.einsum("tki,tkf->tif", tile_block, picked, preferred_element_type=jnp.float32)
    product = product * live_mask[:, None, None]
    placing = (
        (positions % blocks)[:, None] == jnp.arange(blocks, dtype=jnp.int32)[None, :]
    ).astype(jnp.float32)
    return jnp.einsum("tn,tif->nif", placing, product).reshape(
        blocks * tile_size, grad_rows.shape[-1]
    )


def skew_forward(value, rep_index, rep_size):
    for bit_index in range((rep_size - 1).bit_length()):
        moved = passed_along(value, "blk", 1 << bit_index)
        value = jnp.where(jnp.right_shift(rep_index, bit_index) % 2 == 1, moved, value)
    return value


def skew_back(value, rep_index, rep_size):
    for bit_index in range((rep_size - 1).bit_length()):
        moved = passed_along(value, "blk", -(1 << bit_index))
        value = jnp.where(jnp.right_shift(rep_index, bit_index) % 2 == 1, moved, value)
    return value


def local(features, weight, tile_vals, tile_pos, tile_count, cotangent):
    rep_size = lax.axis_size("rep")
    rep_index = lax.axis_index("rep")
    local_tiles = tile_vals[0, 0]
    local_pos = tile_pos[0, 0]
    local_count = tile_count[0, 0]
    section_count = local_tiles.shape[0]
    tile_size = local_tiles.shape[-1]
    blocks = features.shape[0] // tile_size
    rows_share = features.shape[0] // rep_size
    row_start = rep_index * rows_share

    def section_terms(section, current):
        return section_forward(
            lax.dynamic_index_in_dim(local_tiles, section, 0, keepdims=False),
            lax.dynamic_index_in_dim(local_pos, section, 0, keepdims=False),
            lax.dynamic_index_in_dim(local_count, section, 0, keepdims=False),
            current,
            blocks,
        )

    hidden = jnp.dot(features, weight, preferred_element_type=jnp.float32).astype(jnp.bfloat16)
    seeded = skew_forward(hidden, rep_index, rep_size)
    zeros_total = jnp.zeros((features.shape[0], weight.shape[1]), jnp.float32)

    def one_step(section, state):
        current, total = state
        total = total + section_terms(section, current)
        current = passed_along(current, "blk", rep_size)
        return (current, total)

    current, total = lax.fori_loop(0, section_count - 1, one_step, (seeded, zeros_total))
    total = total + section_terms(section_count - 1, current)
    pre = lax.psum_scatter(total, "rep", scatter_dimension=0, tiled=True)
    outputs, pullback = jax.vjp(gelu_tanh, pre)
    activations = outputs.astype(jnp.bfloat16)
    pre_grad = pullback(cotangent.astype(jnp.float32))[0].astype(jnp.bfloat16)
    grad_rows = lax.all_gather(pre_grad, "rep", axis=0, tiled=True)

    def back_terms(section):
        return section_backward(
            lax.dynamic_index_in_dim(local_tiles, section, 0, keepdims=False),
            lax.dynamic_index_in_dim(local_pos, section, 0, keepdims=False),
            lax.dynamic_index_in_dim(local_count, section, 0, keepdims=False),
            grad_rows,
            blocks,
        )

    def back_step(section, carried):
        return passed_along(carried + back_terms(section), "blk", rep_size)

    carried = lax.fori_loop(0, section_count, back_step, zeros_total)
    carried = skew_back(carried, rep_index, rep_size)
    hidden_grad = lax.psum_scatter(carried, "rep", scatter_dimension=0, tiled=True).astype(
        jnp.bfloat16
    )
    feat_grad = lax.dot_general(
        hidden_grad, weight, (((1,), (1,)), ((), ())), preferred_element_type=jnp.float32
    ).astype(jnp.bfloat16)
    feat_rows = lax.dynamic_slice_in_dim(features, row_start, rows_share, 0)
    partial_grad = lax.dot_general(
        feat_rows, hidden_grad, (((0,), (0,)), ((), ())), preferred_element_type=jnp.float32
    )
    weight_grad = lax.psum(partial_grad, ("blk", "rep"))
    return (activations, feat_grad, weight_grad)


def solution(mesh):
    placed = (
        P("blk", None),
        P(),
        P("blk", "rep", None, None, None, None),
        P("blk", "rep", None, None),
        P("blk", "rep", None),
        P(("blk", "rep"), None),
    )
    return jax.shard_map(
        local,
        mesh=mesh,
        in_specs=placed,
        out_specs=(P(("blk", "rep"), None), P(("blk", "rep"), None), P()),
        check_vma=False,
    )
```

profile of v0, /device:TPU:0, one launch (start us, length us, event | category | flops | bytes accessed | tf_op | source)
XLA Modules:
  0.0 430.1 jit_solution(17606837988501651629)
XLA Ops:
  13.0 5.7 %collective-permute-done.2 = bf16[512,256]{1,0:T(8,128)(2,1)S(1)} collective-permute-done((bf16[512,256]{1,0:T(8,128)(2,1)S(1)}, bf16[512,256]{1,0:T(8,128)(2,1)S(1)}, u32[]{:S(2)}, u32[]{:S(2)}) %collective-permute-start.2) | collective-permute-done | bytes 262176 | tf_op jit(solution)/shard_map/ppermute | solution.py:10
  18.7 71.0 %while.34 = (s32[]{:T(128)}, bf16[512,256]{1,0:T(8,128)(2,1)S(1)}, f32[512,256]{1,0:T(8,128)S(1)}, s32[8,12]{1,0:T(8,128)}, bf16[8,12,128,128]{3,2,1,0:T(8,128)(2,1)}, /*index=5*/s32[8]{0:T(128)}, s32[]{:T(128)}, s32[]{:T(128)}) while((s32[]{:T(128)}, bf16[512,256]{1,0:T(8,128)(2,1)S(1)}, f32[512,256]{1,0:T(8,128)S(1)}, ...), condition=%wide.region_1.2_spmd.clone, body=%wide.region_0.1_spmd.clone.sunk | while | flops 104465824 | bytes 10621531 | solution.py:92
  20.2 1.2 dynamic_slice.123
  22.7 1.3 fusion.77
  25.3 2.6 collective-permute-done.1
  29.4 1.2 dynamic_slice.123
  31.9 1.4 fusion.77
  34.4 2.6 collective-permute-done.1
  41.0 1.4 fusion.77
  43.6 3.7 collective-permute-done.1
  51.2 1.4 fusion.77
  53.8 4.9 %collective-permute-done.1 = bf16[512,256]{1,0:T(8,128)(2,1)S(1)} collective-permute-done((bf16[512,256]{1,0:T(8,128)(2,1)S(1)}, bf16[512,256]{1,0:T(8,128)(2,1)S(1)}, u32[]{:S(2)}, u32[]{:S(2)}) %collective-permute-start.1) | collective-permute-done | bytes 262176 | tf_op jit(solution)/shard_map/while/body/eval_jaxpr/ppermute | solution.py:10
  62.7 1.4 fusion.77
  65.2 4.8 %collective-permute-done.1 = bf16[512,256]{1,0:T(8,128)(2,1)S(1)} collective-permute-done((bf16[512,256]{1,0:T(8,128)(2,1)S(1)}, bf16[512,256]{1,0:T(8,128)(2,1)S(1)}, u32[]{:S(2)}, u32[]{:S(2)}) %collective-permute-start.1) | collective-permute-done | bytes 262176 | tf_op jit(solution)/shard_map/while/body/eval_jaxpr/ppermute | solution.py:10
  71.5 1.2 dynamic_slice.123
  74.0 1.3 fusion.77
  76.6 4.0 collective-permute-done.1
  84.5 1.4 fusion.77
  87.1 2.6 collective-permute-done.1
  90.3 2.6 fusion.26
  92.8 2.2 copy.14
  96.5 14.6 %reduce-scatter.3.cloned.1.call-done = f32[256,256]{1,0:T(8,128)} async-done(((f32[512,256]{1,0:T(8,128)}), f32[256,256]{1,0:T(8,128)}) %reduce-scatter.3.cloned.1.call-update) | async-done | bytes 262160 | tf_op jit(solution)/shard_map/reduce_scatter | solution.py:94
  111.1 1.8 fusion.31
  112.9 5.9 %all_gather.3 = bf16[512,256]{1,0:T(8,128)(2,1)S(1)} all-gather(bf16[256,256]{1,0:T(8,128)(2,1)S(1)} %get-tuple-element.366), channel_id=1, replica_groups=mesh['blk'=16,'rep'=2] {'rep'}, dimensions={0}, use_global_device_ids=true | all-gather | bytes 393216 | tf_op jit(solution)/shard_map/all_gather | solution.py:98
  118.9 151.0 %while.33 = (s32[]{:T(128)}, f32[512,256]{1,0:T(8,128)S(1)}, s32[8,12]{1,0:T(8,128)}, bf16[8,12,128,128]{3,2,1,0:T(8,128)(2,1)}, bf16[512,256]{1,0:T(8,128)(2,1)S(1)}, /*index=5*/s32[8]{0:T(128)S(1)}, s32[]{:T(128)}) while((s32[]{:T(128)}, f32[512,256]{1,0:T(8,128)S(1)}, s32[8,12]{1,0:T(8,128)}, bf16[8,12,128,128]{3,2,1,0:T(8,128)(2,1)}, ...), condition=%wide.region_4.5_spmd, body=%wide.region_3.4_spmd.sunk | while | flops 104334752 | bytes 11146301 | solution.py:112
  122.2 1.4 fusion.71
  124.7 1.5 collective-permute-start
  126.3 14.0 %collective-permute-done = f32[512,256]{1,0:T(8,128)S(1)} collective-permute-done((f32[512,256]{1,0:T(8,128)S(1)}, f32[512,256]{1,0:T(8,128)S(1)}, u32[]{:S(2)}, u32[]{:S(2)}) %collective-permute-start) | collective-permute-done | bytes 524320 | tf_op jit(solution)/shard_map/while/body/eval_jaxpr/ppermute | solution.py:10
  143.5 1.4 fusion.71
  146.2 14.6 %collective-permute-done = f32[512,256]{1,0:T(8,128)S(1)} collective-permute-done((f32[512,256]{1,0:T(8,128)S(1)}, f32[512,256]{1,0:T(8,128)S(1)}, u32[]{:S(2)}, u32[]{:S(2)}) %collective-permute-start) | collective-permute-done | bytes 524320 | tf_op jit(solution)/shard_map/while/body/eval_jaxpr/ppermute | solution.py:10
  164.0 1.4 fusion.71
  166.6 13.6 %collective-permute-done = f32[512,256]{1,0:T(8,128)S(1)} collective-permute-done((f32[512,256]{1,0:T(8,128)S(1)}, f32[512,256]{1,0:T(8,128)S(1)}, u32[]{:S(2)}, u32[]{:S(2)}) %collective-permute-start) | collective-permute-done | bytes 524320 | tf_op jit(solution)/shard_map/while/body/eval_jaxpr/ppermute | solution.py:10
  183.5 1.4 fusion.71
  186.1 12.7 %collective-permute-done = f32[512,256]{1,0:T(8,128)S(1)} collective-permute-done((f32[512,256]{1,0:T(8,128)S(1)}, f32[512,256]{1,0:T(8,128)S(1)}, u32[]{:S(2)}, u32[]{:S(2)}) %collective-permute-start) | collective-permute-done | bytes 524320 | tf_op jit(solution)/shard_map/while/body/eval_jaxpr/ppermute | solution.py:10
  202.1 1.4 fusion.71
  204.7 11.9 %collective-permute-done = f32[512,256]{1,0:T(8,128)S(1)} collective-permute-done((f32[512,256]{1,0:T(8,128)S(1)}, f32[512,256]{1,0:T(8,128)S(1)}, u32[]{:S(2)}, u32[]{:S(2)}) %collective-permute-start) | collective-permute-done | bytes 524320 | tf_op jit(solution)/shard_map/while/body/eval_jaxpr/ppermute | solution.py:10
  219.9 1.4 fusion.71
  222.5 11.9 %collective-permute-done = f32[512,256]{1,0:T(8,128)S(1)} collective-permute-done((f32[512,256]{1,0:T(8,128)S(1)}, f32[512,256]{1,0:T(8,128)S(1)}, u32[]{:S(2)}, u32[]{:S(2)}) %collective-permute-start) | collective-permute-done | bytes 524320 | tf_op jit(solution)/shard_map/while/body/eval_jaxpr/ppermute | solution.py:10
  237.6 1.4 fusion.71
  240.3 11.9 %collective-permute-done = f32[512,256]{1,0:T(8,128)S(1)} collective-permute-done((f32[512,256]{1,0:T(8,128)S(1)}, f32[512,256]{1,0:T(8,128)S(1)}, u32[]{:S(2)}, u32[]{:S(2)}) %collective-permute-start) | collective-permute-done | bytes 524320 | tf_op jit(solution)/shard_map/while/body/eval_jaxpr/ppermute | solution.py:10
  255.4 1.4 fusion.71
  258.0 11.9 %collective-permute-done = f32[512,256]{1,0:T(8,128)S(1)} collective-permute-done((f32[512,256]{1,0:T(8,128)S(1)}, f32[512,256]{1,0:T(8,128)S(1)}, u32[]{:S(2)}, u32[]{:S(2)}) %collective-permute-start) | collective-permute-done | bytes 524320 | tf_op jit(solution)/shard_map/while/body/eval_jaxpr/ppermute | solution.py:10
  269.9 6.7 %collective-permute-done.3 = f32[512,256]{1,0:T(8,128)S(1)} collective-permute-done((f32[512,256]{1,0:T(8,128)S(1)}, f32[512,256]{1,0:T(8,128)S(1)}, u32[]{:S(2)}, u32[]{:S(2)}) %collective-permute-start.3) | collective-permute-done | bytes 524320 | tf_op jit(solution)/shard_map/ppermute | solution.py:10
  277.5 15.8 %reduce-scatter.5.cloned.1.call-done = f32[256,256]{1,0:T(8,128)} async-done(((f32[512,256]{1,0:T(8,128)}), f32[256,256]{1,0:T(8,128)}) %reduce-scatter.5.cloned.1.call-update) | async-done | bytes 262160 | tf_op jit(solution)/shard_map/reduce_scatter | solution.py:114
  293.3 1.8 fusion.39
  295.2 1.8 convolution_convert_fusion.1
  296.9 125.0 %all-reduce.2.cloned.1.call-done = f32[128,256]{1,0:T(8,128)} async-done(((f32[128,256]{1,0:T(8,128)}), f32[128,256]{1,0:T(8,128)}) %all-reduce.2.cloned.1.call-update) | async-done | bytes 131088 | tf_op jit(solution)/shard_map/psum | solution.py:124
  422.0 1.6 copy.43
  (183 shorter events, 76.5 us)
Async XLA Ops:
  7.2 0.9 copy-start
  7.2 103.9 %reduce-scatter.3.cloned.1.call-start = ((), (), s32[]{:S(2)}) async-start(), calls=%async_computation.2 | async-start | bytes 786432 | tf_op jit(solution)/shard_map/reduce_scatter | solution.py:94
  9.1 9.5 %collective-permute-start.2 = (bf16[512,256]{1,0:T(8,128)(2,1)S(1)}, bf16[512,256]{1,0:T(8,128)(2,1)S(1)}, u32[]{:S(2)}, u32[]{:S(2)}) collective-permute-start(bf16[512,256]{1,0:T(8,128)(2,1)S(1)} %convolution_convert_fusion), channel_id=1, source_target_pairs={{30,0},{0,2},{2,4},{4,6},{6,8},{8,10},{10,12},{12,14},{14,16},{16,... | collective-permute-start | bytes 786440 | tf_op jit(solution)/shard_map/ppermute | solution.py:10
  18.7 9.1 %collective-permute-start.1 = (bf16[512,256]{1,0:T(8,128)(2,1)S(1)}, bf16[512,256]{1,0:T(8,128)(2,1)S(1)}, u32[]{:S(2)}, u32[]{:S(2)}) collective-permute-start(bf16[512,256]{1,0:T(8,128)(2,1)S(1)} %copy.31), channel_id=1, source_target_pairs={{28,0},{30,2},{0,4},{2,6},{4,8},{6,10},{8,12},{10,14},{12,16},{14,... | collective-permute-start | bytes 786440 | tf_op jit(solution)/shard_map/while/body/eval_jaxpr/ppermute | solution.py:10
  27.9 9.1 %collective-permute-start.1 = (bf16[512,256]{1,0:T(8,128)(2,1)S(1)}, bf16[512,256]{1,0:T(8,128)(2,1)S(1)}, u32[]{:S(2)}, u32[]{:S(2)}) collective-permute-start(bf16[512,256]{1,0:T(8,128)(2,1)S(1)} %copy.31), channel_id=1, source_target_pairs={{28,0},{30,2},{0,4},{2,6},{4,8},{6,10},{8,12},{10,14},{12,16},{14,... | collective-permute-start | bytes 786440 | tf_op jit(solution)/shard_map/while/body/eval_jaxpr/ppermute | solution.py:10
  37.0 10.2 %collective-permute-start.1 = (bf16[512,256]{1,0:T(8,128)(2,1)S(1)}, bf16[512,256]{1,0:T(8,128)(2,1)S(1)}, u32[]{:S(2)}, u32[]{:S(2)}) collective-permute-start(bf16[512,256]{1,0:T(8,128)(2,1)S(1)} %copy.31), channel_id=1, source_target_pairs={{28,0},{30,2},{0,4},{2,6},{4,8},{6,10},{8,12},{10,14},{12,16},{14,... | collective-permute-start | bytes 786440 | tf_op jit(solution)/shard_map/while/body/eval_jaxpr/ppermute | solution.py:10
  47.3 11.4 %collective-permute-start.1 = (bf16[512,256]{1,0:T(8,128)(2,1)S(1)}, bf16[512,256]{1,0:T(8,128)(2,1)S(1)}, u32[]{:S(2)}, u32[]{:S(2)}) collective-permute-start(bf16[512,256]{1,0:T(8,128)(2,1)S(1)} %copy.31), channel_id=1, source_target_pairs={{28,0},{30,2},{0,4},{2,6},{4,8},{6,10},{8,12},{10,14},{12,16},{14,... | collective-permute-start | bytes 786440 | tf_op jit(solution)/shard_map/while/body/eval_jaxpr/ppermute | solution.py:10
  58.7 11.3 %collective-permute-start.1 = (bf16[512,256]{1,0:T(8,128)(2,1)S(1)}, bf16[512,256]{1,0:T(8,128)(2,1)S(1)}, u32[]{:S(2)}, u32[]{:S(2)}) collective-permute-start(bf16[512,256]{1,0:T(8,128)(2,1)S(1)} %copy.31), channel_id=1, source_target_pairs={{28,0},{30,2},{0,4},{2,6},{4,8},{6,10},{8,12},{10,14},{12,16},{14,... | collective-permute-start | bytes 786440 | tf_op jit(solution)/shard_map/while/body/eval_jaxpr/ppermute | solution.py:10
  70.0 10.5 %collective-permute-start.1 = (bf16[512,256]{1,0:T(8,128)(2,1)S(1)}, bf16[512,256]{1,0:T(8,128)(2,1)S(1)}, u32[]{:S(2)}, u32[]{:S(2)}) collective-permute-start(bf16[512,256]{1,0:T(8,128)(2,1)S(1)} %copy.31), channel_id=1, source_target_pairs={{28,0},{30,2},{0,4},{2,6},{4,8},{6,10},{8,12},{10,14},{12,16},{14,... | collective-permute-start | bytes 786440 | tf_op jit(solution)/shard_map/while/body/eval_jaxpr/ppermute | solution.py:10
  80.5 9.1 %collective-permute-start.1 = (bf16[512,256]{1,0:T(8,128)(2,1)S(1)}, bf16[512,256]{1,0:T(8,128)(2,1)S(1)}, u32[]{:S(2)}, u32[]{:S(2)}) collective-permute-start(bf16[512,256]{1,0:T(8,128)(2,1)S(1)} %copy.31), channel_id=1, source_target_pairs={{28,0},{30,2},{0,4},{2,6},{4,8},{6,10},{8,12},{10,14},{12,16},{14,... | collective-permute-start | bytes 786440 | tf_op jit(solution)/shard_map/while/body/eval_jaxpr/ppermute | solution.py:10
  95.4 15.7 %copy-start.2 = (bf16[256,256]{1,0:T(8,128)(2,1)S(1)}, bf16[256,256]{1,0:T(8,128)(2,1)}, u32[]{:S(2)}) copy-start(bf16[256,256]{1,0:T(8,128)(2,1)} %param.15) | copy-start | bytes 393220
  95.5 23.3 %copy-start.3 = (s32[8]{0:T(128)S(1)}, s32[8]{0:T(128)}, u32[]{:S(2)}) copy-start(s32[8]{0:T(128)} %get-tuple-element.512) | copy-start | bytes 100
  96.4 196.9 %reduce-scatter.5.cloned.1.call-start = ((), (), s32[]{:S(2)}) async-start(), calls=%async_computation.3 | async-start | bytes 786432 | tf_op jit(solution)/shard_map/reduce_scatter | solution.py:114
  124.7 15.5 %collective-permute-start = (f32[512,256]{1,0:T(8,128)S(1)}, f32[512,256]{1,0:T(8,128)S(1)}, u32[]{:S(2)}, u32[]{:S(2)}) collective-permute-start(f32[512,256]{1,0:T(8,128)S(1)} %bitcast_add_fusion.5), channel_id=1, source_target_pairs={{28,0},{30,2},{0,4},{2,6},{4,8},{6,10},{8,12},{10,14},{12,16},{14,... | collective-permute-start | bytes 1572872 | tf_op jit(solution)/shard_map/while/body/eval_jaxpr/ppermute | solution.py:10
  146.1 14.6 %collective-permute-start = (f32[512,256]{1,0:T(8,128)S(1)}, f32[512,256]{1,0:T(8,128)S(1)}, u32[]{:S(2)}, u32[]{:S(2)}) collective-permute-start(f32[512,256]{1,0:T(8,128)S(1)} %bitcast_add_fusion.5), channel_id=1, source_target_pairs={{28,0},{30,2},{0,4},{2,6},{4,8},{6,10},{8,12},{10,14},{12,16},{14,... | collective-permute-start | bytes 1572872 | tf_op jit(solution)/shard_map/while/body/eval_jaxpr/ppermute | solution.py:10
  166.5 13.7 %collective-permute-start = (f32[512,256]{1,0:T(8,128)S(1)}, f32[512,256]{1,0:T(8,128)S(1)}, u32[]{:S(2)}, u32[]{:S(2)}) collective-permute-start(f32[512,256]{1,0:T(8,128)S(1)} %bitcast_add_fusion.5), channel_id=1, source_target_pairs={{28,0},{30,2},{0,4},{2,6},{4,8},{6,10},{8,12},{10,14},{12,16},{14,... | collective-permute-start | bytes 1572872 | tf_op jit(solution)/shard_map/while/body/eval_jaxpr/ppermute | solution.py:10
  186.1 12.8 %collective-permute-start = (f32[512,256]{1,0:T(8,128)S(1)}, f32[512,256]{1,0:T(8,128)S(1)}, u32[]{:S(2)}, u32[]{:S(2)}) collective-permute-start(f32[512,256]{1,0:T(8,128)S(1)} %bitcast_add_fusion.5), channel_id=1, source_target_pairs={{28,0},{30,2},{0,4},{2,6},{4,8},{6,10},{8,12},{10,14},{12,16},{14,... | collective-permute-start | bytes 1572872 | tf_op jit(solution)/shard_map/while/body/eval_jaxpr/ppermute | solution.py:10
  204.7 11.9 %collective-permute-start = (f32[512,256]{1,0:T(8,128)S(1)}, f32[512,256]{1,0:T(8,128)S(1)}, u32[]{:S(2)}, u32[]{:S(2)}) collective-permute-start(f32[512,256]{1,0:T(8,128)S(1)} %bitcast_add_fusion.5), channel_id=1, source_target_pairs={{28,0},{30,2},{0,4},{2,6},{4,8},{6,10},{8,12},{10,14},{12,16},{14,... | collective-permute-start | bytes 1572872 | tf_op jit(solution)/shard_map/while/body/eval_jaxpr/ppermute | solution.py:10
  222.4 11.9 %collective-permute-start = (f32[512,256]{1,0:T(8,128)S(1)}, f32[512,256]{1,0:T(8,128)S(1)}, u32[]{:S(2)}, u32[]{:S(2)}) collective-permute-start(f32[512,256]{1,0:T(8,128)S(1)} %bitcast_add_fusion.5), channel_id=1, source_target_pairs={{28,0},{30,2},{0,4},{2,6},{4,8},{6,10},{8,12},{10,14},{12,16},{14,... | collective-permute-start | bytes 1572872 | tf_op jit(solution)/shard_map/while/body/eval_jaxpr/ppermute | solution.py:10
  240.2 11.9 %collective-permute-start = (f32[512,256]{1,0:T(8,128)S(1)}, f32[512,256]{1,0:T(8,128)S(1)}, u32[]{:S(2)}, u32[]{:S(2)}) collective-permute-start(f32[512,256]{1,0:T(8,128)S(1)} %bitcast_add_fusion.5), channel_id=1, source_target_pairs={{28,0},{30,2},{0,4},{2,6},{4,8},{6,10},{8,12},{10,14},{12,16},{14,... | collective-permute-start | bytes 1572872 | tf_op jit(solution)/shard_map/while/body/eval_jaxpr/ppermute | solution.py:10
  258.0 11.9 %collective-permute-start = (f32[512,256]{1,0:T(8,128)S(1)}, f32[512,256]{1,0:T(8,128)S(1)}, u32[]{:S(2)}, u32[]{:S(2)}) collective-permute-start(f32[512,256]{1,0:T(8,128)S(1)} %bitcast_add_fusion.5), channel_id=1, source_target_pairs={{28,0},{30,2},{0,4},{2,6},{4,8},{6,10},{8,12},{10,14},{12,16},{14,... | collective-permute-start | bytes 1572872 | tf_op jit(solution)/shard_map/while/body/eval_jaxpr/ppermute | solution.py:10
  269.9 25.3 %copy-start.1 = (bf16[128,256]{1,0:T(8,128)(2,1)S(1)}, bf16[128,256]{1,0:T(8,128)(2,1)}, u32[]{:S(2)}) copy-start(bf16[128,256]{1,0:T(8,128)(2,1)} %param.11) | copy-start | bytes 196612
  269.9 6.7 %collective-permute-start.3 = (f32[512,256]{1,0:T(8,128)S(1)}, f32[512,256]{1,0:T(8,128)S(1)}, u32[]{:S(2)}, u32[]{:S(2)}) collective-permute-start(f32[512,256]{1,0:T(8,128)S(1)} %get-tuple-element.320), channel_id=1, source_target_pairs={{2,0},{4,2},{6,4},{8,6},{10,8},{12,10},{14,12},{16,14},{18,16},{20... | collective-permute-start | bytes 1572872 | tf_op jit(solution)/shard_map/ppermute | solution.py:10
  277.5 144.5 %all-reduce.2.cloned.1.call-start = ((), (), s32[]{:S(2)}) async-start(), calls=%async_computation.4 | async-start | bytes 262144 | tf_op jit(solution)/shard_map/psum | solution.py:124
Sparse Core Ops, SparseCore 0:
  96.6 14.5 reduce-scatter.2
  277.6 15.6 reduce-scatter.4
  299.5 122.4 all-reduce.1
where the time goes:
time: 432 us; the launch traced here: 430 us
  waiting for transfers between devices  295 us (68%)
  matrix products  42.8 us (10%)
  other arithmetic  37.9 us (9%)
  local copies, waits for them, and re-layouts  30.7 us (7%)
  between operations  13.9 us (3%)
  blocking collectives  5.91 us (1%)
    ppermute x17, waiting for transfers between devices, passed_along(): return lax.ppermute(block, axis, route)  140 us
    psum x1, waiting for transfers between devices, local(): weight_grad = lax.psum(partial_grad, ('blk', 'rep'))  125 us
    reduce_scatter x1, waiting for transfers between devices, local(): lax.psum_scatter(carried, 'rep', scatter_dimension=0, tiled=True)  15.8 us
    reduce_scatter x1, waiting for transfers between devices, local(): pre = lax.psum_scatter(total, 'rep', scatter_dimension=0, tiled=True)  14.6 us
    dot_general x8, matrix products, section_forward(): jnp.einsum('tik,tkf->tif', tile_block, picked, preferred_element_type=jnp...  12 us
    dot_general x8, matrix products, section_backward(): jnp.einsum('tki,tkf->tif', tile_block, picked, preferred_element_type=jnp...  11.3 us
    dynamic_slice x8, local copies, waits for them, and re-layouts, section_terms(): lax.dynamic_index_in_dim(local_count, section, 0, keepdims=False)  9.94 us
  transfers between devices with their start and end apart: 20, of which 20 were waited for; matrix products, arithmetic and copies ran while one was open for 12% of the time, Pallas kernels for 0%

commit v1 on v0

v1 whole, which is shorter than its diff:
```python
import functools

import jax
import jax.numpy as jnp
from jax import lax
from jax.experimental import pallas as pl
from jax.experimental.pallas import tpu as pltpu
from jax.sharding import PartitionSpec as P

AXES = ("blk", "rep")
VMEM_LIMIT = 32 * 1024 * 1024


def params():
    return pltpu.CompilerParams(vmem_limit_bytes=VMEM_LIMIT)


def in_vmem(count):
    return [pl.BlockSpec(memory_space=pltpu.VMEM)] * count


def gelu_and_slope(v):
    scale = 0.7978845608028654
    square = v * v
    t = jnp.tanh(scale * (v + 0.044715 * (square * v)))
    half = 0.5 * (1.0 + t)
    slope = half + (0.5 * scale) * v * (1.0 - t * t) * (1.0 + 3.0 * 0.044715 * square)
    return v * half, slope


def nt_dot(a, b):
    return lax.dot_general(a, b, (((1,), (1,)), ((), ())), preferred_element_type=jnp.float32)


def tn_dot(a, b):
    return lax.dot_general(a, b, (((0,), (0,)), ((), ())), preferred_element_type=jnp.float32)


def dot(a, b):
    return jnp.dot(a, b, preferred_element_type=jnp.float32)


def dense_kernel(blocks, halves, pos, count, place, flip, tiles_ref, out_ref):
    section = pl.program_id(0)
    tile = tiles_ref.shape[-1]
    per_half = blocks // halves
    out_ref[...] = jnp.zeros_like(out_ref)
    for slot in range(tiles_ref.shape[1]):
        position = pos[section, slot]
        row = lax.div(position, blocks) ^ flip[0]
        col = lax.rem(position, blocks) ^ flip[0]
        half = lax.div(col, per_half)
        row_at = pl.multiple_of(row * tile, tile)
        col_at = pl.multiple_of(lax.rem(col, per_half) * tile, tile)

        @pl.when(slot < count[section])
        def _():
            out_ref[0, half, pl.ds(row_at, tile), pl.ds(col_at, tile)] = tiles_ref[0, slot]


def dense_blocks(tiles, pos, count, place, flip, near, halves, blocks):
    sections, slots, tile = tiles.shape[0], tiles.shape[1], tiles.shape[-1]
    rows = blocks * tile
    piece = rows // halves
    grid_spec = pltpu.PrefetchScalarGridSpec(
        num_scalar_prefetch=4,
        grid=(sections,),
        in_specs=[pl.BlockSpec((1, slots, tile, tile), lambda j, *_: (j, 0, 0, 0))],
        out_specs=pl.BlockSpec(
            (1, halves, rows, piece),
            lambda j, pos, count, place, flip: (lax.rem(place[j], near), 0, 0, lax.div(place[j], near)),
        ),
    )
    return pl.pallas_call(
        functools.partial(dense_kernel, blocks, halves),
        grid_spec=grid_spec,
        out_shape=jax.ShapeDtypeStruct((near, halves, rows, sections // near * piece), jnp.bfloat16),
        compiler_params=params(),
        name="dense_blocks",
    )(pos, count, place, flip, tiles)


def aggregate_kernel(dense_ref, *refs):
    parts, (total_ref, sent_ref) = refs[:-2], refs[-2:]
    halves = dense_ref.shape[1]
    total = None
    for at, part in enumerate(parts):
        term = dot(dense_ref[at // halves, at % halves], part[...])
        total = term if total is None else total + term
    total_ref[...] = total
    sent_ref[...] = total.astype(jnp.bfloat16)


def aggregate(dense, parts):
    rows, width = dense.shape[2], parts[0].shape[1]
    return pl.pallas_call(
        aggregate_kernel,
        in_specs=in_vmem(1 + len(parts)),
        out_specs=in_vmem(2),
        out_shape=[
            jax.ShapeDtypeStruct((rows, width), jnp.float32),
            jax.ShapeDtypeStruct((rows, width), jnp.bfloat16),
        ],
        compiler_params=params(),
        name="aggregate",
    )(dense, *parts)


def turn_kernel(share, own_ref, other_ref, weight_ref, cot_ref, far_cot_ref, dense_ref,
                act_ref, g_ref, grad_ref, back_ref, *sent_refs):
    rows = own_ref.shape[0]
    weight = weight_ref[...]
    for half, cot in enumerate((cot_ref, far_cot_ref)):
        at, there = half * share, rows - share - half * share
        g = (own_ref[pl.ds(at, share)] + other_ref[pl.ds(there, share)].astype(jnp.float32)).astype(jnp.bfloat16)
        value, slope = gelu_and_slope(dot(g, weight))
        grad = (cot[...].astype(jnp.float32) * slope).astype(jnp.bfloat16)
        if half == 0:
            act_ref[...] = value.astype(jnp.bfloat16)
            g_ref[...] = g
            grad_ref[...] = grad
        back_ref[:, pl.ds(at, share)] = nt_dot(weight, grad).astype(jnp.bfloat16)
    back = back_ref[...]
    halves = dense_ref.shape[1]
    for at, sent in enumerate(sent_refs, 1):
        sent[...] = dot(back, dense_ref[at // halves, at % halves]).astype(jnp.bfloat16)


def turn(own, other, weight, cot, far_cot, dense):
    rows, width = own.shape
    share, hid = cot.shape
    near, halves, _, span = dense.shape
    bf = jnp.bfloat16
    return pl.pallas_call(
        functools.partial(turn_kernel, share),
        in_specs=in_vmem(6),
        out_specs=in_vmem(4 + near * halves - 1),
        out_shape=[
            jax.ShapeDtypeStruct((share, hid), bf),
            jax.ShapeDtypeStruct((share, width), bf),
            jax.ShapeDtypeStruct((share, hid), bf),
            jax.ShapeDtypeStruct((width, rows), bf),
        ] + [jax.ShapeDtypeStruct((width, span), bf)] * (near * halves - 1),
        compiler_params=params(),
        name="turn",
    )(own, other, weight, cot, far_cot, dense)


def kept_kernel(back_ref, dense_ref, g_ref, grad_ref, kept_ref, wg_ref):
    wg_ref[...] = tn_dot(g_ref[...], grad_ref[...])
    kept_ref[...] = dot(back_ref[...], dense_ref[0, 0])


def kept_terms(back, dense, g, grad):
    width, span, hid = back.shape[0], dense.shape[3], grad.shape[1]
    return pl.pallas_call(
        kept_kernel,
        in_specs=in_vmem(4),
        out_specs=in_vmem(2),
        out_shape=[
            jax.ShapeDtypeStruct((width, span), jnp.float32),
            jax.ShapeDtypeStruct((width, hid), jnp.float32),
        ],
        compiler_params=params(),
        name="kept_terms",
    )(back, dense, g, grad)


def near_sum_kernel(kept_ref, a_ref, b_ref, c_ref, wg_ref, *out_refs):
    width = kept_ref.shape[0]
    piece = kept_ref.shape[1] // len(out_refs)
    wg = wg_ref[...].astype(jnp.bfloat16)
    for at, out in enumerate(out_refs):
        span = pl.ds(at * piece, piece)
        total = kept_ref[:, span] + a_ref[:, span].astype(jnp.float32)
        total += b_ref[:, span].astype(jnp.float32) + c_ref[:, span].astype(jnp.float32)
        out[0:width, :] = total.astype(jnp.bfloat16)
        out[width:, :] = wg


def near_sum(kept, parts, wg, far):
    width, span = kept.shape
    return pl.pallas_call(
        near_sum_kernel,
        in_specs=in_vmem(5),
        out_specs=in_vmem(far),
        out_shape=[jax.ShapeDtypeStruct((width + wg.shape[0], span // far), jnp.bfloat16)] * far,
        compiler_params=params(),
        name="near_sum",
    )(kept, *parts, wg)


def far_sum_kernel(*refs):
    parts, (feat_ref, wg_ref) = refs[:-2], refs[-2:]
    width = feat_ref.shape[1]
    terms = [part[...].astype(jnp.float32) for part in parts]
    while len(terms) > 1:
        terms = [terms[i] + terms[i + 1] for i in range(0, len(terms), 2)]
    feat_ref[...] = terms[0][0:width].T.astype(jnp.bfloat16)
    wg_ref[...] = terms[0][width:]


def far_sum(parts, width):
    total, piece = parts[0].shape
    return pl.pallas_call(
        far_sum_kernel,
        in_specs=in_vmem(len(parts)),
        out_specs=in_vmem(2),
        out_shape=[
            jax.ShapeDtypeStruct((piece, width), jnp.bfloat16),
            jax.ShapeDtypeStruct((total - width, piece), jnp.float32),
        ],
        compiler_params=params(),
        name="far_sum",
    )(*parts)


class Layout:
    def __init__(self, n_blk, reps):
        self.n_blk, self.reps = n_blk, reps

    def route(self, moved):
        pairs = []
        for b in range(self.n_blk):
            for r in range(self.reps):
                to_b, to_r = moved(b, r)
                pairs.append((b * self.reps + r, to_b * self.reps + to_r))
        return pairs

    def owner_to_class(self, mask):
        reps = self.reps
        return self.route(lambda b, r: (((b // reps) ^ mask) * reps + (b + r) % reps, r))

    def class_to_owner(self, mask):
        reps = self.reps
        return self.route(lambda b, r: (((b // reps) ^ mask) * reps + (b - r) % reps, r))

    def in_class(self, mask, rep_mask):
        reps = self.reps

        def moved(b, r):
            to_r = r ^ rep_mask
            return (((b // reps) ^ mask) * reps + (b - r + to_r) % reps, to_r)

        return self.route(moved)

    def plain(self, mask, rep_mask):
        return self.route(lambda b, r: (b ^ mask, r ^ rep_mask))


def send(value, route):
    return lax.ppermute(value, AXES, route)


def section_places(sections):
    reps, n_blk = lax.axis_size("rep"), lax.axis_size("blk")
    b, r = lax.axis_index("blk"), lax.axis_index("rep")
    columns = (b - r - jnp.arange(sections, dtype=jnp.int32) * reps) % n_blk
    return (columns // reps) ^ (b // reps)


def local_pairs(features, weight, tiles, pos, count, cotangent):
    near, halves = 2, 2
    lay = Layout(lax.axis_size("blk"), lax.axis_size("rep"))
    b, r = lax.axis_index("blk"), lax.axis_index("rep")
    sections, tile = tiles.shape[0], tiles.shape[-1]
    rows, width = features.shape
    blocks, share, far = rows // tile, rows // halves, sections // near
    flip = (r * (blocks // halves)).astype(jnp.int32).reshape(1)
    quad = ((0, 1), (1, 0), (1, 1))

    own_rows = lax.dynamic_slice_in_dim(features, r * share, share, 0)
    line = jnp.concatenate([send(own_rows, lay.owner_to_class(at * near)) for at in range(far)], 0)
    far_cot = send(cotangent, lay.plain(0, 1))
    parts = [line] + [send(line, lay.in_class(*mask)) for mask in quad]
    dense = dense_blocks(tiles, pos, count, section_places(sections), flip, near, halves, blocks)
    partial, sent = aggregate(dense, parts)
    other = send(sent, lay.plain(0, 1))
    act, g, grad, back, *outgoing = turn(partial, other, weight, cotangent, far_cot, dense)
    arrived = [send(value, lay.in_class(*mask)) for value, mask in zip(outgoing, quad)]
    kept, wg = kept_terms(back, dense, g, grad)

    lane = b % 2
    wg_rows = wg.shape[0] // 2
    wg_own = lax.dynamic_slice_in_dim(wg, lane * wg_rows, wg_rows, 0)
    wg_sent = lax.dynamic_slice_in_dim(wg, (1 - lane) * wg_rows, wg_rows, 0)
    wg_own = wg_own + send(wg_sent, lay.plain(1, 0))
    wg_own = wg_own + send(wg_own, lay.plain(0, 1))
    wg_own = wg_own + send(wg_own, lay.plain(2, 0))

    lines = near_sum(kept, arrived, wg_own, far)
    lines = [send(value, lay.class_to_owner(at * near)) for at, value in enumerate(lines)]
    feat_grad, wg_half = far_sum(lines, width)
    wg_other = send(wg_half, lay.plain(1, 0))
    first = (lane ^ r) == 0
    weight_grad = jnp.concatenate(
        [jnp.where(first, wg_half, wg_other), jnp.where(first, wg_other, wg_half)], 0
    )
    return act, feat_grad, weight_grad


def local_any(features, weight, tiles, pos, count, cotangent):
    reps = lax.axis_size("rep")
    lay = Layout(lax.axis_size("blk"), reps)
    r = lax.axis_index("rep")
    sections, tile = tiles.shape[0], tiles.shape[-1]
    rows = features.shape[0]
    blocks, share = rows // tile, rows // reps
    bf = jnp.bfloat16

    line = jnp.concatenate([send(features, lay.owner_to_class(at)) for at in range(sections)], 0)
    flip = jnp.zeros((1,), jnp.int32)
    dense = dense_blocks(tiles, pos, count, section_places(sections), flip, 1, 1, blocks)
    partial, _ = aggregate(dense, [line])
    g = lax.psum(partial, "rep").astype(bf)
    value, slope = gelu_and_slope(dot(g, weight))
    cot = lax.all_gather(cotangent, "rep", axis=0, tiled=True)
    grad = (cot.astype(jnp.float32) * slope).astype(bf)
    act = lax.dynamic_slice_in_dim(value, r * share, share, 0).astype(bf)
    own_g = lax.dynamic_slice_in_dim(g, r * share, share, 0)
    own_grad = lax.dynamic_slice_in_dim(grad, r * share, share, 0)
    weight_grad = lax.psum(tn_dot(own_g, own_grad), AXES)
    back = nt_dot(weight, grad).astype(bf)
    terms = dot(back, dense[0, 0]).astype(bf)
    total = jnp.zeros((back.shape[0], rows), jnp.float32)
    for at in range(sections):
        total += send(terms[:, at * rows:(at + 1) * rows], lay.class_to_owner(at)).astype(jnp.float32)
    feat_grad = lax.psum_scatter(total.T, "rep", scatter_dimension=0, tiled=True).astype(bf)
    return act, feat_grad, weight_grad


def local(features, weight, tile_vals, tile_pos, tile_count, cotangent):
    tiles, pos, count = tile_vals[0, 0], tile_pos[0, 0], tile_count[0, 0]
    reps, tile = lax.axis_size("rep"), tiles.shape[-1]
    paired = reps == 2 and tiles.shape[0] == 8 and features.shape[0] % (2 * tile) == 0
    work = local_pairs if paired else local_any
    return work(features, weight, tiles, pos, count, cotangent)


def solution(mesh):
    placed = (
        P("blk", None),
        P(),
        P("blk", "rep", None, None, None, None),
        P("blk", "rep", None, None),
        P("blk", "rep", None),
        P(("blk", "rep"), None),
    )
    return jax.shard_map(
        local,
        mesh=mesh,
        in_specs=placed,
        out_specs=(P(("blk", "rep"), None), P(("blk", "rep"), None), P()),
        check_vma=False,
    )
```

time: 432 us -> 79 us (0.18)
  the two profiles are of different devices: /device:TPU:0 before, /device:TPU:11 now
where the time goes in v1:
time: 79 us; the launch traced here: 78.7 us
  waiting for transfers between devices  41 us (52%)
  starting transfers between devices  21 us (27%)
  local copies, waits for them, and re-layouts  8.34 us (11%)
  Pallas kernels  6.78 us (9%)
  between operations  0.83 us (1%)
    ppermute x20, waiting for transfers between devices, send(): return lax.ppermute(value, AXES, route)  41 us
    ppermute x20, starting transfers between devices, send(): return lax.ppermute(value, AXES, route)  21 us
    unnamed x19, local copies, waits for them, and re-layouts  8.31 us
    pallas_call x1, Pallas kernels, dense_blocks(): pl.pallas_call(functools.partial(dense_kernel, blocks, halves), grid_spec...  2.84 us
  transfers between devices with their start and end apart: 20, of which 11 were waited for; matrix products, arithmetic and copies ran while one was open for 0% of the time, Pallas kernels for 5%

profile of v1, /device:TPU:11, one launch (start us, length us, event | category | flops | bytes accessed | tf_op | source)
XLA Modules:
  0.0 78.7 jit_solution(4472924272390089284)
XLA Ops:
  0.6 0.0 copy-start
  0.7 0.9 %copy-done = bf16[512,128]{1,0:T(8,128)(2,1)S(1)} copy-done((bf16[512,128]{1,0:T(8,128)(2,1)S(1)}, bf16[512,128]{1,0:T(8,128)(2,1)}, u32[]{:S(2)}) %copy-start) | copy-done | bytes 131096
  1.5 2.6 %collective-permute-start = (bf16[256,128]{1,0:T(8,128)(2,1)S(1)}, bf16[256,128]{1,0:T(8,128)(2,1)S(1)}, u32[]{:S(2)}, u32[]{:S(2)}) collective-permute-start(bf16[256,128]{1,0:T(8,128)(2,1)S(1)} %constant_dynamic-slice_fusion.1), channel_id=1, source_target_pairs={{0,0},{1,3},{2,2},{3,1},{4,4},{5,7},{6,6},{7,5},{8,8},{9,11},{10,1... | collective-permute-start | bytes 196616 | tf_op jit(solution)/shard_map/ppermute | solution.py:252
  4.1 1.3 %collective-permute-start.3 = (bf16[256,128]{1,0:T(8,128)(2,1)S(1)}, bf16[256,128]{1,0:T(8,128)(2,1)S(1)}, u32[]{:S(2)}, u32[]{:S(2)}) collective-permute-start(bf16[256,128]{1,0:T(8,128)(2,1)S(1)} %constant_dynamic-slice_fusion.1), channel_id=1, source_target_pairs={{0,24},{1,27},{2,26},{3,25},{4,28},{5,31},{6,30},{7,29},{8,16},{9,... | collective-permute-start | bytes 196616 | tf_op jit(solution)/shard_map/ppermute | solution.py:252
  5.4 1.3 %collective-permute-start.2 = (bf16[256,128]{1,0:T(8,128)(2,1)S(1)}, bf16[256,128]{1,0:T(8,128)(2,1)S(1)}, u32[]{:S(2)}, u32[]{:S(2)}) collective-permute-start(bf16[256,128]{1,0:T(8,128)(2,1)S(1)} %constant_dynamic-slice_fusion.1), channel_id=1, source_target_pairs={{0,16},{1,19},{2,18},{3,17},{4,20},{5,23},{6,22},{7,21},{8,24},{9,... | collective-permute-start | bytes 196616 | tf_op jit(solution)/shard_map/ppermute | solution.py:252
  6.7 1.2 %collective-permute-start.1 = (bf16[256,128]{1,0:T(8,128)(2,1)S(1)}, bf16[256,128]{1,0:T(8,128)(2,1)S(1)}, u32[]{:S(2)}, u32[]{:S(2)}) collective-permute-start(bf16[256,128]{1,0:T(8,128)(2,1)S(1)} %constant_dynamic-slice_fusion.1), channel_id=1, source_target_pairs={{0,8},{1,11},{2,10},{3,9},{4,12},{5,15},{6,14},{7,13},{8,0},{9,3},... | collective-permute-start | bytes 196616 | tf_op jit(solution)/shard_map/ppermute | solution.py:252
  8.0 4.8 %collective-permute-done.1 = bf16[256,128]{1,0:T(8,128)(2,1)S(1)} collective-permute-done((bf16[256,128]{1,0:T(8,128)(2,1)S(1)}, bf16[256,128]{1,0:T(8,128)(2,1)S(1)}, u32[]{:S(2)}, u32[]{:S(2)}) %collective-permute-start.1) | collective-permute-done | bytes 65568 | tf_op jit(solution)/shard_map/ppermute | solution.py:252
  12.8 0.0 collective-permute-done.2
  12.8 0.0 collective-permute-done.3
  12.9 0.1 collective-permute-start.6
  12.9 1.3 %collective-permute-start.5 = (bf16[1024,128]{1,0:T(8,128)(2,1)S(1)}, bf16[1024,128]{1,0:T(8,128)(2,1)S(1)}, u32[]{:S(2)}, u32[]{:S(2)}) collective-permute-start(bf16[1024,128]{1,0:T(8,128)(2,1)S(1)} %constant_dynamic-update-slice_fusion.refs_0_), channel_id=1, source_target_pairs={{0,4},{1,5},{2,6},{3,7},{4,0},{5,1},{6,2},{7,3},{8,12},{9,13},{10,... | collective-permute-start | bytes 786440 | tf_op jit(solution)/shard_map/ppermute | solution.py:252
  14.2 1.9 %collective-permute-start.4 = (bf16[1024,128]{1,0:T(8,128)(2,1)S(1)}, bf16[1024,128]{1,0:T(8,128)(2,1)S(1)}, u32[]{:S(2)}, u32[]{:S(2)}) collective-permute-start(bf16[1024,128]{1,0:T(8,128)(2,1)S(1)} %constant_dynamic-update-slice_fusion.refs_0_), channel_id=1, source_target_pairs={{0,3},{1,2},{2,1},{3,0},{4,7},{5,6},{6,5},{7,4},{8,11},{9,10},{10,... | collective-permute-start | bytes 786440 | tf_op jit(solution)/shard_map/ppermute | solution.py:252
  16.2 0.0 copy-start.3
  16.2 1.9 %copy-done.3 = bf16[1,1,8,12,128,128]{5,4,3,2,1,0:T(8,128)(2,1)S(1)} copy-done((bf16[1,1,8,12,128,128]{5,4,3,2,1,0:T(8,128)(2,1)S(1)}, bf16[1,1,8,12,128,128]{5,4,3,2,1,0:T(8,128)(2,1)}, u32[]{:S(2)}) %copy-start.3) | copy-done | bytes 3145752
  18.1 0.7 copy-done.6
  18.7 0.7 copy-done.7
  19.4 2.8 %dense_blocks.1.dense_ref = bf16[2,2,512,1024]{3,2,1,0:T(8,128)(2,1)S(1)} custom-call(s32[8,12]{1,0:T(8,128)S(1)} %bitcast.5, s32[8]{0:T(128)S(1)} %bitcast.6, s32[8]{0:T(128)S(1)} %fusion.1.place, s32[1]{0:T(128)} %bitcast.2.flip, bf16[8,12,128,128]{3,2,1,0:T(8,128)(2,1)S(1)} %bitcast.4), custom_call_target="tpu_custom_call" | custom-call | tf_op jit(solution)/shard_map/dense_blocks/pallas_call | solution.py:74
  22.2 0.0 copy-start.4
  22.3 0.0 copy-start.5
  22.3 0.2 collective-permute-done.6.refs_3_
  22.4 4.1 %collective-permute-done.5.refs_2_ = bf16[1024,128]{1,0:T(8,128)(2,1)S(1)} collective-permute-done((bf16[1024,128]{1,0:T(8,128)(2,1)S(1)}, bf16[1024,128]{1,0:T(8,128)(2,1)S(1)}, u32[]{:S(2)}, u32[]{:S(2)}) %collective-permute-start.5) | collective-permute-done | bytes 262176 | tf_op jit(solution)/shard_map/ppermute | solution.py:252
  26.5 1.6 %collective-permute-done.4.refs_1_ = bf16[1024,128]{1,0:T(8,128)(2,1)S(1)} collective-permute-done((bf16[1024,128]{1,0:T(8,128)(2,1)S(1)}, bf16[1024,128]{1,0:T(8,128)(2,1)S(1)}, u32[]{:S(2)}, u32[]{:S(2)}) %collective-permute-start.4) | collective-permute-done | bytes 262176 | tf_op jit(solution)/shard_map/ppermute | solution.py:252
  28.1 1.2 %aggregate.1 = (f32[512,128]{1,0:T(8,128)S(1)}, bf16[512,128]{1,0:T(8,128)(2,1)S(1)}) custom-call(bf16[2,2,512,1024]{3,2,1,0:T(8,128)(2,1)S(1)} %dense_blocks.1.dense_ref, bf16[1024,128]{1,0:T(8,128)(2,1)S(1)} %constant_dynamic-update-slice_fusion.refs_0_, bf16[1024,128]{1,0:T(8,128)(2,1)S(1)} %collective-permute-done.4.refs_1_, ...), custom_call_target="tpu_custom_call" | custom-call | tf_op jit(solution)/shard_map/aggregate/pallas_call | solution.py:96
  29.4 1.9 %copy-done.1 = bf16[2,2,512,1024]{3,2,1,0:T(8,128)(2,1)} copy-done((bf16[2,2,512,1024]{3,2,1,0:T(8,128)(2,1)}, bf16[2,2,512,1024]{3,2,1,0:T(8,128)(2,1)S(1)}, u32[]{:S(2)}) %copy-start.1) | copy-done | bytes 4194328
  31.3 5.5 %collective-permute-done.7.other_ref = bf16[512,128]{1,0:T(8,128)(2,1)S(1)} collective-permute-done((bf16[512,128]{1,0:T(8,128)(2,1)S(1)}, bf16[512,128]{1,0:T(8,128)(2,1)S(1)}, u32[]{:S(2)}, u32[]{:S(2)}) %collective-permute-start.7) | collective-permute-done | bytes 131104 | tf_op jit(solution)/shard_map/ppermute | solution.py:252
  36.8 2.2 %copy-done.2 = bf16[2,2,512,1024]{3,2,1,0:T(8,128)(2,1)S(1)} copy-done((bf16[2,2,512,1024]{3,2,1,0:T(8,128)(2,1)S(1)}, bf16[2,2,512,1024]{3,2,1,0:T(8,128)(2,1)}, u32[]{:S(2)}) %copy-start.2) | copy-done | bytes 4194328
  39.0 1.5 %turn.1 = (bf16[256,256]{1,0:T(8,128)(2,1)}, bf16[256,128]{1,0:T(8,128)(2,1)S(1)}, bf16[256,256]{1,0:T(8,128)(2,1)S(1)}, bf16[128,512]{1,0:T(8,128)(2,1)S(1)}, b...) custom-call(f32[512,128]{1,0:T(8,128)S(1)} %get-tuple-element.20.own_ref, ...), custom_call_target="tpu_custom_call" | custom-call | tf_op jit(solution)/shard_map/turn/pallas_call | solution.py:134
  40.5 0.3 kept_terms.1
  40.9 0.5 collective-permute-start.12
  41.3 0.2 collective-permute-start.10
  41.6 3.0 %collective-permute-start.11 = (bf16[128,1024]{1,0:T(8,128)(2,1)S(1)}, bf16[128,1024]{1,0:T(8,128)(2,1)S(1)}, u32[]{:S(2)}, u32[]{:S(2)}) collective-permute-start(bf16[128,1024]{1,0:T(8,128)(2,1)S(1)} %get-tuple-element.29), channel_id=1, source_target_pairs={{0,7},{1,6},{2,5},{3,4},{4,3},{5,2},{6,1},{7,0},{8,15},{9,14},{10,... | collective-permute-start | bytes 786440 | tf_op jit(solution)/shard_map/ppermute | solution.py:252
  44.6 0.1 collective-permute-start.13
  44.7 11.5 %collective-permute-done.13 = f32[64,256]{1,0:T(8,128)S(1)} collective-permute-done((f32[64,256]{1,0:T(8,128)S(1)}, f32[64,256]{1,0:T(8,128)S(1)}, u32[]{:S(2)}, u32[]{:S(2)}) %collective-permute-start.13) | collective-permute-done | bytes 65568 | tf_op jit(solution)/shard_map/ppermute | solution.py:252
  56.1 0.3 collective-permute-start.14
  56.4 2.9 %collective-permute-done.14 = f32[64,256]{1,0:T(8,128)S(1)} collective-permute-done((f32[64,256]{1,0:T(8,128)S(1)}, f32[64,256]{1,0:T(8,128)S(1)}, u32[]{:S(2)}, u32[]{:S(2)}) %collective-permute-start.14) | collective-permute-done | bytes 65568 | tf_op jit(solution)/shard_map/ppermute | solution.py:252
  59.3 0.0 collective-permute-done.9.a_ref
  59.4 0.1 near_sum.1
  59.5 4.0 %collective-permute-start.15 = (bf16[192,256]{1,0:T(8,128)(2,1)S(1)}, bf16[192,256]{1,0:T(8,128)(2,1)S(1)}, u32[]{:S(2)}, u32[]{:S(2)}) collective-permute-start(bf16[192,256]{1,0:T(8,128)(2,1)S(1)} %get-tuple-element.31), channel_id=1, source_target_pairs={{0,0},{1,3},{2,2},{3,1},{4,4},{5,7},{6,6},{7,5},{8,8},{9,11},{10,1... | collective-permute-start | bytes 294920 | tf_op jit(solution)/shard_map/ppermute | solution.py:252
  63.5 0.7 collective-permute-start.16
  64.2 1.0 %collective-permute-start.17 = (bf16[192,256]{1,0:T(8,128)(2,1)S(1)}, bf16[192,256]{1,0:T(8,128)(2,1)S(1)}, u32[]{:S(2)}, u32[]{:S(2)}) collective-permute-start(bf16[192,256]{1,0:T(8,128)(2,1)S(1)} %get-tuple-element.33), channel_id=1, source_target_pairs={{0,16},{1,19},{2,18},{3,17},{4,20},{5,23},{6,22},{7,21},{8,24},{9,... | collective-permute-start | bytes 294920 | tf_op jit(solution)/shard_map/ppermute | solution.py:252
  65.2 1.2 %collective-permute-start.18 = (bf16[192,256]{1,0:T(8,128)(2,1)S(1)}, bf16[192,256]{1,0:T(8,128)(2,1)S(1)}, u32[]{:S(2)}, u32[]{:S(2)}) collective-permute-start(bf16[192,256]{1,0:T(8,128)(2,1)S(1)} %get-tuple-element.34), channel_id=1, source_target_pairs={{0,24},{1,27},{2,26},{3,25},{4,28},{5,31},{6,30},{7,29},{8,16},{9,... | collective-permute-start | bytes 294920 | tf_op jit(solution)/shard_map/ppermute | solution.py:252
  66.4 1.6 %collective-permute-done.16.refs_1_ = bf16[192,256]{1,0:T(8,128)(2,1)S(1)} collective-permute-done((bf16[192,256]{1,0:T(8,128)(2,1)S(1)}, bf16[192,256]{1,0:T(8,128)(2,1)S(1)}, u32[]{:S(2)}, u32[]{:S(2)}) %collective-permute-start.16) | collective-permute-done | bytes 98336 | tf_op jit(solution)/shard_map/ppermute | solution.py:252
  68.1 2.6 %collective-permute-done.17.refs_2_ = bf16[192,256]{1,0:T(8,128)(2,1)S(1)} collective-permute-done((bf16[192,256]{1,0:T(8,128)(2,1)S(1)}, bf16[192,256]{1,0:T(8,128)(2,1)S(1)}, u32[]{:S(2)}, u32[]{:S(2)}) %collective-permute-start.17) | collective-permute-done | bytes 98336 | tf_op jit(solution)/shard_map/ppermute | solution.py:252
  70.7 5.3 %collective-permute-done.18.refs_3_ = bf16[192,256]{1,0:T(8,128)(2,1)S(1)} collective-permute-done((bf16[192,256]{1,0:T(8,128)(2,1)S(1)}, bf16[192,256]{1,0:T(8,128)(2,1)S(1)}, u32[]{:S(2)}, u32[]{:S(2)}) %collective-permute-start.18) | collective-permute-done | bytes 98336 | tf_op jit(solution)/shard_map/ppermute | solution.py:252
  76.0 0.7 far_sum.1
  76.7 0.4 collective-permute-start.19
  77.1 0.9 %collective-permute-done.19 = f32[64,256]{1,0:T(8,128)S(1)} collective-permute-done((f32[64,256]{1,0:T(8,128)S(1)}, f32[64,256]{1,0:T(8,128)S(1)}, u32[]{:S(2)}, u32[]{:S(2)}) %collective-permute-start.19) | collective-permute-done | bytes 65568 | tf_op jit(solution)/shard_map/ppermute | solution.py:252
  78.0 0.7 pad_maximum_fusion
  (26 shorter events, 0.2 us)
Async XLA Ops:
  0.6 0.9 %copy-start = (bf16[512,128]{1,0:T(8,128)(2,1)S(1)}, bf16[512,128]{1,0:T(8,128)(2,1)}, u32[]{:S(2)}) copy-start(bf16[512,128]{1,0:T(8,128)(2,1)} %param.6) | copy-start | bytes 393220
  1.5 6.4 %collective-permute-start = (bf16[256,128]{1,0:T(8,128)(2,1)S(1)}, bf16[256,128]{1,0:T(8,128)(2,1)S(1)}, u32[]{:S(2)}, u32[]{:S(2)}) collective-permute-start(bf16[256,128]{1,0:T(8,128)(2,1)S(1)} %constant_dynamic-slice_fusion.1), channel_id=1, source_target_pairs={{0,0},{1,3},{2,2},{3,1},{4,4},{5,7},{6,6},{7,5},{8,8},{9,11},{10,1... | collective-permute-start | bytes 196616 | tf_op jit(solution)/shard_map/ppermute | solution.py:252
  4.1 8.7 %collective-permute-start.3 = (bf16[256,128]{1,0:T(8,128)(2,1)S(1)}, bf16[256,128]{1,0:T(8,128)(2,1)S(1)}, u32[]{:S(2)}, u32[]{:S(2)}) collective-permute-start(bf16[256,128]{1,0:T(8,128)(2,1)S(1)} %constant_dynamic-slice_fusion.1), channel_id=1, source_target_pairs={{0,24},{1,27},{2,26},{3,25},{4,28},{5,31},{6,30},{7,29},{8,16},{9,... | collective-permute-start | bytes 196616 | tf_op jit(solution)/shard_map/ppermute | solution.py:252
  5.4 7.4 %collective-permute-start.2 = (bf16[256,128]{1,0:T(8,128)(2,1)S(1)}, bf16[256,128]{1,0:T(8,128)(2,1)S(1)}, u32[]{:S(2)}, u32[]{:S(2)}) collective-permute-start(bf16[256,128]{1,0:T(8,128)(2,1)S(1)} %constant_dynamic-slice_fusion.1), channel_id=1, source_target_pairs={{0,16},{1,19},{2,18},{3,17},{4,20},{5,23},{6,22},{7,21},{8,24},{9,... | collective-permute-start | bytes 196616 | tf_op jit(solution)/shard_map/ppermute | solution.py:252
  6.7 6.1 %collective-permute-start.1 = (bf16[256,128]{1,0:T(8,128)(2,1)S(1)}, bf16[256,128]{1,0:T(8,128)(2,1)S(1)}, u32[]{:S(2)}, u32[]{:S(2)}) collective-permute-start(bf16[256,128]{1,0:T(8,128)(2,1)S(1)} %constant_dynamic-slice_fusion.1), channel_id=1, source_target_pairs={{0,8},{1,11},{2,10},{3,9},{4,12},{5,15},{6,14},{7,13},{8,0},{9,3},... | collective-permute-start | bytes 196616 | tf_op jit(solution)/shard_map/ppermute | solution.py:252
  12.9 9.6 %collective-permute-start.6 = (bf16[1024,128]{1,0:T(8,128)(2,1)S(1)}, bf16[1024,128]{1,0:T(8,128)(2,1)S(1)}, u32[]{:S(2)}, u32[]{:S(2)}) collective-permute-start(bf16[1024,128]{1,0:T(8,128)(2,1)S(1)} %constant_dynamic-update-slice_fusion.refs_0_), channel_id=1, source_target_pairs={{0,7},{1,6},{2,5},{3,4},{4,3},{5,2},{6,1},{7,0},{8,15},{9,14},{10,... | collective-permute-start | bytes 786440 | tf_op jit(solution)/shard_map/ppermute | solution.py:252
  12.9 13.6 %collective-permute-start.5 = (bf16[1024,128]{1,0:T(8,128)(2,1)S(1)}, bf16[1024,128]{1,0:T(8,128)(2,1)S(1)}, u32[]{:S(2)}, u32[]{:S(2)}) collective-permute-start(bf16[1024,128]{1,0:T(8,128)(2,1)S(1)} %constant_dynamic-update-slice_fusion.refs_0_), channel_id=1, source_target_pairs={{0,4},{1,5},{2,6},{3,7},{4,0},{5,1},{6,2},{7,3},{8,12},{9,13},{10,... | collective-permute-start | bytes 786440 | tf_op jit(solution)/shard_map/ppermute | solution.py:252
  14.2 13.8 %collective-permute-start.4 = (bf16[1024,128]{1,0:T(8,128)(2,1)S(1)}, bf16[1024,128]{1,0:T(8,128)(2,1)S(1)}, u32[]{:S(2)}, u32[]{:S(2)}) collective-permute-start(bf16[1024,128]{1,0:T(8,128)(2,1)S(1)} %constant_dynamic-update-slice_fusion.refs_0_), channel_id=1, source_target_pairs={{0,3},{1,2},{2,1},{3,0},{4,7},{5,6},{6,5},{7,4},{8,11},{9,10},{10,... | collective-permute-start | bytes 786440 | tf_op jit(solution)/shard_map/ppermute | solution.py:252
  16.1 15.2 %collective-permute-start.8 = (bf16[256,256]{1,0:T(8,128)(2,1)}, bf16[256,256]{1,0:T(8,128)(2,1)S(1)}, u32[]{:S(2)}, u32[]{:S(2)}) collective-permute-start(bf16[256,256]{1,0:T(8,128)(2,1)} %cot_ref.1), channel_id=1, source_target_pairs={{0,1},{1,0},{2,3},{3,2},{4,5},{5,4},{6,7},{7,6},{8,9},{9,8},{10,11... | collective-permute-start | bytes 393224 | tf_op jit(solution)/shard_map/ppermute | solution.py:252
  16.2 1.9 %copy-start.3 = (bf16[1,1,8,12,128,128]{5,4,3,2,1,0:T(8,128)(2,1)S(1)}, bf16[1,1,8,12,128,128]{5,4,3,2,1,0:T(8,128)(2,1)}, u32[]{:S(2)}) copy-start(bf16[1,1,8,12,128,128]{5,4,3,2,1,0:T(8,128)(2,1)} %param.8) | copy-start | bytes 9437188
  18.0 0.7 copy-start.6
  18.7 0.7 copy-start.7
  22.2 14.6 %copy-start.4 = (bf16[256,256]{1,0:T(8,128)(2,1)S(1)}, bf16[256,256]{1,0:T(8,128)(2,1)}, u32[]{:S(2)}) copy-start(bf16[256,256]{1,0:T(8,128)(2,1)} %cot_ref.1) | copy-start | bytes 393220
  22.3 14.6 %copy-start.5 = (bf16[128,256]{1,0:T(8,128)(2,1)S(1)}, bf16[128,256]{1,0:T(8,128)(2,1)}, u32[]{:S(2)}) copy-start(bf16[128,256]{1,0:T(8,128)(2,1)} %weight_ref.1) | copy-start | bytes 196612
  29.3 2.0 %copy-start.1 = (bf16[2,2,512,1024]{3,2,1,0:T(8,128)(2,1)}, bf16[2,2,512,1024]{3,2,1,0:T(8,128)(2,1)S(1)}, u32[]{:S(2)}) copy-start(bf16[2,2,512,1024]{3,2,1,0:T(8,128)(2,1)S(1)} %dense_blocks.1.dense_ref) | copy-start | bytes 12582916
  31.3 5.5 %collective-permute-start.7 = (bf16[512,128]{1,0:T(8,128)(2,1)S(1)}, bf16[512,128]{1,0:T(8,128)(2,1)S(1)}, u32[]{:S(2)}, u32[]{:S(2)}) collective-permute-start(bf16[512,128]{1,0:T(8,128)(2,1)S(1)} %get-tuple-element.21), channel_id=1, source_target_pairs={{0,1},{1,0},{2,3},{3,2},{4,5},{5,4},{6,7},{7,6},{8,9},{9,8},{10,11... | collective-permute-start | bytes 393224 | tf_op jit(solution)/shard_map/ppermute | solution.py:252
  36.8 2.2 %copy-start.2 = (bf16[2,2,512,1024]{3,2,1,0:T(8,128)(2,1)S(1)}, bf16[2,2,512,1024]{3,2,1,0:T(8,128)(2,1)}, u32[]{:S(2)}) copy-start(bf16[2,2,512,1024]{3,2,1,0:T(8,128)(2,1)} %copy-done.1) | copy-start | bytes 12582916
  40.9 3.7 %collective-permute-start.12 = (f32[64,256]{1,0:T(8,128)S(1)}, f32[64,256]{1,0:T(8,128)S(1)}, u32[]{:S(2)}, u32[]{:S(2)}) collective-permute-start(f32[64,256]{1,0:T(8,128)S(1)} %constant_dynamic-slice_fusion), channel_id=1, source_target_pairs={{0,2},{1,3},{2,0},{3,1},{4,6},{5,7},{6,4},{7,5},{8,10},{9,11},{10,... | collective-permute-start | bytes 196616 | tf_op jit(solution)/shard_map/ppermute | solution.py:252
  41.3 18.0 %collective-permute-start.9 = (bf16[128,1024]{1,0:T(8,128)(2,1)S(1)}, bf16[128,1024]{1,0:T(8,128)(2,1)S(1)}, u32[]{:S(2)}, u32[]{:S(2)}) collective-permute-start(bf16[128,1024]{1,0:T(8,128)(2,1)S(1)} %get-tuple-element.27), channel_id=1, source_target_pairs={{0,3},{1,2},{2,1},{3,0},{4,7},{5,6},{6,5},{7,4},{8,11},{9,10},{10,... | collective-permute-start | bytes 786440 | tf_op jit(solution)/shard_map/ppermute | solution.py:252
  41.3 18.0 %collective-permute-start.10 = (bf16[128,1024]{1,0:T(8,128)(2,1)S(1)}, bf16[128,1024]{1,0:T(8,128)(2,1)S(1)}, u32[]{:S(2)}, u32[]{:S(2)}) collective-permute-start(bf16[128,1024]{1,0:T(8,128)(2,1)S(1)} %get-tuple-element.28), channel_id=1, source_target_pairs={{0,4},{1,5},{2,6},{3,7},{4,0},{5,1},{6,2},{7,3},{8,12},{9,13},{10,... | collective-permute-start | bytes 786440 | tf_op jit(solution)/shard_map/ppermute | solution.py:252
  41.6 17.8 %collective-permute-start.11 = (bf16[128,1024]{1,0:T(8,128)(2,1)S(1)}, bf16[128,1024]{1,0:T(8,128)(2,1)S(1)}, u32[]{:S(2)}, u32[]{:S(2)}) collective-permute-start(bf16[128,1024]{1,0:T(8,128)(2,1)S(1)} %get-tuple-element.29), channel_id=1, source_target_pairs={{0,7},{1,6},{2,5},{3,4},{4,3},{5,2},{6,1},{7,0},{8,15},{9,14},{10,... | collective-permute-start | bytes 786440 | tf_op jit(solution)/shard_map/ppermute | solution.py:252
  44.6 11.5 %collective-permute-start.13 = (f32[64,256]{1,0:T(8,128)S(1)}, f32[64,256]{1,0:T(8,128)S(1)}, u32[]{:S(2)}, u32[]{:S(2)}) collective-permute-start(f32[64,256]{1,0:T(8,128)S(1)} %dynamic-slice_add_fusion), channel_id=1, source_target_pairs={{0,1},{1,0},{2,3},{3,2},{4,5},{5,4},{6,7},{7,6},{8,9},{9,8},{10,11... | collective-permute-start | bytes 196616 | tf_op jit(solution)/shard_map/ppermute | solution.py:252
  56.1 3.2 %collective-permute-start.14 = (f32[64,256]{1,0:T(8,128)S(1)}, f32[64,256]{1,0:T(8,128)S(1)}, u32[]{:S(2)}, u32[]{:S(2)}) collective-permute-start(f32[64,256]{1,0:T(8,128)S(1)} %add.36), channel_id=1, source_target_pairs={{0,4},{1,5},{2,6},{3,7},{4,0},{5,1},{6,2},{7,3},{8,12},{9,13},{10,... | collective-permute-start | bytes 196616 | tf_op jit(solution)/shard_map/ppermute | solution.py:252
  59.5 6.9 %collective-permute-start.15 = (bf16[192,256]{1,0:T(8,128)(2,1)S(1)}, bf16[192,256]{1,0:T(8,128)(2,1)S(1)}, u32[]{:S(2)}, u32[]{:S(2)}) collective-permute-start(bf16[192,256]{1,0:T(8,128)(2,1)S(1)} %get-tuple-element.31), channel_id=1, source_target_pairs={{0,0},{1,3},{2,2},{3,1},{4,4},{5,7},{6,6},{7,5},{8,8},{9,11},{10,1... | collective-permute-start | bytes 294920 | tf_op jit(solution)/shard_map/ppermute | solution.py:252
  63.5 4.5 %collective-permute-start.16 = (bf16[192,256]{1,0:T(8,128)(2,1)S(1)}, bf16[192,256]{1,0:T(8,128)(2,1)S(1)}, u32[]{:S(2)}, u32[]{:S(2)}) collective-permute-start(bf16[192,256]{1,0:T(8,128)(2,1)S(1)} %get-tuple-element.32), channel_id=1, source_target_pairs={{0,8},{1,11},{2,10},{3,9},{4,12},{5,15},{6,14},{7,13},{8,0},{9,3},... | collective-permute-start | bytes 294920 | tf_op jit(solution)/shard_map/ppermute | solution.py:252
  64.2 6.5 %collective-permute-start.17 = (bf16[192,256]{1,0:T(8,128)(2,1)S(1)}, bf16[192,256]{1,0:T(8,128)(2,1)S(1)}, u32[]{:S(2)}, u32[]{:S(2)}) collective-permute-start(bf16[192,256]{1,0:T(8,128)(2,1)S(1)} %get-tuple-element.33), channel_id=1, source_target_pairs={{0,16},{1,19},{2,18},{3,17},{4,20},{5,23},{6,22},{7,21},{8,24},{9,... | collective-permute-start | bytes 294920 | tf_op jit(solution)/shard_map/ppermute | solution.py:252
  65.2 10.8 %collective-permute-start.18 = (bf16[192,256]{1,0:T(8,128)(2,1)S(1)}, bf16[192,256]{1,0:T(8,128)(2,1)S(1)}, u32[]{:S(2)}, u32[]{:S(2)}) collective-permute-start(bf16[192,256]{1,0:T(8,128)(2,1)S(1)} %get-tuple-element.34), channel_id=1, source_target_pairs={{0,24},{1,27},{2,26},{3,25},{4,28},{5,31},{6,30},{7,29},{8,16},{9,... | collective-permute-start | bytes 294920 | tf_op jit(solution)/shard_map/ppermute | solution.py:252
  76.7 1.3 %collective-permute-start.19 = (f32[64,256]{1,0:T(8,128)S(1)}, f32[64,256]{1,0:T(8,128)S(1)}, u32[]{:S(2)}, u32[]{:S(2)}) collective-permute-start(f32[64,256]{1,0:T(8,128)S(1)} %get-tuple-element.36), channel_id=1, source_target_pairs={{0,2},{1,3},{2,0},{3,1},{4,6},{5,7},{6,4},{7,5},{8,10},{9,11},{10,... | collective-permute-start | bytes 196616 | tf_op jit(solution)/shard_map/ppermute | solution.py:252

commit v2 on v1

v2 whole, which is shorter than its diff:
```python
import functools

import jax
import jax.numpy as jnp
from jax import lax
from jax.experimental import pallas as pl
from jax.experimental.pallas import tpu as pltpu
from jax.sharding import PartitionSpec as P

AXES = ("blk", "rep")
VMEM_LIMIT = 16 * 1024 * 1024


def params():
    return pltpu.CompilerParams(vmem_limit_bytes=VMEM_LIMIT)


def in_vmem(count):
    return [pl.BlockSpec(memory_space=pltpu.VMEM)] * count


def held_in_vmem(value):
    return pltpu.with_memory_space_constraint(value, pltpu.VMEM)


def gelu_and_slope(v):
    scale = 0.7978845608028654
    square = v * v
    t = jnp.tanh(scale * (v + 0.044715 * (square * v)))
    half = 0.5 * (1.0 + t)
    slope = half + (0.5 * scale) * v * (1.0 - t * t) * (1.0 + 3.0 * 0.044715 * square)
    return v * half, slope


def nt_dot(a, b):
    return lax.dot_general(a, b, (((1,), (1,)), ((), ())), preferred_element_type=jnp.float32)


def tn_dot(a, b):
    return lax.dot_general(a, b, (((0,), (0,)), ((), ())), preferred_element_type=jnp.float32)


def dot(a, b):
    return jnp.dot(a, b, preferred_element_type=jnp.float32)


def dense_kernel(blocks, near, halves, table, tiles_ref, out_ref, done_ref, held, arrived):
    sections, slots, tile = held.shape[0], held.shape[1], held.shape[-1]
    piece = out_ref.shape[2] // (sections // near)
    per_half = blocks // halves
    copies = [
        pltpu.make_async_copy(tiles_ref.at[section], held.at[section], arrived.at[section])
        for section in range(sections)
    ]
    for copy in copies:
        copy.start()
    out_ref[...] = jnp.zeros_like(out_ref)
    done_ref[...] = jnp.zeros_like(done_ref)
    for section, copy in enumerate(copies):
        copy.wait()
        place = table[section, slots]
        unit = lax.rem(place, near) * halves
        base = lax.div(place, near) * piece
        for slot in range(slots):
            cell = table[section, slot]
            row_at = pl.multiple_of(lax.div(cell, blocks) * tile, tile)
            col = lax.rem(cell, blocks)
            col_at = pl.multiple_of(base + lax.rem(col, per_half) * tile, tile)
            half = lax.div(col, per_half)

            @pl.when(cell >= 0)
            def _():
                out_ref[unit + half, pl.ds(row_at, tile), pl.ds(col_at, tile)] = held[section, slot]


def dense_blocks(tiles, table, near, halves, blocks):
    sections, _, tile, _ = tiles.shape
    rows = blocks * tile
    shape = (near * halves, rows, sections // near * rows // halves)
    return pl.pallas_call(
        functools.partial(dense_kernel, blocks, near, halves),
        in_specs=[pl.BlockSpec(memory_space=pltpu.SMEM), pl.BlockSpec(memory_space=pltpu.HBM)],
        out_specs=in_vmem(2),
        out_shape=[pltpu.VMEM(shape, jnp.bfloat16), jax.ShapeDtypeStruct((8, 128), jnp.float32)],
        scratch_shapes=[pltpu.VMEM(tiles.shape, tiles.dtype), pltpu.SemaphoreType.DMA((sections,))],
        compiler_params=params(),
        name="dense_blocks",
    )(table, pltpu.with_memory_space_constraint(tiles, pltpu.HBM))


def unit_at(unit):
    if unit in (0, 3):
        return unit
    lane = lax.rem(lax.axis_index("blk") + lax.axis_index("rep"), 2)
    return 2 - lane if unit == 1 else 1 + lane


def aggregate_kernel(spans, based, dense_ref, *refs):
    given, out_ref = refs[:-1], refs[-1]
    total = given[0][...] if based else None
    for (unit, start, row, size), part in zip(spans, given[based:]):
        term = dot(dense_ref[unit_at(unit), :, pl.ds(start, size)], part[pl.ds(row, size), :])
        total = term if total is None else total + term
    out_ref[...] = total.astype(out_ref.dtype)


def aggregate(dense, spans, parts, base, dtype):
    rows, width = dense.shape[1], parts[0].shape[1]
    given = ([] if base is None else [base]) + parts
    return pl.pallas_call(
        functools.partial(aggregate_kernel, spans, len(given) - len(parts)),
        in_specs=in_vmem(1 + len(given)),
        out_specs=in_vmem(1)[0],
        out_shape=jax.ShapeDtypeStruct((rows, width), dtype),
        compiler_params=params(),
        name="aggregate",
    )(held_in_vmem(dense), *given)


def turn_kernel(share, own_ref, other_ref, weight_ref, cot_ref, far_cot_ref, dense_ref,
                act_ref, back_ref, sent_ref):
    rows = own_ref.shape[0]
    span = dense_ref.shape[2]
    weight = weight_ref[...]
    weight_grad = None
    for half, cot in enumerate((cot_ref, far_cot_ref)):
        at, there = half * share, rows - share - half * share
        g = own_ref[pl.ds(at, share), :].astype(jnp.float32) + other_ref[pl.ds(there, share), :].astype(jnp.float32)
        g = g.astype(jnp.bfloat16)
        value, slope = gelu_and_slope(dot(g, weight))
        grad = (cot[...].astype(jnp.float32) * slope).astype(jnp.bfloat16)
        if half == 0:
            act_ref[...] = value.astype(jnp.bfloat16)
        term = tn_dot(g, grad)
        weight_grad = term if weight_grad is None else weight_grad + term
        back_ref[:, pl.ds(at, share)] = nt_dot(weight, grad).astype(jnp.bfloat16)
    back = back_ref[...]
    half_span = span // 2
    for second in range(2):
        term = dot(back, dense_ref[unit_at(2 + second), :, pl.ds(half_span, half_span)])
        sent_ref[:, pl.ds(second * half_span, half_span)] = term.astype(jnp.bfloat16)
    sent_ref[:, pl.ds(span, weight.shape[1])] = weight_grad.astype(jnp.bfloat16)


def turn(own, other, weight, cot, far_cot, dense):
    rows, width = own.shape
    share, hid = cot.shape
    span = dense.shape[2]
    bf = jnp.bfloat16
    return pl.pallas_call(
        functools.partial(turn_kernel, share),
        in_specs=in_vmem(6),
        out_specs=in_vmem(3),
        out_shape=[
            jax.ShapeDtypeStruct((share, hid), bf),
            jax.ShapeDtypeStruct((width, rows), bf),
            jax.ShapeDtypeStruct((width, span + hid), bf),
        ],
        compiler_params=params(),
        name="turn",
    )(own, other, weight, cot, far_cot, held_in_vmem(dense))


def rest_kernel(back_ref, dense_ref, sent_ref, kept_ref):
    back = back_ref[...]
    half_span = dense_ref.shape[2] // 2
    for second in range(2):
        term = dot(back, dense_ref[unit_at(2 + second), :, pl.ds(0, half_span)])
        sent_ref[:, pl.ds(second * half_span, half_span)] = term.astype(jnp.bfloat16)
    for second in range(2):
        kept_ref[second] = dot(back, dense_ref[unit_at(second)])


def rest_terms(back, dense):
    width, span = back.shape[0], dense.shape[2]
    return pl.pallas_call(
        rest_kernel,
        in_specs=in_vmem(2),
        out_specs=in_vmem(2),
        out_shape=[
            jax.ShapeDtypeStruct((width, span), jnp.bfloat16),
            jax.ShapeDtypeStruct((2, width, span), jnp.float32),
        ],
        compiler_params=params(),
        name="rest_terms",
    )(back, held_in_vmem(dense))


def first_sum_kernel(start, size, got_ref, kept_ref, own_ref, sent_ref, total_ref):
    extra = sent_ref.shape[1] - size
    total_ref[...] = kept_ref[0, :, pl.ds(start, size)] + got_ref[:, pl.ds(0, size)].astype(jnp.float32)
    passed = kept_ref[1, :, pl.ds(start, size)] + got_ref[:, pl.ds(size, size)].astype(jnp.float32)
    sent_ref[:, pl.ds(0, size)] = passed.astype(jnp.bfloat16)
    if extra:
        ours = own_ref[:, pl.ds(2 * size, extra)].astype(jnp.float32)
        theirs = got_ref[:, pl.ds(2 * size, extra)].astype(jnp.float32)
        sent_ref[:, pl.ds(size, extra)] = (ours + theirs).astype(jnp.bfloat16)


def first_sum(start, got, kept, own):
    width = kept.shape[1]
    size = kept.shape[2] // 2
    extra = got.shape[1] - 2 * size
    return pl.pallas_call(
        functools.partial(first_sum_kernel, start, size),
        in_specs=in_vmem(3),
        out_specs=in_vmem(2),
        out_shape=[
            jax.ShapeDtypeStruct((width, size + extra), jnp.bfloat16),
            jax.ShapeDtypeStruct((width, size), jnp.float32),
        ],
        compiler_params=params(),
        name="first_sum",
    )(got, kept, own)


def add_pieces(got_ref, kept_ref, wg, out_refs):
    width, size = kept_ref.shape
    piece = size // 2
    for at, out in enumerate(out_refs):
        span = pl.ds(at * piece, piece)
        out[0:width, :] = (kept_ref[:, span] + got_ref[:, span].astype(jnp.float32)).astype(jnp.bfloat16)
        out[width:, :] = wg


def second_sum_a_kernel(got_ref, kept_ref, own_ref, two_ref, three_ref, wg_ref):
    size, (part, hid) = kept_ref.shape[1], wg_ref.shape
    lane = lax.rem(lax.axis_index("blk") + lax.axis_index("rep"), 2)
    rows = pl.ds(pl.multiple_of(lane * part, part), part)
    wg = own_ref[rows, pl.ds(size, hid)].astype(jnp.float32) + got_ref[rows, pl.ds(size, hid)].astype(jnp.float32)
    wg_ref[...] = wg.astype(jnp.bfloat16)
    add_pieces(got_ref, kept_ref, wg.astype(jnp.bfloat16), (two_ref, three_ref))


def second_sum_b_kernel(got_ref, kept_ref, wg_ref, zero_ref, one_ref):
    add_pieces(got_ref, kept_ref, wg_ref[...], (zero_ref, one_ref))


def message_shape(kept):
    width, size = kept.shape
    return jax.ShapeDtypeStruct((width + width // 2, size // 2), jnp.bfloat16)


def second_sum_a(got, kept, own):
    width, size = kept.shape
    message = message_shape(kept)
    return pl.pallas_call(
        second_sum_a_kernel,
        in_specs=in_vmem(3),
        out_specs=in_vmem(3),
        out_shape=[message, message, jax.ShapeDtypeStruct((width // 2, got.shape[1] - size), jnp.bfloat16)],
        compiler_params=params(),
        name="second_sum_a",
    )(got, kept, own)


def second_sum_b(got, kept, wg):
    return pl.pallas_call(
        second_sum_b_kernel,
        in_specs=in_vmem(3),
        out_specs=in_vmem(2),
        out_shape=[message_shape(kept)] * 2,
        compiler_params=params(),
        name="second_sum_b",
    )(got, kept, wg)


def line_sum_kernel(three_ref, two_ref, one_ref, zero_ref, feat_ref, wg_ref):
    width, part = feat_ref.shape[0], wg_ref.shape[0]
    for out, rows in ((wg_ref, pl.ds(width, part)), (feat_ref, pl.ds(0, width))):
        near = zero_ref[rows, :].astype(jnp.float32) + one_ref[rows, :].astype(jnp.float32)
        out[...] = near + (two_ref[rows, :].astype(jnp.float32) + three_ref[rows, :].astype(jnp.float32))


def line_sum(three, two, one, zero, width):
    total, piece = three.shape
    return pl.pallas_call(
        line_sum_kernel,
        in_specs=in_vmem(4),
        out_specs=in_vmem(2),
        out_shape=[
            jax.ShapeDtypeStruct((width, piece), jnp.float32),
            jax.ShapeDtypeStruct((total - width, piece), jnp.float32),
        ],
        compiler_params=params(),
        name="line_sum",
    )(three, two, one, zero)


def finish_kernel(feat_sum_ref, half_ref, other_ref, feat_ref, wg_ref):
    part = half_ref.shape[0]
    core = lax.rem(lax.axis_index("blk"), 2)
    wg_ref[pl.ds(pl.multiple_of(core * part, part), part), :] = half_ref[...]
    wg_ref[pl.ds(pl.multiple_of((1 - core) * part, part), part), :] = other_ref[...]
    feat_ref[...] = feat_sum_ref[...].T.astype(jnp.bfloat16)


def finish(feat_sum, half, other):
    return pl.pallas_call(
        finish_kernel,
        in_specs=in_vmem(3),
        out_specs=in_vmem(2),
        out_shape=[
            jax.ShapeDtypeStruct(feat_sum.shape[::-1], jnp.bfloat16),
            jax.ShapeDtypeStruct((2 * half.shape[0], half.shape[1]), jnp.float32),
        ],
        compiler_params=params(),
        name="finish",
    )(feat_sum, half, other)


class Layout:
    def __init__(self, n_blk, reps):
        self.n_blk, self.reps = n_blk, reps

    def route(self, moved):
        pairs = []
        for b in range(self.n_blk):
            for r in range(self.reps):
                to_b, to_r = moved(b, r)
                pairs.append((b * self.reps + r, to_b * self.reps + to_r))
        return pairs

    def owner_to_class(self, mask):
        reps = self.reps
        return self.route(lambda b, r: (((b // reps) ^ mask) * reps + (b + r) % reps, r))

    def class_to_owner(self, mask):
        reps = self.reps
        return self.route(lambda b, r: (((b // reps) ^ mask) * reps + (b - r) % reps, r))

    def in_class(self, mask):
        return self.route(lambda b, r: (b ^ (mask * self.reps), r))

    def along(self, first):
        reps = self.reps

        def moved(b, r):
            lane = (b - r) % reps
            mask, rep_mask = (0, 1) if (lane == 0) == first else (1, 0)
            to_r = r ^ rep_mask
            return (((b // reps) ^ mask) * reps + (lane + to_r) % reps, to_r)

        return self.route(moved)

    def plain(self, mask, rep_mask):
        return self.route(lambda b, r: (b ^ mask, r ^ rep_mask))


def send(value, route):
    return lax.ppermute(value, AXES, route)


def section_table(pos, count, blocks, flip):
    reps, n_blk = lax.axis_size("rep"), lax.axis_size("blk")
    b, r = lax.axis_index("blk"), lax.axis_index("rep")
    sections, slots = pos.shape
    columns = (b - r - jnp.arange(sections, dtype=jnp.int32) * reps) % n_blk
    places = (columns // reps) ^ (b // reps)
    live = jnp.arange(slots, dtype=jnp.int32)[None, :] < count[:, None]
    cells = jnp.where(live, pos ^ (flip * (blocks + 1)), -1)
    return jnp.concatenate([cells, places[:, None]], 1).astype(jnp.int32)


def local_pairs(features, weight, tiles, pos, count, cotangent):
    near, halves = 2, 2
    lay = Layout(lax.axis_size("blk"), lax.axis_size("rep"))
    b, r = lax.axis_index("blk"), lax.axis_index("rep")
    sections, tile = tiles.shape[0], tiles.shape[-1]
    rows, width = features.shape
    blocks, share = rows // tile, rows // halves
    table = section_table(pos, count, blocks, r * (blocks // halves))
    own_rows = lax.dynamic_slice_in_dim(features, r * share, share, 0)
    three, two, one, zero = [send(own_rows, lay.owner_to_class(at * near)) for at in (3, 2, 1, 0)]
    half_span = 2 * share
    far_cot = send(cotangent, lay.plain(0, 1))
    mine_a, mine_b = jnp.concatenate([zero, one], 0), jnp.concatenate([two, three], 0)
    mine_a, table = lax.optimization_barrier((mine_a, table))
    beside_a = send(mine_a, lay.along(False))
    beside_a, far_cot = lax.optimization_barrier((beside_a, far_cot))
    beside_b = send(mine_b, lay.along(False))
    across_a = send(jnp.concatenate([mine_a, beside_a], 0), lay.along(True))
    across_b = send(jnp.concatenate([mine_b, beside_b], 0), lay.along(True))

    dense, _ = dense_blocks(tiles, table, near, halves, blocks)

    def spans(at, units):
        return [(unit, at * half_span, row, half_span) for unit, row in units]

    local_units, far_units = [(0, 0), (1, 0)], [(2, 0), (3, half_span)]
    partial = aggregate(
        dense, spans(0, local_units + far_units) + spans(1, local_units),
        [mine_a, beside_a, across_a, across_a, mine_b, beside_b], None, jnp.float32)
    partial = aggregate(dense, spans(1, far_units), [across_b, across_b], partial, jnp.bfloat16)
    other = send(partial, lay.plain(0, 1))
    act, back, sent_a = turn(partial, other, weight, cotangent, far_cot, dense)

    got_a = send(sent_a, lay.along(True))
    sent_b, kept = rest_terms(back, dense)
    got_b = send(sent_b, lay.along(True))
    passed_a, kept_a = first_sum(half_span, got_a, kept, sent_a)
    passed_b, kept_b = first_sum(0, got_b, kept, sent_b)
    back_a = send(passed_a, lay.along(False))
    back_b = send(passed_b, lay.along(False))
    two, three, wg = second_sum_a(back_a, kept_a, passed_a)
    three = send(three, lay.class_to_owner(3 * near))
    two = send(two, lay.class_to_owner(2 * near))
    zero, one = second_sum_b(back_b, kept_b, wg)
    one = send(one, lay.class_to_owner(near))
    zero = send(zero, lay.class_to_owner(0))
    feat_sum, wg_half = line_sum(three, two, one, zero, width)
    wg_other = send(wg_half, lay.plain(1, 0))
    feat_grad, weight_grad = finish(feat_sum, wg_half, wg_other)
    return act, feat_grad, weight_grad


def local_any(features, weight, tiles, pos, count, cotangent):
    reps = lax.axis_size("rep")
    lay = Layout(lax.axis_size("blk"), reps)
    r = lax.axis_index("rep")
    sections, tile = tiles.shape[0], tiles.shape[-1]
    rows = features.shape[0]
    blocks, share = rows // tile, rows // reps
    bf = jnp.bfloat16

    line = jnp.concatenate([send(features, lay.owner_to_class(at)) for at in range(sections)], 0)
    dense, _ = dense_blocks(tiles, section_table(pos, count, blocks, 0), 1, 1, blocks)
    size = line.shape[0]
    partial = aggregate(dense, [(0, 0, 0, size)], [line], None, jnp.float32)
    g = lax.psum(partial, "rep").astype(bf)
    value, slope = gelu_and_slope(dot(g, weight))
    cot = lax.all_gather(cotangent, "rep", axis=0, tiled=True)
    grad = (cot.astype(jnp.float32) * slope).astype(bf)
    act = lax.dynamic_slice_in_dim(value, r * share, share, 0).astype(bf)
    own_g = lax.dynamic_slice_in_dim(g, r * share, share, 0)
    own_grad = lax.dynamic_slice_in_dim(grad, r * share, share, 0)
    weight_grad = lax.psum(tn_dot(own_g, own_grad), AXES)
    back = nt_dot(weight, grad).astype(bf)
    terms = dot(back, dense[0]).astype(bf)
    total = jnp.zeros((back.shape[0], rows), jnp.float32)
    for at in range(sections):
        total += send(terms[:, at * rows:(at + 1) * rows], lay.class_to_owner(at)).astype(jnp.float32)
    feat_grad = lax.psum_scatter(total.T, "rep", scatter_dimension=0, tiled=True).astype(bf)
    return act, feat_grad, weight_grad


def local(features, weight, tile_vals, tile_pos, tile_count, cotangent):
    tiles, pos, count = tile_vals[0, 0], tile_pos[0, 0], tile_count[0, 0]
    reps, tile = lax.axis_size("rep"), tiles.shape[-1]
    paired = reps == 2 and tiles.shape[0] == 8 and features.shape[0] % (2 * tile) == 0
    work = local_pairs if paired else local_any
    return work(features, weight, tiles, pos, count, cotangent)


def solution(mesh):
    placed = (
        P("blk", None),
        P(),
        P("blk", "rep", None, None, None, None),
        P("blk", "rep", None, None),
        P("blk", "rep", None),
        P(("blk", "rep"), None),
    )
    return jax.shard_map(
        local,
        mesh=mesh,
        in_specs=placed,
        out_specs=(P(("blk", "rep"), None), P(("blk", "rep"), None), P()),
        check_vma=False,
    )
```

time: 79 us -> 59.7 us (0.76)
  the two profiles are of different devices: /device:TPU:11 before, /device:TPU:0 now
where the time goes in v2:
time: 59.7 us; the launch traced here: 59.5 us
  waiting for transfers between devices  24.9 us (42%)
  starting transfers between devices  24.1 us (40%)
  Pallas kernels  7.82 us (13%)
  local copies, waits for them, and re-layouts  0.93 us (2%)
  other arithmetic  0.9 us (2%)
  between operations  0.76 us (1%)
    ppermute x19, waiting for transfers between devices, send(): return lax.ppermute(value, AXES, route)  24.9 us
    ppermute x19, starting transfers between devices, send(): return lax.ppermute(value, AXES, route)  24.1 us
    pallas_call x1, Pallas kernels, dense_blocks(): pl.pallas_call(functools.partial(dense_kernel, blocks, near, halves), in_...  3.88 us
    pallas_call x2, Pallas kernels, aggregate(): pl.pallas_call(functools.partial(aggregate_kernel, spans, len(given) - le...  1.42 us
  transfers between devices with their start and end apart: 19, of which 12 were waited for; matrix products, arithmetic and copies ran while one was open for 2% of the time, Pallas kernels for 9%

profile of v2, /device:TPU:0, one launch (start us, length us, event | category | flops | bytes accessed | tf_op | source)
XLA Modules:
  0.0 59.5 jit_solution(11909898749058549420)
XLA Ops:
  0.6 0.0 copy-start
  0.7 0.9 %copy-done = bf16[512,128]{1,0:T(8,128)(2,1)S(1)} copy-done((bf16[512,128]{1,0:T(8,128)(2,1)S(1)}, bf16[512,128]{1,0:T(8,128)(2,1)}, u32[]{:S(2)}) %copy-start) | copy-done | bytes 131096
  1.5 5.0 %collective-permute-start.6 = (bf16[256,128]{1,0:T(8,128)(2,1)S(1)}, bf16[256,128]{1,0:T(8,128)(2,1)S(1)}, u32[]{:S(2)}, u32[]{:S(2)}) collective-permute-start(bf16[256,128]{1,0:T(8,128)(2,1)S(1)} %constant_dynamic-slice_fusion), channel_id=1, source_target_pairs={{0,24},{1,27},{2,26},{3,25},{4,28},{5,31},{6,30},{7,29},{8,16},{9,... | collective-permute-start | bytes 196616 | tf_op jit(solution)/shard_map/ppermute | solution.py:351
  6.6 0.0 collective-permute-start.5
  6.6 0.6 %collective-permute-start.1 = (bf16[256,128]{1,0:T(8,128)(2,1)S(1)}, bf16[256,128]{1,0:T(8,128)(2,1)S(1)}, u32[]{:S(2)}, u32[]{:S(2)}) collective-permute-start(bf16[256,128]{1,0:T(8,128)(2,1)S(1)} %constant_dynamic-slice_fusion), channel_id=1, source_target_pairs={{0,8},{1,11},{2,10},{3,9},{4,12},{5,15},{6,14},{7,13},{8,0},{9,3},... | collective-permute-start | bytes 196616 | tf_op jit(solution)/shard_map/ppermute | solution.py:351
  7.2 0.7 %collective-permute-start = (bf16[256,128]{1,0:T(8,128)(2,1)S(1)}, bf16[256,128]{1,0:T(8,128)(2,1)S(1)}, u32[]{:S(2)}, u32[]{:S(2)}) collective-permute-start(bf16[256,128]{1,0:T(8,128)(2,1)S(1)} %constant_dynamic-slice_fusion), channel_id=1, source_target_pairs={{0,0},{1,3},{2,2},{3,1},{4,4},{5,7},{6,6},{7,5},{8,8},{9,11},{10,1... | collective-permute-start | bytes 196616 | tf_op jit(solution)/shard_map/ppermute | solution.py:351
  7.9 2.8 %collective-permute-start.3 = (bf16[256,256]{1,0:T(8,128)(2,1)}, bf16[256,256]{1,0:T(8,128)(2,1)S(1)}, u32[]{:S(2)}, u32[]{:S(2)}) collective-permute-start(bf16[256,256]{1,0:T(8,128)(2,1)} %cot_ref.1), channel_id=1, source_target_pairs={{0,1},{1,0},{2,3},{3,2},{4,5},{5,4},{6,7},{7,6},{8,9},{9,8},{10,11... | collective-permute-start | bytes 393224 | tf_op jit(solution)/shard_map/ppermute | solution.py:351
  10.7 0.8 %bitcast_select_fusion = s32[8,12]{1,0:T(8,128)S(1)} fusion(s32[1,1,8,12]{3,2,1,0:T(8,128)} %param.9, s32[]{:T(128)S(6)} %mul.18, s32[8]{0:T(128)} %bitcast.5), kind=kLoop, calls=%fused_computation.16 | loop fusion | flops 288 | bytes 804 | tf_op jit(solution)/shard_map/jit(_where)/select_n | solution.py:361
  11.5 0.1 pad_add_fusion.table
  11.5 0.0 collective-permute-done.1
  11.5 0.0 collective-permute-done
  11.6 1.6 %collective-permute-start.2 = (bf16[512,128]{1,0:T(8,128)(2,1)S(1)}, bf16[512,128]{1,0:T(8,128)(2,1)S(1)}, u32[]{:S(2)}, u32[]{:S(2)}) collective-permute-start(bf16[512,128]{1,0:T(8,128)(2,1)S(1)} %pad_maximum_fusion.2.refs_0_), channel_id=1, source_target_pairs={{0,4},{1,2},{2,1},{3,7},{4,0},{5,6},{6,5},{7,3},{8,12},{9,10},{10,... | collective-permute-start | bytes 393224 | tf_op jit(solution)/shard_map/ppermute | solution.py:351
  13.1 0.0 collective-permute-done.5
  13.2 0.0 collective-permute-done.6
  13.2 0.6 %collective-permute-start.7 = (bf16[512,128]{1,0:T(8,128)(2,1)S(1)}, bf16[512,128]{1,0:T(8,128)(2,1)S(1)}, u32[]{:S(2)}, u32[]{:S(2)}) collective-permute-start(bf16[512,128]{1,0:T(8,128)(2,1)S(1)} %constant_dynamic-update-slice_fusion.refs_4_), channel_id=1, source_target_pairs={{0,4},{1,2},{2,1},{3,7},{4,0},{5,6},{6,5},{7,3},{8,12},{9,10},{10,... | collective-permute-start | bytes 393224 | tf_op jit(solution)/shard_map/ppermute | solution.py:351
  13.8 1.0 %collective-permute-done.3.far_cot_ref = bf16[256,256]{1,0:T(8,128)(2,1)S(1)} collective-permute-done((bf16[256,256]{1,0:T(8,128)(2,1)}, bf16[256,256]{1,0:T(8,128)(2,1)S(1)}, u32[]{:S(2)}, u32[]{:S(2)}) %collective-permute-start.3) | collective-permute-done | bytes 131104 | tf_op jit(solution)/shard_map/ppermute | solution.py:351
  14.8 1.8 %collective-permute-done.2.refs_1_ = bf16[512,128]{1,0:T(8,128)(2,1)S(1)} collective-permute-done((bf16[512,128]{1,0:T(8,128)(2,1)S(1)}, bf16[512,128]{1,0:T(8,128)(2,1)S(1)}, u32[]{:S(2)}, u32[]{:S(2)}) %collective-permute-start.2) | collective-permute-done | bytes 131104 | tf_op jit(solution)/shard_map/ppermute | solution.py:351
  16.6 0.2 collective-permute-start.4
  16.8 1.4 %collective-permute-done.7.refs_5_ = bf16[512,128]{1,0:T(8,128)(2,1)S(1)} collective-permute-done((bf16[512,128]{1,0:T(8,128)(2,1)S(1)}, bf16[512,128]{1,0:T(8,128)(2,1)S(1)}, u32[]{:S(2)}, u32[]{:S(2)}) %collective-permute-start.7) | collective-permute-done | bytes 131104 | tf_op jit(solution)/shard_map/ppermute | solution.py:351
  18.2 0.3 collective-permute-start.8
  18.5 3.9 %dense_blocks.1 = (bf16[4,512,1024]{2,1,0:T(8,128)(2,1)S(1)}, f32[8,128]{1,0:T(8,128)}) custom-call(s32[8,13]{1,0:T(8,128)S(1)} %pad_add_fusion.table, bf16[8,12,128,128]{3,2,1,0:T(8,128)(2,1)} %bitcast.4), custom_call_target="tpu_custom_call" | custom-call | tf_op jit(solution)/shard_map/dense_blocks/pallas_call | solution.py:80
  22.4 0.1 collective-permute-done.4.refs_2_.refs_3_
  22.5 1.0 %aggregate.2.refs_0_ = f32[512,128]{1,0:T(8,128)S(1)} custom-call(bf16[4,512,1024]{2,1,0:T(8,128)(2,1)S(1)} %get-tuple-element.27.dense_ref, bf16[512,128]{1,0:T(8,128)(2,1)S(1)} %pad_maximum_fusion.2.refs_0_, bf16[512,128]{1,0:T(8,128)(2,1)S(1)} %collective-permute-done.2.refs_1_, bf16[1024,128]{1,0:T(8,128)(2,1)S(1)} %collective-permute-done.4.refs_2_.refs_3_, ...), custom_call_target="tpu_custom_call" | custom-call | tf_op jit(solution)/shard_map/aggregate/pallas_call | solution.py:110
  23.5 1.8 %collective-permute-done.8.refs_1_.refs_2_ = bf16[1024,128]{1,0:T(8,128)(2,1)S(1)} collective-permute-done((bf16[1024,128]{1,0:T(8,128)(2,1)S(1)}, bf16[1024,128]{1,0:T(8,128)(2,1)S(1)}, u32[]{:S(2)}, u32[]{:S(2)}) %collective-permute-start.8) | collective-permute-done | bytes 262176 | tf_op jit(solution)/shard_map/ppermute | solution.py:351
  25.3 0.4 aggregate.3.own_ref
  25.7 2.0 %collective-permute-start.9 = (bf16[512,128]{1,0:T(8,128)(2,1)S(1)}, bf16[512,128]{1,0:T(8,128)(2,1)S(1)}, u32[]{:S(2)}, u32[]{:S(2)}) collective-permute-start(bf16[512,128]{1,0:T(8,128)(2,1)S(1)} %aggregate.3.own_ref), channel_id=1, source_target_pairs={{0,1},{1,0},{2,3},{3,2},{4,5},{5,4},{6,7},{7,6},{8,9},{9,8},{10,11... | collective-permute-start | bytes 393224 | tf_op jit(solution)/shard_map/ppermute | solution.py:351
  27.7 3.0 %collective-permute-done.9.other_ref = bf16[512,128]{1,0:T(8,128)(2,1)S(1)} collective-permute-done((bf16[512,128]{1,0:T(8,128)(2,1)S(1)}, bf16[512,128]{1,0:T(8,128)(2,1)S(1)}, u32[]{:S(2)}, u32[]{:S(2)}) %collective-permute-start.9) | collective-permute-done | bytes 131104 | tf_op jit(solution)/shard_map/ppermute | solution.py:351
  30.8 1.0 %turn.1 = (bf16[256,256]{1,0:T(8,128)(2,1)}, bf16[128,512]{1,0:T(8,128)(2,1)S(1)}, bf16[128,1280]{1,0:T(8,128)(2,1)S(1)}) custom-call(bf16[512,128]{1,0:T(8,128)(2,1)S(1)} %aggregate.3.own_ref, bf16[512,128]{1,0:T(8,128)(2,1)S(1)} %collective-permute-done.9.other_ref, bf16[128,256]{1,0:T(8,128)(2,1)S(1)} %copy-done.2, bf16[256,256]{1,0:T(8,128)(2,1)S(1)} %copy-done.1, ...), custom_call_target="tpu_custom_call" | custom-call | tf_op jit(solution)/shard_map/turn/pallas_call | solution.py:150
  31.8 0.0 collective-permute-start.10
  31.8 0.6 rest_terms.1
  32.4 1.8 %collective-permute-start.14 = (bf16[128,1024]{1,0:T(8,128)(2,1)S(1)}, bf16[128,1024]{1,0:T(8,128)(2,1)S(1)}, u32[]{:S(2)}, u32[]{:S(2)}) collective-permute-start(bf16[128,1024]{1,0:T(8,128)(2,1)S(1)} %get-tuple-element.39.own_ref), channel_id=1, source_target_pairs={{0,3},{1,5},{2,6},{3,0},{4,7},{5,1},{6,2},{7,4},{8,11},{9,13},{10,... | collective-permute-start | bytes 786440 | tf_op jit(solution)/shard_map/ppermute | solution.py:351
  34.2 4.1 %collective-permute-done.10.got_ref = bf16[128,1280]{1,0:T(8,128)(2,1)S(1)} collective-permute-done((bf16[128,1280]{1,0:T(8,128)(2,1)S(1)}, bf16[128,1280]{1,0:T(8,128)(2,1)S(1)}, u32[]{:S(2)}, u32[]{:S(2)}) %collective-permute-start.10) | collective-permute-done | bytes 327712 | tf_op jit(solution)/shard_map/ppermute | solution.py:351
  38.3 0.1 first_sum.2
  38.3 1.6 %collective-permute-start.11 = (bf16[128,768]{1,0:T(8,128)(2,1)S(1)}, bf16[128,768]{1,0:T(8,128)(2,1)S(1)}, u32[]{:S(2)}, u32[]{:S(2)}) collective-permute-start(bf16[128,768]{1,0:T(8,128)(2,1)S(1)} %get-tuple-element.35.own_ref), channel_id=1, source_target_pairs={{0,4},{1,2},{2,1},{3,7},{4,0},{5,6},{6,5},{7,3},{8,12},{9,10},{10,... | collective-permute-start | bytes 589832 | tf_op jit(solution)/shard_map/ppermute | solution.py:351
  39.9 1.2 %collective-permute-done.14.got_ref = bf16[128,1024]{1,0:T(8,128)(2,1)S(1)} collective-permute-done((bf16[128,1024]{1,0:T(8,128)(2,1)S(1)}, bf16[128,1024]{1,0:T(8,128)(2,1)S(1)}, u32[]{:S(2)}, u32[]{:S(2)}) %collective-permute-start.14) | collective-permute-done | bytes 262176 | tf_op jit(solution)/shard_map/ppermute | solution.py:351
  41.1 1.6 %collective-permute-start.15 = (bf16[128,512]{1,0:T(8,128)(2,1)S(1)}, bf16[128,512]{1,0:T(8,128)(2,1)S(1)}, u32[]{:S(2)}, u32[]{:S(2)}) collective-permute-start(bf16[128,512]{1,0:T(8,128)(2,1)S(1)} %get-tuple-element.40), channel_id=1, source_target_pairs={{0,4},{1,2},{2,1},{3,7},{4,0},{5,6},{6,5},{7,3},{8,12},{9,10},{10,... | collective-permute-start | bytes 393224 | tf_op jit(solution)/shard_map/ppermute | solution.py:351
  42.7 1.4 %collective-permute-done.11.got_ref = bf16[128,768]{1,0:T(8,128)(2,1)S(1)} collective-permute-done((bf16[128,768]{1,0:T(8,128)(2,1)S(1)}, bf16[128,768]{1,0:T(8,128)(2,1)S(1)}, u32[]{:S(2)}, u32[]{:S(2)}) %collective-permute-start.11) | collective-permute-done | bytes 196640 | tf_op jit(solution)/shard_map/ppermute | solution.py:351
  44.1 3.7 %collective-permute-start.12 = (bf16[192,256]{1,0:T(8,128)(2,1)S(1)}, bf16[192,256]{1,0:T(8,128)(2,1)S(1)}, u32[]{:S(2)}, u32[]{:S(2)}) collective-permute-start(bf16[192,256]{1,0:T(8,128)(2,1)S(1)} %get-tuple-element.37), channel_id=1, source_target_pairs={{0,24},{1,27},{2,26},{3,25},{4,28},{5,31},{6,30},{7,29},{8,16},{9,... | collective-permute-start | bytes 294920 | tf_op jit(solution)/shard_map/ppermute | solution.py:351
  47.8 0.0 collective-permute-start.13
  47.8 0.0 collective-permute-done.15.got_ref
  47.8 0.8 %collective-permute-start.16 = (bf16[192,256]{1,0:T(8,128)(2,1)S(1)}, bf16[192,256]{1,0:T(8,128)(2,1)S(1)}, u32[]{:S(2)}, u32[]{:S(2)}) collective-permute-start(bf16[192,256]{1,0:T(8,128)(2,1)S(1)} %get-tuple-element.43), channel_id=1, source_target_pairs={{0,8},{1,11},{2,10},{3,9},{4,12},{5,15},{6,14},{7,13},{8,0},{9,3},... | collective-permute-start | bytes 294920 | tf_op jit(solution)/shard_map/ppermute | solution.py:351
  48.7 0.7 %collective-permute-start.17 = (bf16[192,256]{1,0:T(8,128)(2,1)S(1)}, bf16[192,256]{1,0:T(8,128)(2,1)S(1)}, u32[]{:S(2)}, u32[]{:S(2)}) collective-permute-start(bf16[192,256]{1,0:T(8,128)(2,1)S(1)} %get-tuple-element.44), channel_id=1, source_target_pairs={{0,0},{1,3},{2,2},{3,1},{4,4},{5,7},{6,6},{7,5},{8,8},{9,11},{10,1... | collective-permute-start | bytes 294920 | tf_op jit(solution)/shard_map/ppermute | solution.py:351
  49.3 1.9 %collective-permute-done.12.three_ref = bf16[192,256]{1,0:T(8,128)(2,1)S(1)} collective-permute-done((bf16[192,256]{1,0:T(8,128)(2,1)S(1)}, bf16[192,256]{1,0:T(8,128)(2,1)S(1)}, u32[]{:S(2)}, u32[]{:S(2)}) %collective-permute-start.12) | collective-permute-done | bytes 98336 | tf_op jit(solution)/shard_map/ppermute | solution.py:351
  51.2 6.2 %collective-permute-done.13.two_ref = bf16[192,256]{1,0:T(8,128)(2,1)S(1)} collective-permute-done((bf16[192,256]{1,0:T(8,128)(2,1)S(1)}, bf16[192,256]{1,0:T(8,128)(2,1)S(1)}, u32[]{:S(2)}, u32[]{:S(2)}) %collective-permute-start.13) | collective-permute-done | bytes 98336 | tf_op jit(solution)/shard_map/ppermute | solution.py:351
  57.4 0.0 collective-permute-done.16.one_ref
  57.4 0.2 collective-permute-start.18
  57.6 1.1 %collective-permute-done.18.other_ref = f32[64,256]{1,0:T(8,128)S(1)} collective-permute-done((f32[64,256]{1,0:T(8,128)S(1)}, f32[64,256]{1,0:T(8,128)S(1)}, u32[]{:S(2)}, u32[]{:S(2)}) %collective-permute-start.18) | collective-permute-done | bytes 65568 | tf_op jit(solution)/shard_map/ppermute | solution.py:351
  58.7 0.7 %finish.1 = (bf16[256,128]{1,0:T(8,128)(2,1)}, f32[128,256]{1,0:T(8,128)}) custom-call(f32[128,256]{1,0:T(8,128)S(1)} %get-tuple-element.45.feat_sum_ref, f32[64,256]{1,0:T(8,128)S(1)} %get-tuple-element.46.half_ref, f32[64,256]{1,0:T(8,128)S(1)} %collective-permute-done.18.other_ref), custom_call_target="tpu_custom_call" | custom-call | tf_op jit(solution)/shard_map/finish/pallas_call | solution.py:299
  (16 shorter events, 0.3 us)
Async XLA Ops:
  0.6 0.9 %copy-start = (bf16[512,128]{1,0:T(8,128)(2,1)S(1)}, bf16[512,128]{1,0:T(8,128)(2,1)}, u32[]{:S(2)}) copy-start(bf16[512,128]{1,0:T(8,128)(2,1)} %param.6) | copy-start | bytes 393220
  1.5 11.6 %collective-permute-start.6 = (bf16[256,128]{1,0:T(8,128)(2,1)S(1)}, bf16[256,128]{1,0:T(8,128)(2,1)S(1)}, u32[]{:S(2)}, u32[]{:S(2)}) collective-permute-start(bf16[256,128]{1,0:T(8,128)(2,1)S(1)} %constant_dynamic-slice_fusion), channel_id=1, source_target_pairs={{0,24},{1,27},{2,26},{3,25},{4,28},{5,31},{6,30},{7,29},{8,16},{9,... | collective-permute-start | bytes 196616 | tf_op jit(solution)/shard_map/ppermute | solution.py:351
  6.6 6.6 %collective-permute-start.5 = (bf16[256,128]{1,0:T(8,128)(2,1)S(1)}, bf16[256,128]{1,0:T(8,128)(2,1)S(1)}, u32[]{:S(2)}, u32[]{:S(2)}) collective-permute-start(bf16[256,128]{1,0:T(8,128)(2,1)S(1)} %constant_dynamic-slice_fusion), channel_id=1, source_target_pairs={{0,16},{1,19},{2,18},{3,17},{4,20},{5,23},{6,22},{7,21},{8,24},{9,... | collective-permute-start | bytes 196616 | tf_op jit(solution)/shard_map/ppermute | solution.py:351
  6.6 4.9 %collective-permute-start.1 = (bf16[256,128]{1,0:T(8,128)(2,1)S(1)}, bf16[256,128]{1,0:T(8,128)(2,1)S(1)}, u32[]{:S(2)}, u32[]{:S(2)}) collective-permute-start(bf16[256,128]{1,0:T(8,128)(2,1)S(1)} %constant_dynamic-slice_fusion), channel_id=1, source_target_pairs={{0,8},{1,11},{2,10},{3,9},{4,12},{5,15},{6,14},{7,13},{8,0},{9,3},... | collective-permute-start | bytes 196616 | tf_op jit(solution)/shard_map/ppermute | solution.py:351
  7.2 4.3 %collective-permute-start = (bf16[256,128]{1,0:T(8,128)(2,1)S(1)}, bf16[256,128]{1,0:T(8,128)(2,1)S(1)}, u32[]{:S(2)}, u32[]{:S(2)}) collective-permute-start(bf16[256,128]{1,0:T(8,128)(2,1)S(1)} %constant_dynamic-slice_fusion), channel_id=1, source_target_pairs={{0,0},{1,3},{2,2},{3,1},{4,4},{5,7},{6,6},{7,5},{8,8},{9,11},{10,1... | collective-permute-start | bytes 196616 | tf_op jit(solution)/shard_map/ppermute | solution.py:351
  7.9 6.9 %collective-permute-start.3 = (bf16[256,256]{1,0:T(8,128)(2,1)}, bf16[256,256]{1,0:T(8,128)(2,1)S(1)}, u32[]{:S(2)}, u32[]{:S(2)}) collective-permute-start(bf16[256,256]{1,0:T(8,128)(2,1)} %cot_ref.1), channel_id=1, source_target_pairs={{0,1},{1,0},{2,3},{3,2},{4,5},{5,4},{6,7},{7,6},{8,9},{9,8},{10,11... | collective-permute-start | bytes 393224 | tf_op jit(solution)/shard_map/ppermute | solution.py:351
  11.6 5.0 %collective-permute-start.2 = (bf16[512,128]{1,0:T(8,128)(2,1)S(1)}, bf16[512,128]{1,0:T(8,128)(2,1)S(1)}, u32[]{:S(2)}, u32[]{:S(2)}) collective-permute-start(bf16[512,128]{1,0:T(8,128)(2,1)S(1)} %pad_maximum_fusion.2.refs_0_), channel_id=1, source_target_pairs={{0,4},{1,2},{2,1},{3,7},{4,0},{5,6},{6,5},{7,3},{8,12},{9,10},{10,... | collective-permute-start | bytes 393224 | tf_op jit(solution)/shard_map/ppermute | solution.py:351
  13.2 5.0 %collective-permute-start.7 = (bf16[512,128]{1,0:T(8,128)(2,1)S(1)}, bf16[512,128]{1,0:T(8,128)(2,1)S(1)}, u32[]{:S(2)}, u32[]{:S(2)}) collective-permute-start(bf16[512,128]{1,0:T(8,128)(2,1)S(1)} %constant_dynamic-update-slice_fusion.refs_4_), channel_id=1, source_target_pairs={{0,4},{1,2},{2,1},{3,7},{4,0},{5,6},{6,5},{7,3},{8,12},{9,10},{10,... | collective-permute-start | bytes 393224 | tf_op jit(solution)/shard_map/ppermute | solution.py:351
  16.6 5.9 %collective-permute-start.4 = (bf16[1024,128]{1,0:T(8,128)(2,1)S(1)}, bf16[1024,128]{1,0:T(8,128)(2,1)S(1)}, u32[]{:S(2)}, u32[]{:S(2)}) collective-permute-start(bf16[1024,128]{1,0:T(8,128)(2,1)S(1)} %pad_maximum_fusion), channel_id=1, source_target_pairs={{0,3},{1,5},{2,6},{3,0},{4,7},{5,1},{6,2},{7,4},{8,11},{9,13},{10,... | collective-permute-start | bytes 786440 | tf_op jit(solution)/shard_map/ppermute | solution.py:351
  18.2 7.0 %collective-permute-start.8 = (bf16[1024,128]{1,0:T(8,128)(2,1)S(1)}, bf16[1024,128]{1,0:T(8,128)(2,1)S(1)}, u32[]{:S(2)}, u32[]{:S(2)}) collective-permute-start(bf16[1024,128]{1,0:T(8,128)(2,1)S(1)} %pad_maximum_fusion.1), channel_id=1, source_target_pairs={{0,3},{1,5},{2,6},{3,0},{4,7},{5,1},{6,2},{7,4},{8,11},{9,13},{10,... | collective-permute-start | bytes 786440 | tf_op jit(solution)/shard_map/ppermute | solution.py:351
  22.5 8.3 %copy-start.1 = (bf16[256,256]{1,0:T(8,128)(2,1)S(1)}, bf16[256,256]{1,0:T(8,128)(2,1)}, u32[]{:S(2)}) copy-start(bf16[256,256]{1,0:T(8,128)(2,1)} %cot_ref.1) | copy-start | bytes 393220
  22.5 8.3 %copy-start.2 = (bf16[128,256]{1,0:T(8,128)(2,1)S(1)}, bf16[128,256]{1,0:T(8,128)(2,1)}, u32[]{:S(2)}) copy-start(bf16[128,256]{1,0:T(8,128)(2,1)} %weight_ref.1) | copy-start | bytes 196612
  25.7 5.0 %collective-permute-start.9 = (bf16[512,128]{1,0:T(8,128)(2,1)S(1)}, bf16[512,128]{1,0:T(8,128)(2,1)S(1)}, u32[]{:S(2)}, u32[]{:S(2)}) collective-permute-start(bf16[512,128]{1,0:T(8,128)(2,1)S(1)} %aggregate.3.own_ref), channel_id=1, source_target_pairs={{0,1},{1,0},{2,3},{3,2},{4,5},{5,4},{6,7},{7,6},{8,9},{9,8},{10,11... | collective-permute-start | bytes 393224 | tf_op jit(solution)/shard_map/ppermute | solution.py:351
  31.8 6.5 %collective-permute-start.10 = (bf16[128,1280]{1,0:T(8,128)(2,1)S(1)}, bf16[128,1280]{1,0:T(8,128)(2,1)S(1)}, u32[]{:S(2)}, u32[]{:S(2)}) collective-permute-start(bf16[128,1280]{1,0:T(8,128)(2,1)S(1)} %get-tuple-element.32.own_ref), channel_id=1, source_target_pairs={{0,3},{1,5},{2,6},{3,0},{4,7},{5,1},{6,2},{7,4},{8,11},{9,13},{10,... | collective-permute-start | bytes 983048 | tf_op jit(solution)/shard_map/ppermute | solution.py:351
  32.4 8.7 %collective-permute-start.14 = (bf16[128,1024]{1,0:T(8,128)(2,1)S(1)}, bf16[128,1024]{1,0:T(8,128)(2,1)S(1)}, u32[]{:S(2)}, u32[]{:S(2)}) collective-permute-start(bf16[128,1024]{1,0:T(8,128)(2,1)S(1)} %get-tuple-element.39.own_ref), channel_id=1, source_target_pairs={{0,3},{1,5},{2,6},{3,0},{4,7},{5,1},{6,2},{7,4},{8,11},{9,13},{10,... | collective-permute-start | bytes 786440 | tf_op jit(solution)/shard_map/ppermute | solution.py:351
  38.3 5.7 %collective-permute-start.11 = (bf16[128,768]{1,0:T(8,128)(2,1)S(1)}, bf16[128,768]{1,0:T(8,128)(2,1)S(1)}, u32[]{:S(2)}, u32[]{:S(2)}) collective-permute-start(bf16[128,768]{1,0:T(8,128)(2,1)S(1)} %get-tuple-element.35.own_ref), channel_id=1, source_target_pairs={{0,4},{1,2},{2,1},{3,7},{4,0},{5,6},{6,5},{7,3},{8,12},{9,10},{10,... | collective-permute-start | bytes 589832 | tf_op jit(solution)/shard_map/ppermute | solution.py:351
  41.1 6.6 %collective-permute-start.15 = (bf16[128,512]{1,0:T(8,128)(2,1)S(1)}, bf16[128,512]{1,0:T(8,128)(2,1)S(1)}, u32[]{:S(2)}, u32[]{:S(2)}) collective-permute-start(bf16[128,512]{1,0:T(8,128)(2,1)S(1)} %get-tuple-element.40), channel_id=1, source_target_pairs={{0,4},{1,2},{2,1},{3,7},{4,0},{5,6},{6,5},{7,3},{8,12},{9,10},{10,... | collective-permute-start | bytes 393224 | tf_op jit(solution)/shard_map/ppermute | solution.py:351
  44.1 7.1 %collective-permute-start.12 = (bf16[192,256]{1,0:T(8,128)(2,1)S(1)}, bf16[192,256]{1,0:T(8,128)(2,1)S(1)}, u32[]{:S(2)}, u32[]{:S(2)}) collective-permute-start(bf16[192,256]{1,0:T(8,128)(2,1)S(1)} %get-tuple-element.37), channel_id=1, source_target_pairs={{0,24},{1,27},{2,26},{3,25},{4,28},{5,31},{6,30},{7,29},{8,16},{9,... | collective-permute-start | bytes 294920 | tf_op jit(solution)/shard_map/ppermute | solution.py:351
  47.8 9.6 %collective-permute-start.13 = (bf16[192,256]{1,0:T(8,128)(2,1)S(1)}, bf16[192,256]{1,0:T(8,128)(2,1)S(1)}, u32[]{:S(2)}, u32[]{:S(2)}) collective-permute-start(bf16[192,256]{1,0:T(8,128)(2,1)S(1)} %get-tuple-element.38), channel_id=1, source_target_pairs={{0,16},{1,19},{2,18},{3,17},{4,20},{5,23},{6,22},{7,21},{8,24},{9,... | collective-permute-start | bytes 294920 | tf_op jit(solution)/shard_map/ppermute | solution.py:351
  47.8 9.6 %collective-permute-start.16 = (bf16[192,256]{1,0:T(8,128)(2,1)S(1)}, bf16[192,256]{1,0:T(8,128)(2,1)S(1)}, u32[]{:S(2)}, u32[]{:S(2)}) collective-permute-start(bf16[192,256]{1,0:T(8,128)(2,1)S(1)} %get-tuple-element.43), channel_id=1, source_target_pairs={{0,8},{1,11},{2,10},{3,9},{4,12},{5,15},{6,14},{7,13},{8,0},{9,3},... | collective-permute-start | bytes 294920 | tf_op jit(solution)/shard_map/ppermute | solution.py:351
  48.7 8.7 %collective-permute-start.17 = (bf16[192,256]{1,0:T(8,128)(2,1)S(1)}, bf16[192,256]{1,0:T(8,128)(2,1)S(1)}, u32[]{:S(2)}, u32[]{:S(2)}) collective-permute-start(bf16[192,256]{1,0:T(8,128)(2,1)S(1)} %get-tuple-element.44), channel_id=1, source_target_pairs={{0,0},{1,3},{2,2},{3,1},{4,4},{5,7},{6,6},{7,5},{8,8},{9,11},{10,1... | collective-permute-start | bytes 294920 | tf_op jit(solution)/shard_map/ppermute | solution.py:351
  57.4 1.3 %collective-permute-start.18 = (f32[64,256]{1,0:T(8,128)S(1)}, f32[64,256]{1,0:T(8,128)S(1)}, u32[]{:S(2)}, u32[]{:S(2)}) collective-permute-start(f32[64,256]{1,0:T(8,128)S(1)} %get-tuple-element.46.half_ref), channel_id=1, source_target_pairs={{0,2},{1,3},{2,0},{3,1},{4,6},{5,7},{6,4},{7,5},{8,10},{9,11},{10,... | collective-permute-start | bytes 196616 | tf_op jit(solution)/shard_map/ppermute | solution.py:351

commit v3 on v2

v3 whole, which is shorter than its diff:
```python
import functools

import jax
import jax.numpy as jnp
from jax import lax
from jax.experimental import pallas as pl
from jax.experimental.pallas import tpu as pltpu
from jax.sharding import PartitionSpec as P

AXES = ("blk", "rep")
VMEM_LIMIT = 16 * 1024 * 1024


def params():
    return pltpu.CompilerParams(vmem_limit_bytes=VMEM_LIMIT)


def in_vmem(count):
    return [pl.BlockSpec(memory_space=pltpu.VMEM)] * count


def held_in_vmem(value):
    return pltpu.with_memory_space_constraint(value, pltpu.VMEM)


def gelu_and_slope(v):
    scale = 0.7978845608028654
    square = v * v
    t = jnp.tanh(scale * (v + 0.044715 * (square * v)))
    half = 0.5 * (1.0 + t)
    slope = half + (0.5 * scale) * v * (1.0 - t * t) * (1.0 + 3.0 * 0.044715 * square)
    return v * half, slope


def nt_dot(a, b):
    return lax.dot_general(a, b, (((1,), (1,)), ((), ())), preferred_element_type=jnp.float32)


def tn_dot(a, b):
    return lax.dot_general(a, b, (((0,), (0,)), ((), ())), preferred_element_type=jnp.float32)


def dot(a, b):
    return jnp.dot(a, b, preferred_element_type=jnp.float32)


def split_by(value, size):
    if size & (size - 1):
        return lax.div(value, size), lax.rem(value, size)
    return lax.shift_right_logical(value, size.bit_length() - 1), value & (size - 1)


def dense_kernel(blocks, near, halves, table, tiles_ref, out_ref, held, arrived):
    sections, slots, tile = held.shape[0], held.shape[1], held.shape[-1]
    piece = out_ref.shape[2] // (sections // near)
    copies = [
        pltpu.make_async_copy(tiles_ref.at[section], held.at[section], arrived.at[section])
        for section in range(sections)
    ]
    for copy in copies:
        copy.start()
    out_ref[...] = jnp.zeros_like(out_ref)
    for section, copy in enumerate(copies):
        copy.wait()
        far_place, near_place = split_by(table[section, slots], near)
        for slot in range(slots):
            cell = table[section, slot]

            @pl.when(cell >= 0)
            def _():
                row, column = split_by(cell, blocks)
                half, column = split_by(column, blocks // halves)
                row_at = pl.multiple_of(row * tile, tile)
                column_at = pl.multiple_of(far_place * piece + column * tile, tile)
                out_ref[near_place * halves + half, pl.ds(row_at, tile), pl.ds(column_at, tile)] = held[section, slot]


def dense_blocks(tiles, table, near, halves, blocks):
    sections, _, tile, _ = tiles.shape
    rows = blocks * tile
    shape = (near * halves, rows, sections // near * rows // halves)
    return pl.pallas_call(
        functools.partial(dense_kernel, blocks, near, halves),
        in_specs=[pl.BlockSpec(memory_space=pltpu.SMEM), pl.BlockSpec(memory_space=pltpu.HBM)],
        out_specs=in_vmem(1)[0],
        out_shape=pltpu.VMEM(shape, jnp.bfloat16),
        scratch_shapes=[pltpu.VMEM(tiles.shape, tiles.dtype), pltpu.SemaphoreType.DMA((sections,))],
        compiler_params=params(),
        name="dense_blocks",
    )(table, pltpu.with_memory_space_constraint(tiles, pltpu.HBM))


def lane_of_class():
    return lax.rem(lax.axis_index("blk") + lax.axis_index("rep"), 2)


def unit_at(unit):
    if unit in (0, 3):
        return unit
    return 2 - lane_of_class() if unit == 1 else 1 + lane_of_class()


def aggregate_kernel(spans, based, dense_ref, *refs):
    given, out_ref = refs[:-1], refs[-1]
    total = given[0][...] if based else None
    halves = 2 if lax.axis_size("rep") == 2 and dense_ref.shape[0] > 1 else 1
    for at, first, start, base, size in spans:
        for half in range(halves):
            row = base if halves == 1 else pl.multiple_of(base + (half ^ lax.axis_index("rep")) * size, size)
            term = dot(dense_ref[first + half, :, pl.ds(start, size)], given[based + at][pl.ds(row, size), :])
            total = term if total is None else total + term
    out_ref[...] = total.astype(out_ref.dtype)


def aggregate(dense, spans, parts, base, dtype):
    rows, width = dense.shape[1], parts[0].shape[1]
    given = ([] if base is None else [base]) + parts
    return pl.pallas_call(
        functools.partial(aggregate_kernel, spans, len(given) - len(parts)),
        in_specs=in_vmem(1 + len(given)),
        out_specs=in_vmem(1)[0],
        out_shape=jax.ShapeDtypeStruct((rows, width), dtype),
        compiler_params=params(),
        name="aggregate",
    )(held_in_vmem(dense), *given)


def turn_kernel(share, chunk, own_ref, other_ref, weight_ref, cot_ref, far_cot_ref, dense_ref,
                act_ref, back_ref, sent_ref, g_ref, grad_ref):
    rows = own_ref.shape[0]
    weight = weight_ref[...]
    for half, cot in enumerate((cot_ref, far_cot_ref)):
        at, there = half * share, rows - share - half * share
        g = own_ref[pl.ds(at, share), :].astype(jnp.float32) + other_ref[pl.ds(there, share), :].astype(jnp.float32)
        g = g.astype(jnp.bfloat16)
        value, slope = gelu_and_slope(dot(g, weight))
        grad = (cot[...].astype(jnp.float32) * slope).astype(jnp.bfloat16)
        if half == 0:
            act_ref[...] = value.astype(jnp.bfloat16)
        g_ref[pl.ds(at, share), :] = g
        grad_ref[pl.ds(at, share), :] = grad
        back_ref[:, pl.ds(at, share)] = nt_dot(weight, grad).astype(jnp.bfloat16)
    back = back_ref[...]
    start, size = chunk
    for second in range(2):
        term = dot(back, dense_ref[unit_at(2 + second), :, pl.ds(start, size)])
        sent_ref[:, pl.ds(second * size, size)] = term.astype(jnp.bfloat16)
    part = sent_ref.shape[1] - 2 * size
    columns = pl.ds(pl.multiple_of(lane_of_class() * part, part), part)
    sent_ref[:, pl.ds(2 * size, part)] = tn_dot(g_ref[...], grad_ref[:, columns]).astype(jnp.bfloat16)


def turn(chunk, own, other, weight, cot, far_cot, dense):
    rows, width = own.shape
    share, hid = cot.shape
    bf = jnp.bfloat16
    return pl.pallas_call(
        functools.partial(turn_kernel, share, chunk),
        in_specs=in_vmem(6),
        out_specs=in_vmem(3),
        out_shape=[
            jax.ShapeDtypeStruct((share, hid), bf),
            jax.ShapeDtypeStruct((width, rows), bf),
            jax.ShapeDtypeStruct((width, 2 * chunk[1] + hid // 2), bf),
        ],
        scratch_shapes=[pltpu.VMEM((rows, width), bf), pltpu.VMEM((rows, hid), bf)],
        compiler_params=params(),
        name="turn",
    )(own, other, weight, cot, far_cot, held_in_vmem(dense))


def rest_kernel(chunks, back_ref, dense_ref, *refs):
    back = back_ref[...]
    for (start, size), sent in zip(chunks, refs[:-1]):
        for second in range(2):
            term = dot(back, dense_ref[unit_at(2 + second), :, pl.ds(start, size)])
            sent[:, pl.ds(second * size, size)] = term.astype(jnp.bfloat16)
    for second in range(2):
        refs[-1][second] = dot(back, dense_ref[unit_at(second)])


def rest_terms(chunks, back, dense):
    width, span = back.shape[0], dense.shape[2]
    return pl.pallas_call(
        functools.partial(rest_kernel, chunks),
        in_specs=in_vmem(2),
        out_specs=in_vmem(len(chunks) + 1),
        out_shape=[jax.ShapeDtypeStruct((width, 2 * size), jnp.bfloat16) for _, size in chunks]
        + [jax.ShapeDtypeStruct((2, width, span), jnp.float32)],
        compiler_params=params(),
        name="rest_terms",
    )(back, held_in_vmem(dense))


def first_sum_kernel(start, size, got_ref, kept_ref, own_ref, sent_ref, total_ref):
    extra = sent_ref.shape[1] - size
    total_ref[...] = kept_ref[0, :, pl.ds(start, size)] + got_ref[:, pl.ds(0, size)].astype(jnp.float32)
    passed = kept_ref[1, :, pl.ds(start, size)] + got_ref[:, pl.ds(size, size)].astype(jnp.float32)
    sent_ref[:, pl.ds(0, size)] = passed.astype(jnp.bfloat16)
    if extra:
        ours = own_ref[:, pl.ds(2 * size, extra)].astype(jnp.float32)
        theirs = got_ref[:, pl.ds(2 * size, extra)].astype(jnp.float32)
        sent_ref[:, pl.ds(size, extra)] = (ours + theirs).astype(jnp.bfloat16)


def first_sum(chunk, got, kept, own):
    width = kept.shape[1]
    start, size = chunk
    extra = got.shape[1] - 2 * size
    return pl.pallas_call(
        functools.partial(first_sum_kernel, start, size),
        in_specs=in_vmem(3),
        out_specs=in_vmem(2),
        out_shape=[
            jax.ShapeDtypeStruct((width, size + extra), jnp.bfloat16),
            jax.ShapeDtypeStruct((width, size), jnp.float32),
        ],
        compiler_params=params(),
        name="first_sum",
    )(got, kept, own)


def second_sum_kernel(got_ref, kept_ref, own_ref, two_ref, three_ref, wg_ref):
    piece = kept_ref.shape[1] // 2
    part = two_ref.shape[1] - piece
    tail = pl.ds(2 * piece, part)
    wg = own_ref[:, tail].astype(jnp.float32) + got_ref[:, tail].astype(jnp.float32)
    wg_ref[...] = wg.astype(jnp.bfloat16)
    for at, out in enumerate((two_ref, three_ref)):
        span = pl.ds(at * piece, piece)
        out[:, pl.ds(0, piece)] = (kept_ref[:, span] + got_ref[:, span].astype(jnp.float32)).astype(jnp.bfloat16)
        out[:, pl.ds(piece, part)] = wg.astype(jnp.bfloat16)


def second_sum(got, kept, own):
    width, size = kept.shape
    message = jax.ShapeDtypeStruct((width, got.shape[1] - size // 2), jnp.bfloat16)
    return pl.pallas_call(
        second_sum_kernel,
        in_specs=in_vmem(3),
        out_specs=in_vmem(3),
        out_shape=[message] * 2 + [jax.ShapeDtypeStruct((width, got.shape[1] - size), jnp.bfloat16)],
        compiler_params=params(),
        name="second_sum",
    )(got, kept, own)


def last_sum_kernel(got_ref, kept_ref, wg_ref, zero_ref, one_ref):
    piece = zero_ref.shape[1]
    tail = pl.ds(piece, one_ref.shape[1] - piece)
    zero_ref[...] = kept_ref[:, pl.ds(0, piece)] + got_ref[:, pl.ds(0, piece)].astype(jnp.float32)
    span = pl.ds(piece, piece)
    one_ref[:, pl.ds(0, piece)] = (kept_ref[:, span] + got_ref[:, span].astype(jnp.float32)).astype(jnp.bfloat16)
    one_ref[:, tail] = wg_ref[...]


def last_sum(got, kept, wg):
    width, size = kept.shape
    return pl.pallas_call(
        last_sum_kernel,
        in_specs=in_vmem(3),
        out_specs=in_vmem(2),
        out_shape=[
            jax.ShapeDtypeStruct((width, size // 2), jnp.float32),
            jax.ShapeDtypeStruct((width, size // 2 + wg.shape[1]), jnp.bfloat16),
        ],
        compiler_params=params(),
        name="last_sum",
    )(got, kept, wg)


def line_sum_kernel(three_ref, two_ref, one_ref, sent_one_ref, zero_ref, out_ref):
    piece = zero_ref.shape[1]
    span, tail = pl.ds(0, piece), pl.ds(piece, out_ref.shape[1] - piece)
    three, two, one = [ref[:, span].astype(jnp.float32) for ref in (three_ref, two_ref, one_ref)]
    out_ref[:, span] = ((zero_ref[...] + one) + (two + three)).astype(jnp.bfloat16)
    three, two, one, own = [ref[:, tail].astype(jnp.float32) for ref in (three_ref, two_ref, one_ref, sent_one_ref)]
    out_ref[:, tail] = ((own + one) + (two + three)).astype(jnp.bfloat16)


def line_sum(three, two, one, sent_one, zero):
    return pl.pallas_call(
        line_sum_kernel,
        in_specs=in_vmem(5),
        out_specs=in_vmem(1)[0],
        out_shape=jax.ShapeDtypeStruct(two.shape, jnp.bfloat16),
        compiler_params=params(),
        name="line_sum",
    )(three, two, one, sent_one, zero)


def finish_kernel(own_ref, got_ref, feat_ref, wg_ref):
    piece = feat_ref.shape[0]
    part = own_ref.shape[1] - piece
    lane = lane_of_class()
    wg_ref[:, pl.ds(pl.multiple_of(lane * part, part), part)] = own_ref[:, pl.ds(piece, part)].astype(jnp.float32)
    wg_ref[:, pl.ds(pl.multiple_of((1 - lane) * part, part), part)] = got_ref[:, pl.ds(piece, part)].astype(jnp.float32)
    span = pl.ds(0, piece)
    ours = jnp.where(lax.axis_index("rep") == 0, own_ref[:, span].astype(jnp.float32), got_ref[:, span].astype(jnp.float32))
    feat_ref[...] = ours.T.astype(jnp.bfloat16)


def finish(own, got, piece):
    width, total = own.shape
    return pl.pallas_call(
        finish_kernel,
        in_specs=in_vmem(2),
        out_specs=in_vmem(2),
        out_shape=[
            jax.ShapeDtypeStruct((piece, width), jnp.bfloat16),
            jax.ShapeDtypeStruct((width, 2 * (total - piece)), jnp.float32),
        ],
        compiler_params=params(),
        name="finish",
    )(own, got)


class Layout:
    def __init__(self, n_blk, reps):
        self.n_blk, self.reps = n_blk, reps

    def route(self, moved):
        pairs = []
        for b in range(self.n_blk):
            for r in range(self.reps):
                to_b, to_r = moved(b, r)
                pairs.append((b * self.reps + r, to_b * self.reps + to_r))
        return pairs

    def owner_to_class(self, mask):
        reps = self.reps
        return self.route(lambda b, r: (((b // reps) ^ mask) * reps + (b + r) % reps, r))

    def class_to_owner(self, mask):
        reps = self.reps
        return self.route(lambda b, r: (((b // reps) ^ mask) * reps + (b - r) % reps, r))

    def in_class(self, mask):
        return self.route(lambda b, r: (b ^ (mask * self.reps), r))

    def along(self, first):
        reps = self.reps

        def moved(b, r):
            lane = (b - r) % reps
            mask, rep_mask = (0, 1) if (lane == 0) == first else (1, 0)
            to_r = r ^ rep_mask
            return (((b // reps) ^ mask) * reps + (lane + to_r) % reps, to_r)

        return self.route(moved)

    def plain(self, mask, rep_mask):
        return self.route(lambda b, r: (b ^ mask, r ^ rep_mask))


def send(value, route):
    return lax.ppermute(value, AXES, route)


def section_table(pos, count, blocks, flip):
    reps, n_blk = lax.axis_size("rep"), lax.axis_size("blk")
    b, r = lax.axis_index("blk"), lax.axis_index("rep")
    sections, slots = pos.shape
    columns = (b - r - jnp.arange(sections, dtype=jnp.int32) * reps) % n_blk
    places = (columns // reps) ^ (b // reps)
    live = jnp.arange(slots, dtype=jnp.int32)[None, :] < count[:, None]
    cells = jnp.where(live, pos ^ (flip * (blocks + 1)), -1)
    return jnp.concatenate([cells, places[:, None]], 1).astype(jnp.int32)


def local_pairs(features, weight, tiles, pos, count, cotangent):
    near, halves = 2, 2
    lay = Layout(lax.axis_size("blk"), lax.axis_size("rep"))
    b, r = lax.axis_index("blk"), lax.axis_index("rep")
    sections, tile = tiles.shape[0], tiles.shape[-1]
    rows, width = features.shape
    blocks, share = rows // tile, rows // halves
    table = section_table(pos, count, blocks, r * (blocks // halves))
    two, one = [send(features, lay.owner_to_class(at * near)) for at in (2, 1)]
    whole, whole_beside = [send(features, lay.owner_to_class(at)) for at in range(2)]
    far_cot = send(cotangent, lay.plain(0, 1))
    three = send(two, lay.in_class(near))
    mine = jnp.concatenate([one, two], 0)
    beside = send(mine, lay.in_class(1))
    beside_three = send(three, lay.in_class(1))
    dense = dense_blocks(tiles, table, near, halves, blocks)
    spans = [(0, 0, 0, 0, share), (1, 2, 0, 0, share), (2, 0, share, 0, share), (2, 0, 2 * share, rows, share),
             (3, 2, share, 0, share), (3, 2, 2 * share, rows, share), (4, 0, 3 * share, 0, share)]
    partial = aggregate(dense, spans, [whole, whole_beside, mine, beside, three], None, jnp.float32)
    partial = aggregate(dense, [(0, 2, 3 * share, 0, share)], [beside_three], partial, jnp.bfloat16)
    other = send(partial, lay.plain(0, 1))
    chunk_a, chunk_b = (2 * share, 2 * share), (0, 2 * share)
    act, back, sent_a = turn(chunk_a, partial, other, weight, cotangent, far_cot, dense)
    got_a = send(sent_a, lay.along(True))
    sent_b, kept = rest_terms([chunk_b], back, dense)
    got_b = send(sent_b, lay.along(True))
    passed_a, kept_a = first_sum(chunk_a, got_a, kept, sent_a)
    back_a = send(passed_a, lay.along(False))
    passed_b, kept_b = first_sum(chunk_b, got_b, kept, sent_b)
    back_b = send(passed_b, lay.along(False))
    sent_two, sent_three, wg = second_sum(back_a, kept_a, passed_a)
    three = send(sent_three, lay.in_class(3 * near))
    two = send(sent_two, lay.in_class(2 * near))
    zero, sent_one = last_sum(back_b, kept_b, wg)
    one = send(sent_one, lay.in_class(near))
    ours = line_sum(three, two, one, sent_one, zero)
    feat_grad, weight_grad = finish(ours, send(ours, lay.plain(1, 0)), share)
    return act, feat_grad, weight_grad


def local_any(features, weight, tiles, pos, count, cotangent):
    reps = lax.axis_size("rep")
    lay = Layout(lax.axis_size("blk"), reps)
    r = lax.axis_index("rep")
    sections, tile = tiles.shape[0], tiles.shape[-1]
    rows = features.shape[0]
    blocks, share = rows // tile, rows // reps
    bf = jnp.bfloat16

    line = jnp.concatenate([send(features, lay.owner_to_class(at)) for at in range(sections)], 0)
    dense = dense_blocks(tiles, section_table(pos, count, blocks, 0), 1, 1, blocks)
    size = line.shape[0]
    partial = aggregate(dense, [(0, 0, 0, 0, size)], [line], None, jnp.float32)
    g = lax.psum(partial, "rep").astype(bf)
    value, slope = gelu_and_slope(dot(g, weight))
    cot = lax.all_gather(cotangent, "rep", axis=0, tiled=True)
    grad = (cot.astype(jnp.float32) * slope).astype(bf)
    act = lax.dynamic_slice_in_dim(value, r * share, share, 0).astype(bf)
    own_g = lax.dynamic_slice_in_dim(g, r * share, share, 0)
    own_grad = lax.dynamic_slice_in_dim(grad, r * share, share, 0)
    weight_grad = lax.psum(tn_dot(own_g, own_grad), AXES)
    back = nt_dot(weight, grad).astype(bf)
    terms = dot(back, dense[0]).astype(bf)
    total = jnp.zeros((back.shape[0], rows), jnp.float32)
    for at in range(sections):
        total += send(terms[:, at * rows:(at + 1) * rows], lay.class_to_owner(at)).astype(jnp.float32)
    feat_grad = lax.psum_scatter(total.T, "rep", scatter_dimension=0, tiled=True).astype(bf)
    return act, feat_grad, weight_grad


def local(features, weight, tile_vals, tile_pos, tile_count, cotangent):
    tiles, pos, count = tile_vals[0, 0], tile_pos[0, 0], tile_count[0, 0]
    reps, tile = lax.axis_size("rep"), tiles.shape[-1]
    paired = reps == 2 and tiles.shape[0] == 8 and features.shape[0] % (2 * tile) == 0
    work = local_pairs if paired else local_any
    return work(features, weight, tiles, pos, count, cotangent)


def solution(mesh):
    placed = (
        P("blk", None),
        P(),
        P("blk", "rep", None, None, None, None),
        P("blk", "rep", None, None),
        P("blk", "rep", None),
        P(("blk", "rep"), None),
    )
    return jax.shard_map(
        local,
        mesh=mesh,
        in_specs=placed,
        out_specs=(P(("blk", "rep"), None), P(("blk", "rep"), None), P()),
        check_vma=False,
    )
```

time: 59.7 us -> 56.8 us (0.951)
  waiting for transfers between devices: 24.9 us -> 23.8 us
  local copies, waits for them, and re-layouts: 0.93 us -> 0.04 us
    ppermute x19 -> x17, waiting for transfers between devices: 24.9 us -> 23.8 us  [send(): return lax.ppermute(value, AXES, route)]
    pallas_call x1, Pallas kernels: 3.88 us -> 2.98 us  [dense_blocks(): pl.pallas_call(functools.partial(dense_kernel, blocks, near, halves), in_...]
    unnamed x7 -> x5, local copies, waits for them, and re-layouts: 0.91 us -> 0.02 us
    ppermute x19 -> x17, starting transfers between devices: 24.1 us -> 23.9 us  [send(): return lax.ppermute(value, AXES, route)]
  transfers between devices with their start and end apart: 19 -> 17, of which waited for: 12 -> 10; matrix products, arithmetic and copies ran while one was open for 2% -> 2% of each run, Pallas kernels for 9% -> 9%
where the time goes in v3:
time: 56.8 us; the launch traced here: 56.6 us
  starting transfers between devices  23.9 us (42%)
  waiting for transfers between devices  23.8 us (42%)
  Pallas kernels  7.27 us (13%)
  other arithmetic  0.86 us (2%)
  between operations  0.75 us (1%)
    ppermute x17, starting transfers between devices, send(): return lax.ppermute(value, AXES, route)  23.9 us
    ppermute x17, waiting for transfers between devices, send(): return lax.ppermute(value, AXES, route)  23.8 us
    pallas_call x1, Pallas kernels, dense_blocks(): pl.pallas_call(functools.partial(dense_kernel, blocks, near, halves), in_...  2.98 us
    pallas_call x2, Pallas kernels, aggregate(): pl.pallas_call(functools.partial(aggregate_kernel, spans, len(given) - le...  1.42 us
    pallas_call x1, Pallas kernels, turn(): pl.pallas_call(functools.partial(turn_kernel, share, chunk), in_specs=in_...  1.35 us
  transfers between devices with their start and end apart: 17, of which 10 were waited for; matrix products, arithmetic and copies ran while one was open for 2% of the time, Pallas kernels for 9%

profile of v3, /device:TPU:0, one launch (start us, length us, event | category | flops | bytes accessed | tf_op | source)
XLA Modules:
  0.0 56.6 jit_solution(17797816042521402818)
XLA Ops:
  0.6 3.1 %collective-permute-start.2 = (bf16[512,128]{1,0:T(8,128)(2,1)}, bf16[512,128]{1,0:T(8,128)(2,1)S(1)}, u32[]{:S(2)}, u32[]{:S(2)}) collective-permute-start(bf16[512,128]{1,0:T(8,128)(2,1)} %param.6), channel_id=1, source_target_pairs={{0,8},{1,11},{2,10},{3,9},{4,12},{5,15},{6,14},{7,13},{8,0},{9,3},... | collective-permute-start | bytes 393224 | tf_op jit(solution)/shard_map/ppermute | solution.py:357
  3.7 2.6 %collective-permute-start.3 = (bf16[512,128]{1,0:T(8,128)(2,1)}, bf16[512,128]{1,0:T(8,128)(2,1)S(1)}, u32[]{:S(2)}, u32[]{:S(2)}) collective-permute-start(bf16[512,128]{1,0:T(8,128)(2,1)} %param.6), channel_id=1, source_target_pairs={{0,16},{1,19},{2,18},{3,17},{4,20},{5,23},{6,22},{7,21},{8,24},{9,... | collective-permute-start | bytes 393224 | tf_op jit(solution)/shard_map/ppermute | solution.py:357
  6.3 1.5 %collective-permute-start.1 = (bf16[512,128]{1,0:T(8,128)(2,1)}, bf16[512,128]{1,0:T(8,128)(2,1)S(1)}, u32[]{:S(2)}, u32[]{:S(2)}) collective-permute-start(bf16[512,128]{1,0:T(8,128)(2,1)} %param.6), channel_id=1, source_target_pairs={{0,4},{1,7},{2,6},{3,5},{4,0},{5,3},{6,2},{7,1},{8,12},{9,15},{10,... | collective-permute-start | bytes 393224 | tf_op jit(solution)/shard_map/ppermute | solution.py:357
  7.8 1.6 %collective-permute-start = (bf16[512,128]{1,0:T(8,128)(2,1)}, bf16[512,128]{1,0:T(8,128)(2,1)S(1)}, u32[]{:S(2)}, u32[]{:S(2)}) collective-permute-start(bf16[512,128]{1,0:T(8,128)(2,1)} %param.6), channel_id=1, source_target_pairs={{0,0},{1,3},{2,2},{3,1},{4,4},{5,7},{6,6},{7,5},{8,8},{9,11},{10,1... | collective-permute-start | bytes 393224 | tf_op jit(solution)/shard_map/ppermute | solution.py:357
  9.4 1.7 %collective-permute-start.8 = (bf16[256,256]{1,0:T(8,128)(2,1)}, bf16[256,256]{1,0:T(8,128)(2,1)S(1)}, u32[]{:S(2)}, u32[]{:S(2)}) collective-permute-start(bf16[256,256]{1,0:T(8,128)(2,1)} %cot_ref.1), channel_id=1, source_target_pairs={{0,1},{1,0},{2,3},{3,2},{4,5},{5,4},{6,7},{7,6},{8,9},{9,8},{10,11... | collective-permute-start | bytes 393224 | tf_op jit(solution)/shard_map/ppermute | solution.py:357
  11.1 0.0 collective-permute-done.2
  11.1 1.5 %collective-permute-done.3 = bf16[512,128]{1,0:T(8,128)(2,1)S(1)} collective-permute-done((bf16[512,128]{1,0:T(8,128)(2,1)}, bf16[512,128]{1,0:T(8,128)(2,1)S(1)}, u32[]{:S(2)}, u32[]{:S(2)}) %collective-permute-start.3) | collective-permute-done | bytes 131104 | tf_op jit(solution)/shard_map/ppermute | solution.py:357
  12.7 1.6 %collective-permute-start.4 = (bf16[1024,128]{1,0:T(8,128)(2,1)S(1)}, bf16[1024,128]{1,0:T(8,128)(2,1)S(1)}, u32[]{:S(2)}, u32[]{:S(2)}) collective-permute-start(bf16[1024,128]{1,0:T(8,128)(2,1)S(1)} %constant_dynamic-update-slice_fusion.refs_2_), channel_id=1, source_target_pairs={{0,4},{1,5},{2,6},{3,7},{4,0},{5,1},{6,2},{7,3},{8,12},{9,13},{10,... | collective-permute-start | bytes 786440 | tf_op jit(solution)/shard_map/ppermute | solution.py:357
  14.3 0.4 collective-permute-start.5
  14.7 0.8 %bitcast_select_fusion = s32[8,12]{1,0:T(8,128)S(1)} fusion(s32[1,1,8,12]{3,2,1,0:T(8,128)} %param.9, s32[]{:T(128)S(6)} %mul.14, s32[8]{0:T(128)} %bitcast.5), kind=kLoop, calls=%fused_computation.13 | loop fusion | flops 288 | bytes 804 | tf_op jit(solution)/shard_map/jit(_where)/select_n | solution.py:367
  15.5 3.8 %collective-permute-done.5.refs_4_ = bf16[512,128]{1,0:T(8,128)(2,1)S(1)} collective-permute-done((bf16[512,128]{1,0:T(8,128)(2,1)S(1)}, bf16[512,128]{1,0:T(8,128)(2,1)S(1)}, u32[]{:S(2)}, u32[]{:S(2)}) %collective-permute-start.5) | collective-permute-done | bytes 131104 | tf_op jit(solution)/shard_map/ppermute | solution.py:357
  19.2 0.5 collective-permute-start.6
  19.8 0.1 pad_add_fusion.table
  19.8 3.0 %dense_blocks.1.dense_ref = bf16[4,512,1024]{2,1,0:T(8,128)(2,1)S(1)} custom-call(s32[8,13]{1,0:T(8,128)S(1)} %pad_add_fusion.table, bf16[8,12,128,128]{3,2,1,0:T(8,128)(2,1)} %bitcast.4), custom_call_target="tpu_custom_call" | custom-call | tf_op jit(solution)/shard_map/dense_blocks/pallas_call | solution.py:82
  22.8 0.0 copy-start
  22.8 0.0 copy-start.1
  22.8 0.0 collective-permute-done.1.refs_1_
  22.9 0.0 collective-permute-done.refs_0_
  22.9 0.0 collective-permute-done.4.refs_3_
  22.9 1.1 %aggregate.2.refs_0_ = f32[512,128]{1,0:T(8,128)S(1)} custom-call(bf16[4,512,1024]{2,1,0:T(8,128)(2,1)S(1)} %dense_blocks.1.dense_ref, bf16[512,128]{1,0:T(8,128)(2,1)S(1)} %collective-permute-done.refs_0_, bf16[512,128]{1,0:T(8,128)(2,1)S(1)} %collective-permute-done.1.refs_1_, bf16[1024,128]{1,0:T(8,128)(2,1)S(1)} %constant_dynamic-update-slice_fusion.refs_2_, ...), custom_call_target="tpu_custom_call" | custom-call | tf_op jit(solution)/shard_map/aggregate/pallas_call | solution.py:118
  24.0 0.2 collective-permute-done.6.refs_1_
  24.2 0.3 aggregate.3.own_ref
  24.5 2.1 %collective-permute-start.7 = (bf16[512,128]{1,0:T(8,128)(2,1)S(1)}, bf16[512,128]{1,0:T(8,128)(2,1)S(1)}, u32[]{:S(2)}, u32[]{:S(2)}) collective-permute-start(bf16[512,128]{1,0:T(8,128)(2,1)S(1)} %aggregate.3.own_ref), channel_id=1, source_target_pairs={{0,1},{1,0},{2,3},{3,2},{4,5},{5,4},{6,7},{7,6},{8,9},{9,8},{10,11... | collective-permute-start | bytes 393224 | tf_op jit(solution)/shard_map/ppermute | solution.py:357
  26.6 0.0 collective-permute-done.8.far_cot_ref
  26.6 2.9 %collective-permute-done.7.other_ref = bf16[512,128]{1,0:T(8,128)(2,1)S(1)} collective-permute-done((bf16[512,128]{1,0:T(8,128)(2,1)S(1)}, bf16[512,128]{1,0:T(8,128)(2,1)S(1)}, u32[]{:S(2)}, u32[]{:S(2)}) %collective-permute-start.7) | collective-permute-done | bytes 131104 | tf_op jit(solution)/shard_map/ppermute | solution.py:357
  29.5 0.0 copy-done
  29.6 0.0 copy-done.1
  29.6 1.3 %turn.1 = (bf16[256,256]{1,0:T(8,128)(2,1)}, bf16[128,512]{1,0:T(8,128)(2,1)S(1)}, bf16[128,1152]{1,0:T(8,128)(2,1)S(1)}) custom-call(bf16[512,128]{1,0:T(8,128)(2,1)S(1)} %aggregate.3.own_ref, bf16[512,128]{1,0:T(8,128)(2,1)S(1)} %collective-permute-done.7.other_ref, bf16[128,256]{1,0:T(8,128)(2,1)S(1)} %copy-done.1, bf16[256,256]{1,0:T(8,128)(2,1)S(1)} %copy-done, ...), custom_call_target="tpu_custom_call" | custom-call | tf_op jit(solution)/shard_map/turn/pallas_call | solution.py:157
  30.9 0.0 collective-permute-start.9
  30.9 0.6 %rest_terms.1 = (bf16[128,1024]{1,0:T(8,128)(2,1)S(1)}, f32[2,128,1024]{2,1,0:T(8,128)S(1)}) custom-call(bf16[128,512]{1,0:T(8,128)(2,1)S(1)} %get-tuple-element.21.back_ref, bf16[4,512,1024]{2,1,0:T(8,128)(2,1)S(1)} %dense_blocks.1.dense_ref), custom_call_target="tpu_custom_call" | custom-call | tf_op jit(solution)/shard_map/rest_terms/pallas_call | solution.py:184
  31.5 1.8 %collective-permute-start.13 = (bf16[128,1024]{1,0:T(8,128)(2,1)S(1)}, bf16[128,1024]{1,0:T(8,128)(2,1)S(1)}, u32[]{:S(2)}, u32[]{:S(2)}) collective-permute-start(bf16[128,1024]{1,0:T(8,128)(2,1)S(1)} %get-tuple-element.27.own_ref), channel_id=1, source_target_pairs={{0,3},{1,5},{2,6},{3,0},{4,7},{5,1},{6,2},{7,4},{8,11},{9,13},{10,... | collective-permute-start | bytes 786440 | tf_op jit(solution)/shard_map/ppermute | solution.py:357
  33.3 3.7 %collective-permute-done.9.got_ref = bf16[128,1152]{1,0:T(8,128)(2,1)S(1)} collective-permute-done((bf16[128,1152]{1,0:T(8,128)(2,1)S(1)}, bf16[128,1152]{1,0:T(8,128)(2,1)S(1)}, u32[]{:S(2)}, u32[]{:S(2)}) %collective-permute-start.9) | collective-permute-done | bytes 294944 | tf_op jit(solution)/shard_map/ppermute | solution.py:357
  37.0 0.1 first_sum.2
  37.1 1.1 %collective-permute-start.10 = (bf16[128,640]{1,0:T(8,128)(2,1)S(1)}, bf16[128,640]{1,0:T(8,128)(2,1)S(1)}, u32[]{:S(2)}, u32[]{:S(2)}) collective-permute-start(bf16[128,640]{1,0:T(8,128)(2,1)S(1)} %get-tuple-element.23.own_ref), channel_id=1, source_target_pairs={{0,4},{1,2},{2,1},{3,7},{4,0},{5,6},{6,5},{7,3},{8,12},{9,10},{10,... | collective-permute-start | bytes 491528 | tf_op jit(solution)/shard_map/ppermute | solution.py:357
  38.2 1.6 %collective-permute-done.13.got_ref = bf16[128,1024]{1,0:T(8,128)(2,1)S(1)} collective-permute-done((bf16[128,1024]{1,0:T(8,128)(2,1)S(1)}, bf16[128,1024]{1,0:T(8,128)(2,1)S(1)}, u32[]{:S(2)}, u32[]{:S(2)}) %collective-permute-start.13) | collective-permute-done | bytes 262176 | tf_op jit(solution)/shard_map/ppermute | solution.py:357
  39.9 1.1 %collective-permute-start.14 = (bf16[128,512]{1,0:T(8,128)(2,1)S(1)}, bf16[128,512]{1,0:T(8,128)(2,1)S(1)}, u32[]{:S(2)}, u32[]{:S(2)}) collective-permute-start(bf16[128,512]{1,0:T(8,128)(2,1)S(1)} %get-tuple-element.28), channel_id=1, source_target_pairs={{0,4},{1,2},{2,1},{3,7},{4,0},{5,6},{6,5},{7,3},{8,12},{9,10},{10,... | collective-permute-start | bytes 393224 | tf_op jit(solution)/shard_map/ppermute | solution.py:357
  41.0 1.4 %collective-permute-done.10.got_ref = bf16[128,640]{1,0:T(8,128)(2,1)S(1)} collective-permute-done((bf16[128,640]{1,0:T(8,128)(2,1)S(1)}, bf16[128,640]{1,0:T(8,128)(2,1)S(1)}, u32[]{:S(2)}, u32[]{:S(2)}) %collective-permute-start.10) | collective-permute-done | bytes 163872 | tf_op jit(solution)/shard_map/ppermute | solution.py:357
  42.5 2.5 %collective-permute-start.11 = (bf16[128,384]{1,0:T(8,128)(2,1)S(1)}, bf16[128,384]{1,0:T(8,128)(2,1)S(1)}, u32[]{:S(2)}, u32[]{:S(2)}) collective-permute-start(bf16[128,384]{1,0:T(8,128)(2,1)S(1)} %get-tuple-element.25), channel_id=1, source_target_pairs={{0,24},{1,25},{2,26},{3,27},{4,28},{5,29},{6,30},{7,31},{8,16},{9,... | collective-permute-start | bytes 294920 | tf_op jit(solution)/shard_map/ppermute | solution.py:357
  45.0 0.0 collective-permute-start.12
  45.0 0.0 collective-permute-done.14.got_ref
  45.1 2.0 %collective-permute-start.15 = (bf16[128,384]{1,0:T(8,128)(2,1)S(1)}, bf16[128,384]{1,0:T(8,128)(2,1)S(1)}, u32[]{:S(2)}, u32[]{:S(2)}) collective-permute-start(bf16[128,384]{1,0:T(8,128)(2,1)S(1)} %get-tuple-element.31.sent_one_ref), channel_id=1, source_target_pairs={{0,8},{1,9},{2,10},{3,11},{4,12},{5,13},{6,14},{7,15},{8,0},{9,1},... | collective-permute-start | bytes 294920 | tf_op jit(solution)/shard_map/ppermute | solution.py:357
  47.1 2.1 %collective-permute-done.11.three_ref = bf16[128,384]{1,0:T(8,128)(2,1)S(1)} collective-permute-done((bf16[128,384]{1,0:T(8,128)(2,1)S(1)}, bf16[128,384]{1,0:T(8,128)(2,1)S(1)}, u32[]{:S(2)}, u32[]{:S(2)}) %collective-permute-start.11) | collective-permute-done | bytes 98336 | tf_op jit(solution)/shard_map/ppermute | solution.py:357
  49.1 5.3 %collective-permute-done.12.two_ref = bf16[128,384]{1,0:T(8,128)(2,1)S(1)} collective-permute-done((bf16[128,384]{1,0:T(8,128)(2,1)S(1)}, bf16[128,384]{1,0:T(8,128)(2,1)S(1)}, u32[]{:S(2)}, u32[]{:S(2)}) %collective-permute-start.12) | collective-permute-done | bytes 98336 | tf_op jit(solution)/shard_map/ppermute | solution.py:357
  54.4 0.0 collective-permute-done.15.one_ref
  54.5 0.2 collective-permute-start.16
  54.7 1.2 %collective-permute-done.16.got_ref = bf16[128,384]{1,0:T(8,128)(2,1)S(1)} collective-permute-done((bf16[128,384]{1,0:T(8,128)(2,1)S(1)}, bf16[128,384]{1,0:T(8,128)(2,1)S(1)}, u32[]{:S(2)}, u32[]{:S(2)}) %collective-permute-start.16) | collective-permute-done | bytes 98336 | tf_op jit(solution)/shard_map/ppermute | solution.py:357
  55.9 0.7 %finish.1 = (bf16[256,128]{1,0:T(8,128)(2,1)}, f32[128,256]{1,0:T(8,128)}) custom-call(bf16[128,384]{1,0:T(8,128)(2,1)S(1)} %line_sum.1.own_ref, bf16[128,384]{1,0:T(8,128)(2,1)S(1)} %collective-permute-done.16.got_ref), custom_call_target="tpu_custom_call" | custom-call | tf_op jit(solution)/shard_map/finish/pallas_call | solution.py:305
  (7 shorter events, 0.2 us)
Async XLA Ops:
  0.6 10.5 %collective-permute-start.2 = (bf16[512,128]{1,0:T(8,128)(2,1)}, bf16[512,128]{1,0:T(8,128)(2,1)S(1)}, u32[]{:S(2)}, u32[]{:S(2)}) collective-permute-start(bf16[512,128]{1,0:T(8,128)(2,1)} %param.6), channel_id=1, source_target_pairs={{0,8},{1,11},{2,10},{3,9},{4,12},{5,15},{6,14},{7,13},{8,0},{9,3},... | collective-permute-start | bytes 393224 | tf_op jit(solution)/shard_map/ppermute | solution.py:357
  3.7 8.9 %collective-permute-start.3 = (bf16[512,128]{1,0:T(8,128)(2,1)}, bf16[512,128]{1,0:T(8,128)(2,1)S(1)}, u32[]{:S(2)}, u32[]{:S(2)}) collective-permute-start(bf16[512,128]{1,0:T(8,128)(2,1)} %param.6), channel_id=1, source_target_pairs={{0,16},{1,19},{2,18},{3,17},{4,20},{5,23},{6,22},{7,21},{8,24},{9,... | collective-permute-start | bytes 393224 | tf_op jit(solution)/shard_map/ppermute | solution.py:357
  6.3 16.5 %collective-permute-start.1 = (bf16[512,128]{1,0:T(8,128)(2,1)}, bf16[512,128]{1,0:T(8,128)(2,1)S(1)}, u32[]{:S(2)}, u32[]{:S(2)}) collective-permute-start(bf16[512,128]{1,0:T(8,128)(2,1)} %param.6), channel_id=1, source_target_pairs={{0,4},{1,7},{2,6},{3,5},{4,0},{5,3},{6,2},{7,1},{8,12},{9,15},{10,... | collective-permute-start | bytes 393224 | tf_op jit(solution)/shard_map/ppermute | solution.py:357
  7.8 15.0 %collective-permute-start = (bf16[512,128]{1,0:T(8,128)(2,1)}, bf16[512,128]{1,0:T(8,128)(2,1)S(1)}, u32[]{:S(2)}, u32[]{:S(2)}) collective-permute-start(bf16[512,128]{1,0:T(8,128)(2,1)} %param.6), channel_id=1, source_target_pairs={{0,0},{1,3},{2,2},{3,1},{4,4},{5,7},{6,6},{7,5},{8,8},{9,11},{10,1... | collective-permute-start | bytes 393224 | tf_op jit(solution)/shard_map/ppermute | solution.py:357
  9.4 17.2 %collective-permute-start.8 = (bf16[256,256]{1,0:T(8,128)(2,1)}, bf16[256,256]{1,0:T(8,128)(2,1)S(1)}, u32[]{:S(2)}, u32[]{:S(2)}) collective-permute-start(bf16[256,256]{1,0:T(8,128)(2,1)} %cot_ref.1), channel_id=1, source_target_pairs={{0,1},{1,0},{2,3},{3,2},{4,5},{5,4},{6,7},{7,6},{8,9},{9,8},{10,11... | collective-permute-start | bytes 393224 | tf_op jit(solution)/shard_map/ppermute | solution.py:357
  12.7 10.2 %collective-permute-start.4 = (bf16[1024,128]{1,0:T(8,128)(2,1)S(1)}, bf16[1024,128]{1,0:T(8,128)(2,1)S(1)}, u32[]{:S(2)}, u32[]{:S(2)}) collective-permute-start(bf16[1024,128]{1,0:T(8,128)(2,1)S(1)} %constant_dynamic-update-slice_fusion.refs_2_), channel_id=1, source_target_pairs={{0,4},{1,5},{2,6},{3,7},{4,0},{5,1},{6,2},{7,3},{8,12},{9,13},{10,... | collective-permute-start | bytes 786440 | tf_op jit(solution)/shard_map/ppermute | solution.py:357
  14.3 5.0 %collective-permute-start.5 = (bf16[512,128]{1,0:T(8,128)(2,1)S(1)}, bf16[512,128]{1,0:T(8,128)(2,1)S(1)}, u32[]{:S(2)}, u32[]{:S(2)}) collective-permute-start(bf16[512,128]{1,0:T(8,128)(2,1)S(1)} %collective-permute-done.3), channel_id=1, source_target_pairs={{0,8},{1,9},{2,10},{3,11},{4,12},{5,13},{6,14},{7,15},{8,0},{9,1},... | collective-permute-start | bytes 393224 | tf_op jit(solution)/shard_map/ppermute | solution.py:357
  19.2 5.0 %collective-permute-start.6 = (bf16[512,128]{1,0:T(8,128)(2,1)S(1)}, bf16[512,128]{1,0:T(8,128)(2,1)S(1)}, u32[]{:S(2)}, u32[]{:S(2)}) collective-permute-start(bf16[512,128]{1,0:T(8,128)(2,1)S(1)} %collective-permute-done.5.refs_4_), channel_id=1, source_target_pairs={{0,4},{1,5},{2,6},{3,7},{4,0},{5,1},{6,2},{7,3},{8,12},{9,13},{10,... | collective-permute-start | bytes 393224 | tf_op jit(solution)/shard_map/ppermute | solution.py:357
  22.8 6.7 %copy-start = (bf16[256,256]{1,0:T(8,128)(2,1)S(1)}, bf16[256,256]{1,0:T(8,128)(2,1)}, u32[]{:S(2)}) copy-start(bf16[256,256]{1,0:T(8,128)(2,1)} %cot_ref.1) | copy-start | bytes 393220
  22.8 6.7 %copy-start.1 = (bf16[128,256]{1,0:T(8,128)(2,1)S(1)}, bf16[128,256]{1,0:T(8,128)(2,1)}, u32[]{:S(2)}) copy-start(bf16[128,256]{1,0:T(8,128)(2,1)} %weight_ref.1) | copy-start | bytes 196612
  24.5 5.0 %collective-permute-start.7 = (bf16[512,128]{1,0:T(8,128)(2,1)S(1)}, bf16[512,128]{1,0:T(8,128)(2,1)S(1)}, u32[]{:S(2)}, u32[]{:S(2)}) collective-permute-start(bf16[512,128]{1,0:T(8,128)(2,1)S(1)} %aggregate.3.own_ref), channel_id=1, source_target_pairs={{0,1},{1,0},{2,3},{3,2},{4,5},{5,4},{6,7},{7,6},{8,9},{9,8},{10,11... | collective-permute-start | bytes 393224 | tf_op jit(solution)/shard_map/ppermute | solution.py:357
  30.9 6.1 %collective-permute-start.9 = (bf16[128,1152]{1,0:T(8,128)(2,1)S(1)}, bf16[128,1152]{1,0:T(8,128)(2,1)S(1)}, u32[]{:S(2)}, u32[]{:S(2)}) collective-permute-start(bf16[128,1152]{1,0:T(8,128)(2,1)S(1)} %get-tuple-element.20.own_ref), channel_id=1, source_target_pairs={{0,3},{1,5},{2,6},{3,0},{4,7},{5,1},{6,2},{7,4},{8,11},{9,13},{10,... | collective-permute-start | bytes 884744 | tf_op jit(solution)/shard_map/ppermute | solution.py:357
  31.5 8.4 %collective-permute-start.13 = (bf16[128,1024]{1,0:T(8,128)(2,1)S(1)}, bf16[128,1024]{1,0:T(8,128)(2,1)S(1)}, u32[]{:S(2)}, u32[]{:S(2)}) collective-permute-start(bf16[128,1024]{1,0:T(8,128)(2,1)S(1)} %get-tuple-element.27.own_ref), channel_id=1, source_target_pairs={{0,3},{1,5},{2,6},{3,0},{4,7},{5,1},{6,2},{7,4},{8,11},{9,13},{10,... | collective-permute-start | bytes 786440 | tf_op jit(solution)/shard_map/ppermute | solution.py:357
  37.1 5.4 %collective-permute-start.10 = (bf16[128,640]{1,0:T(8,128)(2,1)S(1)}, bf16[128,640]{1,0:T(8,128)(2,1)S(1)}, u32[]{:S(2)}, u32[]{:S(2)}) collective-permute-start(bf16[128,640]{1,0:T(8,128)(2,1)S(1)} %get-tuple-element.23.own_ref), channel_id=1, source_target_pairs={{0,4},{1,2},{2,1},{3,7},{4,0},{5,6},{6,5},{7,3},{8,12},{9,10},{10,... | collective-permute-start | bytes 491528 | tf_op jit(solution)/shard_map/ppermute | solution.py:357
  39.9 5.1 %collective-permute-start.14 = (bf16[128,512]{1,0:T(8,128)(2,1)S(1)}, bf16[128,512]{1,0:T(8,128)(2,1)S(1)}, u32[]{:S(2)}, u32[]{:S(2)}) collective-permute-start(bf16[128,512]{1,0:T(8,128)(2,1)S(1)} %get-tuple-element.28), channel_id=1, source_target_pairs={{0,4},{1,2},{2,1},{3,7},{4,0},{5,6},{6,5},{7,3},{8,12},{9,10},{10,... | collective-permute-start | bytes 393224 | tf_op jit(solution)/shard_map/ppermute | solution.py:357
  42.5 6.6 %collective-permute-start.11 = (bf16[128,384]{1,0:T(8,128)(2,1)S(1)}, bf16[128,384]{1,0:T(8,128)(2,1)S(1)}, u32[]{:S(2)}, u32[]{:S(2)}) collective-permute-start(bf16[128,384]{1,0:T(8,128)(2,1)S(1)} %get-tuple-element.25), channel_id=1, source_target_pairs={{0,24},{1,25},{2,26},{3,27},{4,28},{5,29},{6,30},{7,31},{8,16},{9,... | collective-permute-start | bytes 294920 | tf_op jit(solution)/shard_map/ppermute | solution.py:357
  45.0 9.4 %collective-permute-start.12 = (bf16[128,384]{1,0:T(8,128)(2,1)S(1)}, bf16[128,384]{1,0:T(8,128)(2,1)S(1)}, u32[]{:S(2)}, u32[]{:S(2)}) collective-permute-start(bf16[128,384]{1,0:T(8,128)(2,1)S(1)} %get-tuple-element.26), channel_id=1, source_target_pairs={{0,16},{1,17},{2,18},{3,19},{4,20},{5,21},{6,22},{7,23},{8,24},{9,... | collective-permute-start | bytes 294920 | tf_op jit(solution)/shard_map/ppermute | solution.py:357
  45.1 9.4 %collective-permute-start.15 = (bf16[128,384]{1,0:T(8,128)(2,1)S(1)}, bf16[128,384]{1,0:T(8,128)(2,1)S(1)}, u32[]{:S(2)}, u32[]{:S(2)}) collective-permute-start(bf16[128,384]{1,0:T(8,128)(2,1)S(1)} %get-tuple-element.31.sent_one_ref), channel_id=1, source_target_pairs={{0,8},{1,9},{2,10},{3,11},{4,12},{5,13},{6,14},{7,15},{8,0},{9,1},... | collective-permute-start | bytes 294920 | tf_op jit(solution)/shard_map/ppermute | solution.py:357
  54.5 1.4 %collective-permute-start.16 = (bf16[128,384]{1,0:T(8,128)(2,1)S(1)}, bf16[128,384]{1,0:T(8,128)(2,1)S(1)}, u32[]{:S(2)}, u32[]{:S(2)}) collective-permute-start(bf16[128,384]{1,0:T(8,128)(2,1)S(1)} %line_sum.1.own_ref), channel_id=1, source_target_pairs={{0,2},{1,3},{2,0},{3,1},{4,6},{5,7},{6,4},{7,5},{8,10},{9,11},{10,... | collective-permute-start | bytes 294920 | tf_op jit(solution)/shard_map/ppermute | solution.py:357

commit v4 on v3

--- a/solution.py
+++ b/solution.py
@@ -380,12 +380,12 @@
     whole, whole_beside = [send(features, lay.owner_to_class(at)) for at in range(2)]
     far_cot = send(cotangent, lay.plain(0, 1))
     three = send(two, lay.in_class(near))
-    mine = jnp.concatenate([one, two], 0)
+    mine = jnp.concatenate([two, one], 0)
     beside = send(mine, lay.in_class(1))
     beside_three = send(three, lay.in_class(1))
     dense = dense_blocks(tiles, table, near, halves, blocks)
-    spans = [(0, 0, 0, 0, share), (1, 2, 0, 0, share), (2, 0, share, 0, share), (2, 0, 2 * share, rows, share),
-             (3, 2, share, 0, share), (3, 2, 2 * share, rows, share), (4, 0, 3 * share, 0, share)]
+    spans = [(0, 0, 0, 0, share), (1, 2, 0, 0, share), (2, 0, 2 * share, 0, share), (2, 0, share, rows, share),
+             (3, 2, 2 * share, 0, share), (3, 2, share, rows, share), (4, 0, 3 * share, 0, share)]
     partial = aggregate(dense, spans, [whole, whole_beside, mine, beside, three], None, jnp.float32)
     partial = aggregate(dense, [(0, 2, 3 * share, 0, share)], [beside_three], partial, jnp.bfloat16)
     other = send(partial, lay.plain(0, 1))

time: 56.8 us -> 56.5 us (level)
  waiting for transfers between devices: 23.8 us -> 22 us
  starting transfers between devices: 23.9 us -> 25.4 us
    ppermute x17, waiting for transfers between devices: 23.8 us -> 22 us  [send(): return lax.ppermute(value, AXES, route)]
    ppermute x17, starting transfers between devices: 23.9 us -> 25.4 us  [send(): return lax.ppermute(value, AXES, route)]
  transfers between devices with their start and end apart: 17 -> 17, of which waited for: 10 -> 11; matrix products, arithmetic and copies ran while one was open for 2% -> 2% of each run, Pallas kernels for 9% -> 9%
where the time goes in v4:
time: 56.5 us; the launch traced here: 56.3 us
  starting transfers between devices  25.4 us (45%)
  waiting for transfers between devices  22 us (39%)
  Pallas kernels  7.27 us (13%)
  other arithmetic  0.86 us (2%)
  between operations  0.75 us (1%)
    ppermute x17, starting transfers between devices, send(): return lax.ppermute(value, AXES, route)  25.4 us
    ppermute x17, waiting for transfers between devices, send(): return lax.ppermute(value, AXES, route)  22 us
    pallas_call x1, Pallas kernels, dense_blocks(): pl.pallas_call(functools.partial(dense_kernel, blocks, near, halves), in_...  2.98 us
    pallas_call x2, Pallas kernels, aggregate(): pl.pallas_call(functools.partial(aggregate_kernel, spans, len(given) - le...  1.42 us
    pallas_call x1, Pallas kernels, turn(): pl.pallas_call(functools.partial(turn_kernel, share, chunk), in_specs=in_...  1.35 us
  transfers between devices with their start and end apart: 17, of which 11 were waited for; matrix products, arithmetic and copies ran while one was open for 2% of the time, Pallas kernels for 9%

profile of v4, /device:TPU:0, one launch (start us, length us, event | category | flops | bytes accessed | tf_op | source)
XLA Modules:
  0.0 56.3 jit_solution(14892753066173995399)
XLA Ops:
  0.6 4.1 %collective-permute-start.2 = (bf16[512,128]{1,0:T(8,128)(2,1)}, bf16[512,128]{1,0:T(8,128)(2,1)S(1)}, u32[]{:S(2)}, u32[]{:S(2)}) collective-permute-start(bf16[512,128]{1,0:T(8,128)(2,1)} %param.6), channel_id=1, source_target_pairs={{0,16},{1,19},{2,18},{3,17},{4,20},{5,23},{6,22},{7,21},{8,24},{9,... | collective-permute-start | bytes 393224 | tf_op jit(solution)/shard_map/ppermute | solution.py:357
  4.7 1.6 %collective-permute-start.3 = (bf16[512,128]{1,0:T(8,128)(2,1)}, bf16[512,128]{1,0:T(8,128)(2,1)S(1)}, u32[]{:S(2)}, u32[]{:S(2)}) collective-permute-start(bf16[512,128]{1,0:T(8,128)(2,1)} %param.6), channel_id=1, source_target_pairs={{0,8},{1,11},{2,10},{3,9},{4,12},{5,15},{6,14},{7,13},{8,0},{9,3},... | collective-permute-start | bytes 393224 | tf_op jit(solution)/shard_map/ppermute | solution.py:357
  6.3 1.5 %collective-permute-start.1 = (bf16[512,128]{1,0:T(8,128)(2,1)}, bf16[512,128]{1,0:T(8,128)(2,1)S(1)}, u32[]{:S(2)}, u32[]{:S(2)}) collective-permute-start(bf16[512,128]{1,0:T(8,128)(2,1)} %param.6), channel_id=1, source_target_pairs={{0,4},{1,7},{2,6},{3,5},{4,0},{5,3},{6,2},{7,1},{8,12},{9,15},{10,... | collective-permute-start | bytes 393224 | tf_op jit(solution)/shard_map/ppermute | solution.py:357
  7.8 1.6 %collective-permute-start = (bf16[512,128]{1,0:T(8,128)(2,1)}, bf16[512,128]{1,0:T(8,128)(2,1)S(1)}, u32[]{:S(2)}, u32[]{:S(2)}) collective-permute-start(bf16[512,128]{1,0:T(8,128)(2,1)} %param.6), channel_id=1, source_target_pairs={{0,0},{1,3},{2,2},{3,1},{4,4},{5,7},{6,6},{7,5},{8,8},{9,11},{10,1... | collective-permute-start | bytes 393224 | tf_op jit(solution)/shard_map/ppermute | solution.py:357
  9.4 1.7 %collective-permute-start.8 = (bf16[256,256]{1,0:T(8,128)(2,1)}, bf16[256,256]{1,0:T(8,128)(2,1)S(1)}, u32[]{:S(2)}, u32[]{:S(2)}) collective-permute-start(bf16[256,256]{1,0:T(8,128)(2,1)} %cot_ref.1), channel_id=1, source_target_pairs={{0,1},{1,0},{2,3},{3,2},{4,5},{5,4},{6,7},{7,6},{8,9},{9,8},{10,11... | collective-permute-start | bytes 393224 | tf_op jit(solution)/shard_map/ppermute | solution.py:357
  11.1 0.2 collective-permute-done.2
  11.4 0.2 collective-permute-done.3
  11.6 1.6 %collective-permute-start.4 = (bf16[1024,128]{1,0:T(8,128)(2,1)S(1)}, bf16[1024,128]{1,0:T(8,128)(2,1)S(1)}, u32[]{:S(2)}, u32[]{:S(2)}) collective-permute-start(bf16[1024,128]{1,0:T(8,128)(2,1)S(1)} %constant_dynamic-update-slice_fusion.refs_2_), channel_id=1, source_target_pairs={{0,4},{1,5},{2,6},{3,7},{4,0},{5,1},{6,2},{7,3},{8,12},{9,13},{10,... | collective-permute-start | bytes 786440 | tf_op jit(solution)/shard_map/ppermute | solution.py:357
  13.2 1.4 %collective-permute-start.5 = (bf16[512,128]{1,0:T(8,128)(2,1)S(1)}, bf16[512,128]{1,0:T(8,128)(2,1)S(1)}, u32[]{:S(2)}, u32[]{:S(2)}) collective-permute-start(bf16[512,128]{1,0:T(8,128)(2,1)S(1)} %collective-permute-done.2), channel_id=1, source_target_pairs={{0,8},{1,9},{2,10},{3,11},{4,12},{5,13},{6,14},{7,15},{8,0},{9,1},... | collective-permute-start | bytes 393224 | tf_op jit(solution)/shard_map/ppermute | solution.py:357
  14.6 0.8 %bitcast_select_fusion = s32[8,12]{1,0:T(8,128)S(1)} fusion(s32[1,1,8,12]{3,2,1,0:T(8,128)} %param.9, s32[]{:T(128)S(6)} %mul.14, s32[8]{0:T(128)} %bitcast.5), kind=kLoop, calls=%fused_computation.13 | loop fusion | flops 288 | bytes 804 | tf_op jit(solution)/shard_map/jit(_where)/select_n | solution.py:367
  15.4 2.8 %collective-permute-done.5.refs_4_ = bf16[512,128]{1,0:T(8,128)(2,1)S(1)} collective-permute-done((bf16[512,128]{1,0:T(8,128)(2,1)S(1)}, bf16[512,128]{1,0:T(8,128)(2,1)S(1)}, u32[]{:S(2)}, u32[]{:S(2)}) %collective-permute-start.5) | collective-permute-done | bytes 131104 | tf_op jit(solution)/shard_map/ppermute | solution.py:357
  18.2 0.5 collective-permute-start.6
  18.7 0.1 pad_add_fusion.table
  18.7 3.0 %dense_blocks.1.dense_ref = bf16[4,512,1024]{2,1,0:T(8,128)(2,1)S(1)} custom-call(s32[8,13]{1,0:T(8,128)S(1)} %pad_add_fusion.table, bf16[8,12,128,128]{3,2,1,0:T(8,128)(2,1)} %bitcast.4), custom_call_target="tpu_custom_call" | custom-call | tf_op jit(solution)/shard_map/dense_blocks/pallas_call | solution.py:82
  21.7 0.0 copy-start
  21.7 0.0 copy-start.1
  21.7 0.0 collective-permute-done.1.refs_1_
  21.8 0.0 collective-permute-done.refs_0_
  21.8 0.0 collective-permute-done.4.refs_3_
  21.8 1.1 %aggregate.2.refs_0_ = f32[512,128]{1,0:T(8,128)S(1)} custom-call(bf16[4,512,1024]{2,1,0:T(8,128)(2,1)S(1)} %dense_blocks.1.dense_ref, bf16[512,128]{1,0:T(8,128)(2,1)S(1)} %collective-permute-done.refs_0_, bf16[512,128]{1,0:T(8,128)(2,1)S(1)} %collective-permute-done.1.refs_1_, bf16[1024,128]{1,0:T(8,128)(2,1)S(1)} %constant_dynamic-update-slice_fusion.refs_2_, ...), custom_call_target="tpu_custom_call" | custom-call | tf_op jit(solution)/shard_map/aggregate/pallas_call | solution.py:118
  22.9 0.2 collective-permute-done.6.refs_1_
  23.1 0.3 aggregate.3.own_ref
  23.5 2.2 %collective-permute-start.7 = (bf16[512,128]{1,0:T(8,128)(2,1)S(1)}, bf16[512,128]{1,0:T(8,128)(2,1)S(1)}, u32[]{:S(2)}, u32[]{:S(2)}) collective-permute-start(bf16[512,128]{1,0:T(8,128)(2,1)S(1)} %aggregate.3.own_ref), channel_id=1, source_target_pairs={{0,1},{1,0},{2,3},{3,2},{4,5},{5,4},{6,7},{7,6},{8,9},{9,8},{10,11... | collective-permute-start | bytes 393224 | tf_op jit(solution)/shard_map/ppermute | solution.py:357
  25.7 0.0 collective-permute-done.8.far_cot_ref
  25.7 2.9 %collective-permute-done.7.other_ref = bf16[512,128]{1,0:T(8,128)(2,1)S(1)} collective-permute-done((bf16[512,128]{1,0:T(8,128)(2,1)S(1)}, bf16[512,128]{1,0:T(8,128)(2,1)S(1)}, u32[]{:S(2)}, u32[]{:S(2)}) %collective-permute-start.7) | collective-permute-done | bytes 131104 | tf_op jit(solution)/shard_map/ppermute | solution.py:357
  28.6 0.0 copy-done
  28.6 0.0 copy-done.1
  28.7 1.3 %turn.1 = (bf16[256,256]{1,0:T(8,128)(2,1)}, bf16[128,512]{1,0:T(8,128)(2,1)S(1)}, bf16[128,1152]{1,0:T(8,128)(2,1)S(1)}) custom-call(bf16[512,128]{1,0:T(8,128)(2,1)S(1)} %aggregate.3.own_ref, bf16[512,128]{1,0:T(8,128)(2,1)S(1)} %collective-permute-done.7.other_ref, bf16[128,256]{1,0:T(8,128)(2,1)S(1)} %copy-done.1, bf16[256,256]{1,0:T(8,128)(2,1)S(1)} %copy-done, ...), custom_call_target="tpu_custom_call" | custom-call | tf_op jit(solution)/shard_map/turn/pallas_call | solution.py:157
  30.0 0.0 collective-permute-start.9
  30.0 0.6 %rest_terms.1 = (bf16[128,1024]{1,0:T(8,128)(2,1)S(1)}, f32[2,128,1024]{2,1,0:T(8,128)S(1)}) custom-call(bf16[128,512]{1,0:T(8,128)(2,1)S(1)} %get-tuple-element.21.back_ref, bf16[4,512,1024]{2,1,0:T(8,128)(2,1)S(1)} %dense_blocks.1.dense_ref), custom_call_target="tpu_custom_call" | custom-call | tf_op jit(solution)/shard_map/rest_terms/pallas_call | solution.py:184
  30.6 1.8 %collective-permute-start.13 = (bf16[128,1024]{1,0:T(8,128)(2,1)S(1)}, bf16[128,1024]{1,0:T(8,128)(2,1)S(1)}, u32[]{:S(2)}, u32[]{:S(2)}) collective-permute-start(bf16[128,1024]{1,0:T(8,128)(2,1)S(1)} %get-tuple-element.27.own_ref), channel_id=1, source_target_pairs={{0,3},{1,5},{2,6},{3,0},{4,7},{5,1},{6,2},{7,4},{8,11},{9,13},{10,... | collective-permute-start | bytes 786440 | tf_op jit(solution)/shard_map/ppermute | solution.py:357
  32.4 3.7 %collective-permute-done.9.got_ref = bf16[128,1152]{1,0:T(8,128)(2,1)S(1)} collective-permute-done((bf16[128,1152]{1,0:T(8,128)(2,1)S(1)}, bf16[128,1152]{1,0:T(8,128)(2,1)S(1)}, u32[]{:S(2)}, u32[]{:S(2)}) %collective-permute-start.9) | collective-permute-done | bytes 294944 | tf_op jit(solution)/shard_map/ppermute | solution.py:357
  36.1 0.1 first_sum.2
  36.2 1.0 %collective-permute-start.10 = (bf16[128,640]{1,0:T(8,128)(2,1)S(1)}, bf16[128,640]{1,0:T(8,128)(2,1)S(1)}, u32[]{:S(2)}, u32[]{:S(2)}) collective-permute-start(bf16[128,640]{1,0:T(8,128)(2,1)S(1)} %get-tuple-element.23.own_ref), channel_id=1, source_target_pairs={{0,4},{1,2},{2,1},{3,7},{4,0},{5,6},{6,5},{7,3},{8,12},{9,10},{10,... | collective-permute-start | bytes 491528 | tf_op jit(solution)/shard_map/ppermute | solution.py:357
  37.2 1.7 %collective-permute-done.13.got_ref = bf16[128,1024]{1,0:T(8,128)(2,1)S(1)} collective-permute-done((bf16[128,1024]{1,0:T(8,128)(2,1)S(1)}, bf16[128,1024]{1,0:T(8,128)(2,1)S(1)}, u32[]{:S(2)}, u32[]{:S(2)}) %collective-permute-start.13) | collective-permute-done | bytes 262176 | tf_op jit(solution)/shard_map/ppermute | solution.py:357
  39.0 1.0 %collective-permute-start.14 = (bf16[128,512]{1,0:T(8,128)(2,1)S(1)}, bf16[128,512]{1,0:T(8,128)(2,1)S(1)}, u32[]{:S(2)}, u32[]{:S(2)}) collective-permute-start(bf16[128,512]{1,0:T(8,128)(2,1)S(1)} %get-tuple-element.28), channel_id=1, source_target_pairs={{0,4},{1,2},{2,1},{3,7},{4,0},{5,6},{6,5},{7,3},{8,12},{9,10},{10,... | collective-permute-start | bytes 393224 | tf_op jit(solution)/shard_map/ppermute | solution.py:357
  40.0 1.5 %collective-permute-done.10.got_ref = bf16[128,640]{1,0:T(8,128)(2,1)S(1)} collective-permute-done((bf16[128,640]{1,0:T(8,128)(2,1)S(1)}, bf16[128,640]{1,0:T(8,128)(2,1)S(1)}, u32[]{:S(2)}, u32[]{:S(2)}) %collective-permute-start.10) | collective-permute-done | bytes 163872 | tf_op jit(solution)/shard_map/ppermute | solution.py:357
  41.6 3.4 %collective-permute-start.11 = (bf16[128,384]{1,0:T(8,128)(2,1)S(1)}, bf16[128,384]{1,0:T(8,128)(2,1)S(1)}, u32[]{:S(2)}, u32[]{:S(2)}) collective-permute-start(bf16[128,384]{1,0:T(8,128)(2,1)S(1)} %get-tuple-element.25), channel_id=1, source_target_pairs={{0,24},{1,25},{2,26},{3,27},{4,28},{5,29},{6,30},{7,31},{8,16},{9,... | collective-permute-start | bytes 294920 | tf_op jit(solution)/shard_map/ppermute | solution.py:357
  45.0 0.0 collective-permute-start.12
  45.0 0.0 collective-permute-done.14.got_ref
  45.1 1.1 %collective-permute-start.15 = (bf16[128,384]{1,0:T(8,128)(2,1)S(1)}, bf16[128,384]{1,0:T(8,128)(2,1)S(1)}, u32[]{:S(2)}, u32[]{:S(2)}) collective-permute-start(bf16[128,384]{1,0:T(8,128)(2,1)S(1)} %get-tuple-element.31.sent_one_ref), channel_id=1, source_target_pairs={{0,8},{1,9},{2,10},{3,11},{4,12},{5,13},{6,14},{7,15},{8,0},{9,1},... | collective-permute-start | bytes 294920 | tf_op jit(solution)/shard_map/ppermute | solution.py:357
  46.2 2.0 %collective-permute-done.11.three_ref = bf16[128,384]{1,0:T(8,128)(2,1)S(1)} collective-permute-done((bf16[128,384]{1,0:T(8,128)(2,1)S(1)}, bf16[128,384]{1,0:T(8,128)(2,1)S(1)}, u32[]{:S(2)}, u32[]{:S(2)}) %collective-permute-start.11) | collective-permute-done | bytes 98336 | tf_op jit(solution)/shard_map/ppermute | solution.py:357
  48.2 5.6 %collective-permute-done.12.two_ref = bf16[128,384]{1,0:T(8,128)(2,1)S(1)} collective-permute-done((bf16[128,384]{1,0:T(8,128)(2,1)S(1)}, bf16[128,384]{1,0:T(8,128)(2,1)S(1)}, u32[]{:S(2)}, u32[]{:S(2)}) %collective-permute-start.12) | collective-permute-done | bytes 98336 | tf_op jit(solution)/shard_map/ppermute | solution.py:357
  53.8 0.0 collective-permute-done.15.one_ref
  53.8 0.8 %collective-permute-start.16 = (bf16[128,384]{1,0:T(8,128)(2,1)S(1)}, bf16[128,384]{1,0:T(8,128)(2,1)S(1)}, u32[]{:S(2)}, u32[]{:S(2)}) collective-permute-start(bf16[128,384]{1,0:T(8,128)(2,1)S(1)} %line_sum.1.own_ref), channel_id=1, source_target_pairs={{0,2},{1,3},{2,0},{3,1},{4,6},{5,7},{6,4},{7,5},{8,10},{9,11},{10,... | collective-permute-start | bytes 294920 | tf_op jit(solution)/shard_map/ppermute | solution.py:357
  54.6 0.9 %collective-permute-done.16.got_ref = bf16[128,384]{1,0:T(8,128)(2,1)S(1)} collective-permute-done((bf16[128,384]{1,0:T(8,128)(2,1)S(1)}, bf16[128,384]{1,0:T(8,128)(2,1)S(1)}, u32[]{:S(2)}, u32[]{:S(2)}) %collective-permute-start.16) | collective-permute-done | bytes 98336 | tf_op jit(solution)/shard_map/ppermute | solution.py:357
  55.6 0.7 %finish.1 = (bf16[256,128]{1,0:T(8,128)(2,1)}, f32[128,256]{1,0:T(8,128)}) custom-call(bf16[128,384]{1,0:T(8,128)(2,1)S(1)} %line_sum.1.own_ref, bf16[128,384]{1,0:T(8,128)(2,1)S(1)} %collective-permute-done.16.got_ref), custom_call_target="tpu_custom_call" | custom-call | tf_op jit(solution)/shard_map/finish/pallas_call | solution.py:305
  (7 shorter events, 0.2 us)
Async XLA Ops:
  0.6 10.7 %collective-permute-start.2 = (bf16[512,128]{1,0:T(8,128)(2,1)}, bf16[512,128]{1,0:T(8,128)(2,1)S(1)}, u32[]{:S(2)}, u32[]{:S(2)}) collective-permute-start(bf16[512,128]{1,0:T(8,128)(2,1)} %param.6), channel_id=1, source_target_pairs={{0,16},{1,19},{2,18},{3,17},{4,20},{5,23},{6,22},{7,21},{8,24},{9,... | collective-permute-start | bytes 393224 | tf_op jit(solution)/shard_map/ppermute | solution.py:357
  4.7 6.8 %collective-permute-start.3 = (bf16[512,128]{1,0:T(8,128)(2,1)}, bf16[512,128]{1,0:T(8,128)(2,1)S(1)}, u32[]{:S(2)}, u32[]{:S(2)}) collective-permute-start(bf16[512,128]{1,0:T(8,128)(2,1)} %param.6), channel_id=1, source_target_pairs={{0,8},{1,11},{2,10},{3,9},{4,12},{5,15},{6,14},{7,13},{8,0},{9,3},... | collective-permute-start | bytes 393224 | tf_op jit(solution)/shard_map/ppermute | solution.py:357
  6.3 15.4 %collective-permute-start.1 = (bf16[512,128]{1,0:T(8,128)(2,1)}, bf16[512,128]{1,0:T(8,128)(2,1)S(1)}, u32[]{:S(2)}, u32[]{:S(2)}) collective-permute-start(bf16[512,128]{1,0:T(8,128)(2,1)} %param.6), channel_id=1, source_target_pairs={{0,4},{1,7},{2,6},{3,5},{4,0},{5,3},{6,2},{7,1},{8,12},{9,15},{10,... | collective-permute-start | bytes 393224 | tf_op jit(solution)/shard_map/ppermute | solution.py:357
  7.8 13.9 %collective-permute-start = (bf16[512,128]{1,0:T(8,128)(2,1)}, bf16[512,128]{1,0:T(8,128)(2,1)S(1)}, u32[]{:S(2)}, u32[]{:S(2)}) collective-permute-start(bf16[512,128]{1,0:T(8,128)(2,1)} %param.6), channel_id=1, source_target_pairs={{0,0},{1,3},{2,2},{3,1},{4,4},{5,7},{6,6},{7,5},{8,8},{9,11},{10,1... | collective-permute-start | bytes 393224 | tf_op jit(solution)/shard_map/ppermute | solution.py:357
  9.4 16.3 %collective-permute-start.8 = (bf16[256,256]{1,0:T(8,128)(2,1)}, bf16[256,256]{1,0:T(8,128)(2,1)S(1)}, u32[]{:S(2)}, u32[]{:S(2)}) collective-permute-start(bf16[256,256]{1,0:T(8,128)(2,1)} %cot_ref.1), channel_id=1, source_target_pairs={{0,1},{1,0},{2,3},{3,2},{4,5},{5,4},{6,7},{7,6},{8,9},{9,8},{10,11... | collective-permute-start | bytes 393224 | tf_op jit(solution)/shard_map/ppermute | solution.py:357
  11.6 10.2 %collective-permute-start.4 = (bf16[1024,128]{1,0:T(8,128)(2,1)S(1)}, bf16[1024,128]{1,0:T(8,128)(2,1)S(1)}, u32[]{:S(2)}, u32[]{:S(2)}) collective-permute-start(bf16[1024,128]{1,0:T(8,128)(2,1)S(1)} %constant_dynamic-update-slice_fusion.refs_2_), channel_id=1, source_target_pairs={{0,4},{1,5},{2,6},{3,7},{4,0},{5,1},{6,2},{7,3},{8,12},{9,13},{10,... | collective-permute-start | bytes 786440 | tf_op jit(solution)/shard_map/ppermute | solution.py:357
  13.2 5.0 %collective-permute-start.5 = (bf16[512,128]{1,0:T(8,128)(2,1)S(1)}, bf16[512,128]{1,0:T(8,128)(2,1)S(1)}, u32[]{:S(2)}, u32[]{:S(2)}) collective-permute-start(bf16[512,128]{1,0:T(8,128)(2,1)S(1)} %collective-permute-done.2), channel_id=1, source_target_pairs={{0,8},{1,9},{2,10},{3,11},{4,12},{5,13},{6,14},{7,15},{8,0},{9,1},... | collective-permute-start | bytes 393224 | tf_op jit(solution)/shard_map/ppermute | solution.py:357
  18.2 5.0 %collective-permute-start.6 = (bf16[512,128]{1,0:T(8,128)(2,1)S(1)}, bf16[512,128]{1,0:T(8,128)(2,1)S(1)}, u32[]{:S(2)}, u32[]{:S(2)}) collective-permute-start(bf16[512,128]{1,0:T(8,128)(2,1)S(1)} %collective-permute-done.5.refs_4_), channel_id=1, source_target_pairs={{0,4},{1,5},{2,6},{3,7},{4,0},{5,1},{6,2},{7,3},{8,12},{9,13},{10,... | collective-permute-start | bytes 393224 | tf_op jit(solution)/shard_map/ppermute | solution.py:357
  21.7 6.9 %copy-start = (bf16[256,256]{1,0:T(8,128)(2,1)S(1)}, bf16[256,256]{1,0:T(8,128)(2,1)}, u32[]{:S(2)}) copy-start(bf16[256,256]{1,0:T(8,128)(2,1)} %cot_ref.1) | copy-start | bytes 393220
  21.7 6.9 %copy-start.1 = (bf16[128,256]{1,0:T(8,128)(2,1)S(1)}, bf16[128,256]{1,0:T(8,128)(2,1)}, u32[]{:S(2)}) copy-start(bf16[128,256]{1,0:T(8,128)(2,1)} %weight_ref.1) | copy-start | bytes 196612
  23.5 5.2 %collective-permute-start.7 = (bf16[512,128]{1,0:T(8,128)(2,1)S(1)}, bf16[512,128]{1,0:T(8,128)(2,1)S(1)}, u32[]{:S(2)}, u32[]{:S(2)}) collective-permute-start(bf16[512,128]{1,0:T(8,128)(2,1)S(1)} %aggregate.3.own_ref), channel_id=1, source_target_pairs={{0,1},{1,0},{2,3},{3,2},{4,5},{5,4},{6,7},{7,6},{8,9},{9,8},{10,11... | collective-permute-start | bytes 393224 | tf_op jit(solution)/shard_map/ppermute | solution.py:357
  30.0 6.1 %collective-permute-start.9 = (bf16[128,1152]{1,0:T(8,128)(2,1)S(1)}, bf16[128,1152]{1,0:T(8,128)(2,1)S(1)}, u32[]{:S(2)}, u32[]{:S(2)}) collective-permute-start(bf16[128,1152]{1,0:T(8,128)(2,1)S(1)} %get-tuple-element.20.own_ref), channel_id=1, source_target_pairs={{0,3},{1,5},{2,6},{3,0},{4,7},{5,1},{6,2},{7,4},{8,11},{9,13},{10,... | collective-permute-start | bytes 884744 | tf_op jit(solution)/shard_map/ppermute | solution.py:357
  30.6 8.4 %collective-permute-start.13 = (bf16[128,1024]{1,0:T(8,128)(2,1)S(1)}, bf16[128,1024]{1,0:T(8,128)(2,1)S(1)}, u32[]{:S(2)}, u32[]{:S(2)}) collective-permute-start(bf16[128,1024]{1,0:T(8,128)(2,1)S(1)} %get-tuple-element.27.own_ref), channel_id=1, source_target_pairs={{0,3},{1,5},{2,6},{3,0},{4,7},{5,1},{6,2},{7,4},{8,11},{9,13},{10,... | collective-permute-start | bytes 786440 | tf_op jit(solution)/shard_map/ppermute | solution.py:357
  36.2 5.4 %collective-permute-start.10 = (bf16[128,640]{1,0:T(8,128)(2,1)S(1)}, bf16[128,640]{1,0:T(8,128)(2,1)S(1)}, u32[]{:S(2)}, u32[]{:S(2)}) collective-permute-start(bf16[128,640]{1,0:T(8,128)(2,1)S(1)} %get-tuple-element.23.own_ref), channel_id=1, source_target_pairs={{0,4},{1,2},{2,1},{3,7},{4,0},{5,6},{6,5},{7,3},{8,12},{9,10},{10,... | collective-permute-start | bytes 491528 | tf_op jit(solution)/shard_map/ppermute | solution.py:357
  39.0 6.0 %collective-permute-start.14 = (bf16[128,512]{1,0:T(8,128)(2,1)S(1)}, bf16[128,512]{1,0:T(8,128)(2,1)S(1)}, u32[]{:S(2)}, u32[]{:S(2)}) collective-permute-start(bf16[128,512]{1,0:T(8,128)(2,1)S(1)} %get-tuple-element.28), channel_id=1, source_target_pairs={{0,4},{1,2},{2,1},{3,7},{4,0},{5,6},{6,5},{7,3},{8,12},{9,10},{10,... | collective-permute-start | bytes 393224 | tf_op jit(solution)/shard_map/ppermute | solution.py:357
  41.6 6.6 %collective-permute-start.11 = (bf16[128,384]{1,0:T(8,128)(2,1)S(1)}, bf16[128,384]{1,0:T(8,128)(2,1)S(1)}, u32[]{:S(2)}, u32[]{:S(2)}) collective-permute-start(bf16[128,384]{1,0:T(8,128)(2,1)S(1)} %get-tuple-element.25), channel_id=1, source_target_pairs={{0,24},{1,25},{2,26},{3,27},{4,28},{5,29},{6,30},{7,31},{8,16},{9,... | collective-permute-start | bytes 294920 | tf_op jit(solution)/shard_map/ppermute | solution.py:357
  45.0 8.7 %collective-permute-start.12 = (bf16[128,384]{1,0:T(8,128)(2,1)S(1)}, bf16[128,384]{1,0:T(8,128)(2,1)S(1)}, u32[]{:S(2)}, u32[]{:S(2)}) collective-permute-start(bf16[128,384]{1,0:T(8,128)(2,1)S(1)} %get-tuple-element.26), channel_id=1, source_target_pairs={{0,16},{1,17},{2,18},{3,19},{4,20},{5,21},{6,22},{7,23},{8,24},{9,... | collective-permute-start | bytes 294920 | tf_op jit(solution)/shard_map/ppermute | solution.py:357
  45.1 8.7 %collective-permute-start.15 = (bf16[128,384]{1,0:T(8,128)(2,1)S(1)}, bf16[128,384]{1,0:T(8,128)(2,1)S(1)}, u32[]{:S(2)}, u32[]{:S(2)}) collective-permute-start(bf16[128,384]{1,0:T(8,128)(2,1)S(1)} %get-tuple-element.31.sent_one_ref), channel_id=1, source_target_pairs={{0,8},{1,9},{2,10},{3,11},{4,12},{5,13},{6,14},{7,15},{8,0},{9,1},... | collective-permute-start | bytes 294920 | tf_op jit(solution)/shard_map/ppermute | solution.py:357
  53.8 1.7 %collective-permute-start.16 = (bf16[128,384]{1,0:T(8,128)(2,1)S(1)}, bf16[128,384]{1,0:T(8,128)(2,1)S(1)}, u32[]{:S(2)}, u32[]{:S(2)}) collective-permute-start(bf16[128,384]{1,0:T(8,128)(2,1)S(1)} %line_sum.1.own_ref), channel_id=1, source_target_pairs={{0,2},{1,3},{2,0},{3,1},{4,6},{5,7},{6,4},{7,5},{8,10},{9,11},{10,... | collective-permute-start | bytes 294920 | tf_op jit(solution)/shard_map/ppermute | solution.py:357

commit v5 on v4

--- a/solution.py
+++ b/solution.py
@@ -159,7 +159,7 @@
         in_specs=in_vmem(6),
         out_specs=in_vmem(3),
         out_shape=[
-            jax.ShapeDtypeStruct((share, hid), bf),
+            pltpu.VMEM((share, hid), bf),
             jax.ShapeDtypeStruct((width, rows), bf),
             jax.ShapeDtypeStruct((width, 2 * chunk[1] + hid // 2), bf),
         ],

time: 56.5 us -> 56.1 us (level)
  waiting for transfers between devices: 22 us -> 21.3 us
  local copies, waits for them, and re-layouts: 0.04 us -> 0.69 us
    ppermute x17, waiting for transfers between devices: 22 us -> 21.3 us  [send(): return lax.ppermute(value, AXES, route)]
    unnamed x5 -> x6, local copies, waits for them, and re-layouts: 0.02 us -> 0.68 us
  transfers between devices with their start and end apart: 17 -> 17, of which waited for: 11 -> 11; matrix products, arithmetic and copies ran while one was open for 2% -> 3% of each run, Pallas kernels for 9% -> 9%
where the time goes in v5:
time: 56.1 us; the launch traced here: 55.9 us
  starting transfers between devices  25.5 us (45%)
  waiting for transfers between devices  21.3 us (38%)
  Pallas kernels  6.83 us (12%)
  other arithmetic  0.86 us (2%)
  between operations  0.76 us (1%)
  local copies, waits for them, and re-layouts  0.69 us (1%)
    ppermute x17, starting transfers between devices, send(): return lax.ppermute(value, AXES, route)  25.5 us
    ppermute x17, waiting for transfers between devices, send(): return lax.ppermute(value, AXES, route)  21.3 us
    pallas_call x1, Pallas kernels, dense_blocks(): pl.pallas_call(functools.partial(dense_kernel, blocks, near, halves), in_...  2.98 us
    pallas_call x2, Pallas kernels, aggregate(): pl.pallas_call(functools.partial(aggregate_kernel, spans, len(given) - le...  1.42 us
  transfers between devices with their start and end apart: 17, of which 11 were waited for; matrix products, arithmetic and copies ran while one was open for 3% of the time, Pallas kernels for 9%

profile of v5, /device:TPU:0, one launch (start us, length us, event | category | flops | bytes accessed | tf_op | source)
XLA Modules:
  0.0 55.9 jit_solution(1551038608615519527)
XLA Ops:
  0.6 4.1 %collective-permute-start.2 = (bf16[512,128]{1,0:T(8,128)(2,1)}, bf16[512,128]{1,0:T(8,128)(2,1)S(1)}, u32[]{:S(2)}, u32[]{:S(2)}) collective-permute-start(bf16[512,128]{1,0:T(8,128)(2,1)} %param.6), channel_id=1, source_target_pairs={{0,16},{1,19},{2,18},{3,17},{4,20},{5,23},{6,22},{7,21},{8,24},{9,... | collective-permute-start | bytes 393224 | tf_op jit(solution)/shard_map/ppermute | solution.py:357
  4.7 1.6 %collective-permute-start.3 = (bf16[512,128]{1,0:T(8,128)(2,1)}, bf16[512,128]{1,0:T(8,128)(2,1)S(1)}, u32[]{:S(2)}, u32[]{:S(2)}) collective-permute-start(bf16[512,128]{1,0:T(8,128)(2,1)} %param.6), channel_id=1, source_target_pairs={{0,8},{1,11},{2,10},{3,9},{4,12},{5,15},{6,14},{7,13},{8,0},{9,3},... | collective-permute-start | bytes 393224 | tf_op jit(solution)/shard_map/ppermute | solution.py:357
  6.3 1.5 %collective-permute-start.1 = (bf16[512,128]{1,0:T(8,128)(2,1)}, bf16[512,128]{1,0:T(8,128)(2,1)S(1)}, u32[]{:S(2)}, u32[]{:S(2)}) collective-permute-start(bf16[512,128]{1,0:T(8,128)(2,1)} %param.6), channel_id=1, source_target_pairs={{0,4},{1,7},{2,6},{3,5},{4,0},{5,3},{6,2},{7,1},{8,12},{9,15},{10,... | collective-permute-start | bytes 393224 | tf_op jit(solution)/shard_map/ppermute | solution.py:357
  7.8 1.6 %collective-permute-start = (bf16[512,128]{1,0:T(8,128)(2,1)}, bf16[512,128]{1,0:T(8,128)(2,1)S(1)}, u32[]{:S(2)}, u32[]{:S(2)}) collective-permute-start(bf16[512,128]{1,0:T(8,128)(2,1)} %param.6), channel_id=1, source_target_pairs={{0,0},{1,3},{2,2},{3,1},{4,4},{5,7},{6,6},{7,5},{8,8},{9,11},{10,1... | collective-permute-start | bytes 393224 | tf_op jit(solution)/shard_map/ppermute | solution.py:357
  9.4 1.7 %collective-permute-start.8 = (bf16[256,256]{1,0:T(8,128)(2,1)}, bf16[256,256]{1,0:T(8,128)(2,1)S(1)}, u32[]{:S(2)}, u32[]{:S(2)}) collective-permute-start(bf16[256,256]{1,0:T(8,128)(2,1)} %cot_ref.1), channel_id=1, source_target_pairs={{0,1},{1,0},{2,3},{3,2},{4,5},{5,4},{6,7},{7,6},{8,9},{9,8},{10,11... | collective-permute-start | bytes 393224 | tf_op jit(solution)/shard_map/ppermute | solution.py:357
  11.1 0.2 collective-permute-done.2
  11.4 0.2 collective-permute-done.3
  11.6 1.6 %collective-permute-start.4 = (bf16[1024,128]{1,0:T(8,128)(2,1)S(1)}, bf16[1024,128]{1,0:T(8,128)(2,1)S(1)}, u32[]{:S(2)}, u32[]{:S(2)}) collective-permute-start(bf16[1024,128]{1,0:T(8,128)(2,1)S(1)} %constant_dynamic-update-slice_fusion.refs_2_), channel_id=1, source_target_pairs={{0,4},{1,5},{2,6},{3,7},{4,0},{5,1},{6,2},{7,3},{8,12},{9,13},{10,... | collective-permute-start | bytes 786440 | tf_op jit(solution)/shard_map/ppermute | solution.py:357
  13.2 1.4 %collective-permute-start.5 = (bf16[512,128]{1,0:T(8,128)(2,1)S(1)}, bf16[512,128]{1,0:T(8,128)(2,1)S(1)}, u32[]{:S(2)}, u32[]{:S(2)}) collective-permute-start(bf16[512,128]{1,0:T(8,128)(2,1)S(1)} %collective-permute-done.2), channel_id=1, source_target_pairs={{0,8},{1,9},{2,10},{3,11},{4,12},{5,13},{6,14},{7,15},{8,0},{9,1},... | collective-permute-start | bytes 393224 | tf_op jit(solution)/shard_map/ppermute | solution.py:357
  14.6 0.8 %bitcast_select_fusion = s32[8,12]{1,0:T(8,128)S(1)} fusion(s32[1,1,8,12]{3,2,1,0:T(8,128)} %param.9, s32[]{:T(128)S(6)} %mul.14, s32[8]{0:T(128)} %bitcast.5), kind=kLoop, calls=%fused_computation.13 | loop fusion | flops 288 | bytes 804 | tf_op jit(solution)/shard_map/jit(_where)/select_n | solution.py:367
  15.4 2.8 %collective-permute-done.5.refs_4_ = bf16[512,128]{1,0:T(8,128)(2,1)S(1)} collective-permute-done((bf16[512,128]{1,0:T(8,128)(2,1)S(1)}, bf16[512,128]{1,0:T(8,128)(2,1)S(1)}, u32[]{:S(2)}, u32[]{:S(2)}) %collective-permute-start.5) | collective-permute-done | bytes 131104 | tf_op jit(solution)/shard_map/ppermute | solution.py:357
  18.2 0.5 collective-permute-start.6
  18.7 0.1 pad_add_fusion.table
  18.7 3.0 %dense_blocks.1.dense_ref = bf16[4,512,1024]{2,1,0:T(8,128)(2,1)S(1)} custom-call(s32[8,13]{1,0:T(8,128)S(1)} %pad_add_fusion.table, bf16[8,12,128,128]{3,2,1,0:T(8,128)(2,1)} %bitcast.4), custom_call_target="tpu_custom_call" | custom-call | tf_op jit(solution)/shard_map/dense_blocks/pallas_call | solution.py:82
  21.7 0.0 copy-start
  21.7 0.0 copy-start.1
  21.7 0.0 collective-permute-done.1.refs_1_
  21.8 0.0 collective-permute-done.refs_0_
  21.8 0.0 collective-permute-done.4.refs_3_
  21.8 1.1 %aggregate.2.refs_0_ = f32[512,128]{1,0:T(8,128)S(1)} custom-call(bf16[4,512,1024]{2,1,0:T(8,128)(2,1)S(1)} %dense_blocks.1.dense_ref, bf16[512,128]{1,0:T(8,128)(2,1)S(1)} %collective-permute-done.refs_0_, bf16[512,128]{1,0:T(8,128)(2,1)S(1)} %collective-permute-done.1.refs_1_, bf16[1024,128]{1,0:T(8,128)(2,1)S(1)} %constant_dynamic-update-slice_fusion.refs_2_, ...), custom_call_target="tpu_custom_call" | custom-call | tf_op jit(solution)/shard_map/aggregate/pallas_call | solution.py:118
  22.9 0.2 collective-permute-done.6.refs_1_
  23.1 0.3 aggregate.3.own_ref
  23.5 2.2 %collective-permute-start.7 = (bf16[512,128]{1,0:T(8,128)(2,1)S(1)}, bf16[512,128]{1,0:T(8,128)(2,1)S(1)}, u32[]{:S(2)}, u32[]{:S(2)}) collective-permute-start(bf16[512,128]{1,0:T(8,128)(2,1)S(1)} %aggregate.3.own_ref), channel_id=1, source_target_pairs={{0,1},{1,0},{2,3},{3,2},{4,5},{5,4},{6,7},{7,6},{8,9},{9,8},{10,11... | collective-permute-start | bytes 393224 | tf_op jit(solution)/shard_map/ppermute | solution.py:357
  25.7 0.0 collective-permute-done.8.far_cot_ref
  25.7 2.9 %collective-permute-done.7.other_ref = bf16[512,128]{1,0:T(8,128)(2,1)S(1)} collective-permute-done((bf16[512,128]{1,0:T(8,128)(2,1)S(1)}, bf16[512,128]{1,0:T(8,128)(2,1)S(1)}, u32[]{:S(2)}, u32[]{:S(2)}) %collective-permute-start.7) | collective-permute-done | bytes 131104 | tf_op jit(solution)/shard_map/ppermute | solution.py:357
  28.6 0.0 copy-done
  28.6 0.0 copy-done.1
  28.7 0.9 %turn.1 = (bf16[256,256]{1,0:T(8,128)(2,1)S(1)}, bf16[128,512]{1,0:T(8,128)(2,1)S(1)}, bf16[128,1152]{1,0:T(8,128)(2,1)S(1)}) custom-call(bf16[512,128]{1,0:T(8,128)(2,1)S(1)} %aggregate.3.own_ref, bf16[512,128]{1,0:T(8,128)(2,1)S(1)} %collective-permute-done.7.other_ref, bf16[128,256]{1,0:T(8,128)(2,1)S(1)} %copy-done.1, bf16[256,256]{1,0:T(8,128)(2,1)S(1)} %copy-done, ...), custom_call_target="tpu_custom_call" | custom-call | tf_op jit(solution)/shard_map/turn/pallas_call | solution.py:157
  29.5 0.1 collective-permute-start.9
  29.6 0.6 %rest_terms.1 = (bf16[128,1024]{1,0:T(8,128)(2,1)S(1)}, f32[2,128,1024]{2,1,0:T(8,128)S(1)}) custom-call(bf16[128,512]{1,0:T(8,128)(2,1)S(1)} %get-tuple-element.21.back_ref, bf16[4,512,1024]{2,1,0:T(8,128)(2,1)S(1)} %dense_blocks.1.dense_ref), custom_call_target="tpu_custom_call" | custom-call | tf_op jit(solution)/shard_map/rest_terms/pallas_call | solution.py:184
  30.2 1.8 %collective-permute-start.13 = (bf16[128,1024]{1,0:T(8,128)(2,1)S(1)}, bf16[128,1024]{1,0:T(8,128)(2,1)S(1)}, u32[]{:S(2)}, u32[]{:S(2)}) collective-permute-start(bf16[128,1024]{1,0:T(8,128)(2,1)S(1)} %get-tuple-element.27.own_ref), channel_id=1, source_target_pairs={{0,3},{1,5},{2,6},{3,0},{4,7},{5,1},{6,2},{7,4},{8,11},{9,13},{10,... | collective-permute-start | bytes 786440 | tf_op jit(solution)/shard_map/ppermute | solution.py:357
  32.0 3.7 %collective-permute-done.9.got_ref = bf16[128,1152]{1,0:T(8,128)(2,1)S(1)} collective-permute-done((bf16[128,1152]{1,0:T(8,128)(2,1)S(1)}, bf16[128,1152]{1,0:T(8,128)(2,1)S(1)}, u32[]{:S(2)}, u32[]{:S(2)}) %collective-permute-start.9) | collective-permute-done | bytes 294944 | tf_op jit(solution)/shard_map/ppermute | solution.py:357
  35.8 0.1 first_sum.2
  35.8 1.1 %collective-permute-start.10 = (bf16[128,640]{1,0:T(8,128)(2,1)S(1)}, bf16[128,640]{1,0:T(8,128)(2,1)S(1)}, u32[]{:S(2)}, u32[]{:S(2)}) collective-permute-start(bf16[128,640]{1,0:T(8,128)(2,1)S(1)} %get-tuple-element.23.own_ref), channel_id=1, source_target_pairs={{0,4},{1,2},{2,1},{3,7},{4,0},{5,6},{6,5},{7,3},{8,12},{9,10},{10,... | collective-permute-start | bytes 491528 | tf_op jit(solution)/shard_map/ppermute | solution.py:357
  36.9 1.7 %collective-permute-done.13.got_ref = bf16[128,1024]{1,0:T(8,128)(2,1)S(1)} collective-permute-done((bf16[128,1024]{1,0:T(8,128)(2,1)S(1)}, bf16[128,1024]{1,0:T(8,128)(2,1)S(1)}, u32[]{:S(2)}, u32[]{:S(2)}) %collective-permute-start.13) | collective-permute-done | bytes 262176 | tf_op jit(solution)/shard_map/ppermute | solution.py:357
  38.6 1.1 %collective-permute-start.14 = (bf16[128,512]{1,0:T(8,128)(2,1)S(1)}, bf16[128,512]{1,0:T(8,128)(2,1)S(1)}, u32[]{:S(2)}, u32[]{:S(2)}) collective-permute-start(bf16[128,512]{1,0:T(8,128)(2,1)S(1)} %get-tuple-element.28), channel_id=1, source_target_pairs={{0,4},{1,2},{2,1},{3,7},{4,0},{5,6},{6,5},{7,3},{8,12},{9,10},{10,... | collective-permute-start | bytes 393224 | tf_op jit(solution)/shard_map/ppermute | solution.py:357
  39.7 1.5 %collective-permute-done.10.got_ref = bf16[128,640]{1,0:T(8,128)(2,1)S(1)} collective-permute-done((bf16[128,640]{1,0:T(8,128)(2,1)S(1)}, bf16[128,640]{1,0:T(8,128)(2,1)S(1)}, u32[]{:S(2)}, u32[]{:S(2)}) %collective-permute-start.10) | collective-permute-done | bytes 163872 | tf_op jit(solution)/shard_map/ppermute | solution.py:357
  41.2 3.4 %collective-permute-start.11 = (bf16[128,384]{1,0:T(8,128)(2,1)S(1)}, bf16[128,384]{1,0:T(8,128)(2,1)S(1)}, u32[]{:S(2)}, u32[]{:S(2)}) collective-permute-start(bf16[128,384]{1,0:T(8,128)(2,1)S(1)} %get-tuple-element.25), channel_id=1, source_target_pairs={{0,24},{1,25},{2,26},{3,27},{4,28},{5,29},{6,30},{7,31},{8,16},{9,... | collective-permute-start | bytes 294920 | tf_op jit(solution)/shard_map/ppermute | solution.py:357
  44.7 0.0 collective-permute-start.12
  44.7 0.0 collective-permute-done.14.got_ref
  44.7 1.1 %collective-permute-start.15 = (bf16[128,384]{1,0:T(8,128)(2,1)S(1)}, bf16[128,384]{1,0:T(8,128)(2,1)S(1)}, u32[]{:S(2)}, u32[]{:S(2)}) collective-permute-start(bf16[128,384]{1,0:T(8,128)(2,1)S(1)} %get-tuple-element.31.sent_one_ref), channel_id=1, source_target_pairs={{0,8},{1,9},{2,10},{3,11},{4,12},{5,13},{6,14},{7,15},{8,0},{9,1},... | collective-permute-start | bytes 294920 | tf_op jit(solution)/shard_map/ppermute | solution.py:357
  45.8 2.0 %collective-permute-done.11.three_ref = bf16[128,384]{1,0:T(8,128)(2,1)S(1)} collective-permute-done((bf16[128,384]{1,0:T(8,128)(2,1)S(1)}, bf16[128,384]{1,0:T(8,128)(2,1)S(1)}, u32[]{:S(2)}, u32[]{:S(2)}) %collective-permute-start.11) | collective-permute-done | bytes 98336 | tf_op jit(solution)/shard_map/ppermute | solution.py:357
  47.8 5.6 %collective-permute-done.12.two_ref = bf16[128,384]{1,0:T(8,128)(2,1)S(1)} collective-permute-done((bf16[128,384]{1,0:T(8,128)(2,1)S(1)}, bf16[128,384]{1,0:T(8,128)(2,1)S(1)}, u32[]{:S(2)}, u32[]{:S(2)}) %collective-permute-start.12) | collective-permute-done | bytes 98336 | tf_op jit(solution)/shard_map/ppermute | solution.py:357
  53.4 0.0 collective-permute-done.15.one_ref
  53.5 0.8 %collective-permute-start.16 = (bf16[128,384]{1,0:T(8,128)(2,1)S(1)}, bf16[128,384]{1,0:T(8,128)(2,1)S(1)}, u32[]{:S(2)}, u32[]{:S(2)}) collective-permute-start(bf16[128,384]{1,0:T(8,128)(2,1)S(1)} %line_sum.1.own_ref), channel_id=1, source_target_pairs={{0,2},{1,3},{2,0},{3,1},{4,6},{5,7},{6,4},{7,5},{8,10},{9,11},{10,... | collective-permute-start | bytes 294920 | tf_op jit(solution)/shard_map/ppermute | solution.py:357
  54.2 0.7 %copy.10 = bf16[256,256]{1,0:T(8,128)(2,1)} copy(bf16[256,256]{1,0:T(8,128)(2,1)S(1)} %get-tuple-element.35) | data formatting | bytes 262144
  54.9 0.3 collective-permute-done.16.got_ref
  55.2 0.7 %finish.1 = (bf16[256,128]{1,0:T(8,128)(2,1)}, f32[128,256]{1,0:T(8,128)}) custom-call(bf16[128,384]{1,0:T(8,128)(2,1)S(1)} %line_sum.1.own_ref, bf16[128,384]{1,0:T(8,128)(2,1)S(1)} %collective-permute-done.16.got_ref), custom_call_target="tpu_custom_call" | custom-call | tf_op jit(solution)/shard_map/finish/pallas_call | solution.py:305
  (7 shorter events, 0.2 us)
Async XLA Ops:
  0.6 10.7 %collective-permute-start.2 = (bf16[512,128]{1,0:T(8,128)(2,1)}, bf16[512,128]{1,0:T(8,128)(2,1)S(1)}, u32[]{:S(2)}, u32[]{:S(2)}) collective-permute-start(bf16[512,128]{1,0:T(8,128)(2,1)} %param.6), channel_id=1, source_target_pairs={{0,16},{1,19},{2,18},{3,17},{4,20},{5,23},{6,22},{7,21},{8,24},{9,... | collective-permute-start | bytes 393224 | tf_op jit(solution)/shard_map/ppermute | solution.py:357
  4.7 6.8 %collective-permute-start.3 = (bf16[512,128]{1,0:T(8,128)(2,1)}, bf16[512,128]{1,0:T(8,128)(2,1)S(1)}, u32[]{:S(2)}, u32[]{:S(2)}) collective-permute-start(bf16[512,128]{1,0:T(8,128)(2,1)} %param.6), channel_id=1, source_target_pairs={{0,8},{1,11},{2,10},{3,9},{4,12},{5,15},{6,14},{7,13},{8,0},{9,3},... | collective-permute-start | bytes 393224 | tf_op jit(solution)/shard_map/ppermute | solution.py:357
  6.3 15.4 %collective-permute-start.1 = (bf16[512,128]{1,0:T(8,128)(2,1)}, bf16[512,128]{1,0:T(8,128)(2,1)S(1)}, u32[]{:S(2)}, u32[]{:S(2)}) collective-permute-start(bf16[512,128]{1,0:T(8,128)(2,1)} %param.6), channel_id=1, source_target_pairs={{0,4},{1,7},{2,6},{3,5},{4,0},{5,3},{6,2},{7,1},{8,12},{9,15},{10,... | collective-permute-start | bytes 393224 | tf_op jit(solution)/shard_map/ppermute | solution.py:357
  7.8 13.9 %collective-permute-start = (bf16[512,128]{1,0:T(8,128)(2,1)}, bf16[512,128]{1,0:T(8,128)(2,1)S(1)}, u32[]{:S(2)}, u32[]{:S(2)}) collective-permute-start(bf16[512,128]{1,0:T(8,128)(2,1)} %param.6), channel_id=1, source_target_pairs={{0,0},{1,3},{2,2},{3,1},{4,4},{5,7},{6,6},{7,5},{8,8},{9,11},{10,1... | collective-permute-start | bytes 393224 | tf_op jit(solution)/shard_map/ppermute | solution.py:357
  9.4 16.3 %collective-permute-start.8 = (bf16[256,256]{1,0:T(8,128)(2,1)}, bf16[256,256]{1,0:T(8,128)(2,1)S(1)}, u32[]{:S(2)}, u32[]{:S(2)}) collective-permute-start(bf16[256,256]{1,0:T(8,128)(2,1)} %cot_ref.1), channel_id=1, source_target_pairs={{0,1},{1,0},{2,3},{3,2},{4,5},{5,4},{6,7},{7,6},{8,9},{9,8},{10,11... | collective-permute-start | bytes 393224 | tf_op jit(solution)/shard_map/ppermute | solution.py:357
  11.6 10.2 %collective-permute-start.4 = (bf16[1024,128]{1,0:T(8,128)(2,1)S(1)}, bf16[1024,128]{1,0:T(8,128)(2,1)S(1)}, u32[]{:S(2)}, u32[]{:S(2)}) collective-permute-start(bf16[1024,128]{1,0:T(8,128)(2,1)S(1)} %constant_dynamic-update-slice_fusion.refs_2_), channel_id=1, source_target_pairs={{0,4},{1,5},{2,6},{3,7},{4,0},{5,1},{6,2},{7,3},{8,12},{9,13},{10,... | collective-permute-start | bytes 786440 | tf_op jit(solution)/shard_map/ppermute | solution.py:357
  13.2 5.0 %collective-permute-start.5 = (bf16[512,128]{1,0:T(8,128)(2,1)S(1)}, bf16[512,128]{1,0:T(8,128)(2,1)S(1)}, u32[]{:S(2)}, u32[]{:S(2)}) collective-permute-start(bf16[512,128]{1,0:T(8,128)(2,1)S(1)} %collective-permute-done.2), channel_id=1, source_target_pairs={{0,8},{1,9},{2,10},{3,11},{4,12},{5,13},{6,14},{7,15},{8,0},{9,1},... | collective-permute-start | bytes 393224 | tf_op jit(solution)/shard_map/ppermute | solution.py:357
  18.2 5.0 %collective-permute-start.6 = (bf16[512,128]{1,0:T(8,128)(2,1)S(1)}, bf16[512,128]{1,0:T(8,128)(2,1)S(1)}, u32[]{:S(2)}, u32[]{:S(2)}) collective-permute-start(bf16[512,128]{1,0:T(8,128)(2,1)S(1)} %collective-permute-done.5.refs_4_), channel_id=1, source_target_pairs={{0,4},{1,5},{2,6},{3,7},{4,0},{5,1},{6,2},{7,3},{8,12},{9,13},{10,... | collective-permute-start | bytes 393224 | tf_op jit(solution)/shard_map/ppermute | solution.py:357
  21.7 6.9 %copy-start = (bf16[256,256]{1,0:T(8,128)(2,1)S(1)}, bf16[256,256]{1,0:T(8,128)(2,1)}, u32[]{:S(2)}) copy-start(bf16[256,256]{1,0:T(8,128)(2,1)} %cot_ref.1) | copy-start | bytes 393220
  21.7 6.9 %copy-start.1 = (bf16[128,256]{1,0:T(8,128)(2,1)S(1)}, bf16[128,256]{1,0:T(8,128)(2,1)}, u32[]{:S(2)}) copy-start(bf16[128,256]{1,0:T(8,128)(2,1)} %weight_ref.1) | copy-start | bytes 196612
  23.5 5.2 %collective-permute-start.7 = (bf16[512,128]{1,0:T(8,128)(2,1)S(1)}, bf16[512,128]{1,0:T(8,128)(2,1)S(1)}, u32[]{:S(2)}, u32[]{:S(2)}) collective-permute-start(bf16[512,128]{1,0:T(8,128)(2,1)S(1)} %aggregate.3.own_ref), channel_id=1, source_target_pairs={{0,1},{1,0},{2,3},{3,2},{4,5},{5,4},{6,7},{7,6},{8,9},{9,8},{10,11... | collective-permute-start | bytes 393224 | tf_op jit(solution)/shard_map/ppermute | solution.py:357
  29.5 6.2 %collective-permute-start.9 = (bf16[128,1152]{1,0:T(8,128)(2,1)S(1)}, bf16[128,1152]{1,0:T(8,128)(2,1)S(1)}, u32[]{:S(2)}, u32[]{:S(2)}) collective-permute-start(bf16[128,1152]{1,0:T(8,128)(2,1)S(1)} %get-tuple-element.20.own_ref), channel_id=1, source_target_pairs={{0,3},{1,5},{2,6},{3,0},{4,7},{5,1},{6,2},{7,4},{8,11},{9,13},{10,... | collective-permute-start | bytes 884744 | tf_op jit(solution)/shard_map/ppermute | solution.py:357
  30.2 8.3 %collective-permute-start.13 = (bf16[128,1024]{1,0:T(8,128)(2,1)S(1)}, bf16[128,1024]{1,0:T(8,128)(2,1)S(1)}, u32[]{:S(2)}, u32[]{:S(2)}) collective-permute-start(bf16[128,1024]{1,0:T(8,128)(2,1)S(1)} %get-tuple-element.27.own_ref), channel_id=1, source_target_pairs={{0,3},{1,5},{2,6},{3,0},{4,7},{5,1},{6,2},{7,4},{8,11},{9,13},{10,... | collective-permute-start | bytes 786440 | tf_op jit(solution)/shard_map/ppermute | solution.py:357
  35.8 5.4 %collective-permute-start.10 = (bf16[128,640]{1,0:T(8,128)(2,1)S(1)}, bf16[128,640]{1,0:T(8,128)(2,1)S(1)}, u32[]{:S(2)}, u32[]{:S(2)}) collective-permute-start(bf16[128,640]{1,0:T(8,128)(2,1)S(1)} %get-tuple-element.23.own_ref), channel_id=1, source_target_pairs={{0,4},{1,2},{2,1},{3,7},{4,0},{5,6},{6,5},{7,3},{8,12},{9,10},{10,... | collective-permute-start | bytes 491528 | tf_op jit(solution)/shard_map/ppermute | solution.py:357
  38.6 6.0 %collective-permute-start.14 = (bf16[128,512]{1,0:T(8,128)(2,1)S(1)}, bf16[128,512]{1,0:T(8,128)(2,1)S(1)}, u32[]{:S(2)}, u32[]{:S(2)}) collective-permute-start(bf16[128,512]{1,0:T(8,128)(2,1)S(1)} %get-tuple-element.28), channel_id=1, source_target_pairs={{0,4},{1,2},{2,1},{3,7},{4,0},{5,6},{6,5},{7,3},{8,12},{9,10},{10,... | collective-permute-start | bytes 393224 | tf_op jit(solution)/shard_map/ppermute | solution.py:357
  41.2 6.6 %collective-permute-start.11 = (bf16[128,384]{1,0:T(8,128)(2,1)S(1)}, bf16[128,384]{1,0:T(8,128)(2,1)S(1)}, u32[]{:S(2)}, u32[]{:S(2)}) collective-permute-start(bf16[128,384]{1,0:T(8,128)(2,1)S(1)} %get-tuple-element.25), channel_id=1, source_target_pairs={{0,24},{1,25},{2,26},{3,27},{4,28},{5,29},{6,30},{7,31},{8,16},{9,... | collective-permute-start | bytes 294920 | tf_op jit(solution)/shard_map/ppermute | solution.py:357
  44.7 8.7 %collective-permute-start.12 = (bf16[128,384]{1,0:T(8,128)(2,1)S(1)}, bf16[128,384]{1,0:T(8,128)(2,1)S(1)}, u32[]{:S(2)}, u32[]{:S(2)}) collective-permute-start(bf16[128,384]{1,0:T(8,128)(2,1)S(1)} %get-tuple-element.26), channel_id=1, source_target_pairs={{0,16},{1,17},{2,18},{3,19},{4,20},{5,21},{6,22},{7,23},{8,24},{9,... | collective-permute-start | bytes 294920 | tf_op jit(solution)/shard_map/ppermute | solution.py:357
  44.7 8.7 %collective-permute-start.15 = (bf16[128,384]{1,0:T(8,128)(2,1)S(1)}, bf16[128,384]{1,0:T(8,128)(2,1)S(1)}, u32[]{:S(2)}, u32[]{:S(2)}) collective-permute-start(bf16[128,384]{1,0:T(8,128)(2,1)S(1)} %get-tuple-element.31.sent_one_ref), channel_id=1, source_target_pairs={{0,8},{1,9},{2,10},{3,11},{4,12},{5,13},{6,14},{7,15},{8,0},{9,1},... | collective-permute-start | bytes 294920 | tf_op jit(solution)/shard_map/ppermute | solution.py:357
  53.5 1.7 %collective-permute-start.16 = (bf16[128,384]{1,0:T(8,128)(2,1)S(1)}, bf16[128,384]{1,0:T(8,128)(2,1)S(1)}, u32[]{:S(2)}, u32[]{:S(2)}) collective-permute-start(bf16[128,384]{1,0:T(8,128)(2,1)S(1)} %line_sum.1.own_ref), channel_id=1, source_target_pairs={{0,2},{1,3},{2,0},{3,1},{4,6},{5,7},{6,4},{7,5},{8,10},{9,11},{10,... | collective-permute-start | bytes 294920 | tf_op jit(solution)/shard_map/ppermute | solution.py:357

commit v6 on v5

--- a/solution.py
+++ b/solution.py
@@ -126,7 +126,7 @@
 
 
 def turn_kernel(share, chunk, own_ref, other_ref, weight_ref, cot_ref, far_cot_ref, dense_ref,
-                act_ref, back_ref, sent_ref, g_ref, grad_ref):
+                act_ref, back_ref, sent_ref, wg_ref, g_ref, grad_ref):
     rows = own_ref.shape[0]
     weight = weight_ref[...]
     for half, cot in enumerate((cot_ref, far_cot_ref)):
@@ -145,9 +145,9 @@
     for second in range(2):
         term = dot(back, dense_ref[unit_at(2 + second), :, pl.ds(start, size)])
         sent_ref[:, pl.ds(second * size, size)] = term.astype(jnp.bfloat16)
-    part = sent_ref.shape[1] - 2 * size
+    part = wg_ref.shape[1]
     columns = pl.ds(pl.multiple_of(lane_of_class() * part, part), part)
-    sent_ref[:, pl.ds(2 * size, part)] = tn_dot(g_ref[...], grad_ref[:, columns]).astype(jnp.bfloat16)
+    wg_ref[...] = tn_dot(g_ref[...], grad_ref[:, columns]).astype(jnp.bfloat16)
 
 
 def turn(chunk, own, other, weight, cot, far_cot, dense):
@@ -157,11 +157,12 @@
     return pl.pallas_call(
         functools.partial(turn_kernel, share, chunk),
         in_specs=in_vmem(6),
-        out_specs=in_vmem(3),
+        out_specs=in_vmem(4),
         out_shape=[
             pltpu.VMEM((share, hid), bf),
             jax.ShapeDtypeStruct((width, rows), bf),
-            jax.ShapeDtypeStruct((width, 2 * chunk[1] + hid // 2), bf),
+            jax.ShapeDtypeStruct((width, 2 * chunk[1]), bf),
+            jax.ShapeDtypeStruct((width, hid // 2), bf),
         ],
         scratch_shapes=[pltpu.VMEM((rows, width), bf), pltpu.VMEM((rows, hid), bf)],
         compiler_params=params(),
@@ -192,101 +193,86 @@
     )(back, held_in_vmem(dense))
 
 
-def first_sum_kernel(start, size, got_ref, kept_ref, own_ref, sent_ref, total_ref):
-    extra = sent_ref.shape[1] - size
+def first_sum_kernel(start, size, got_ref, kept_ref, after_ref, sent_ref, total_ref, mark_ref):
     total_ref[...] = kept_ref[0, :, pl.ds(start, size)] + got_ref[:, pl.ds(0, size)].astype(jnp.float32)
     passed = kept_ref[1, :, pl.ds(start, size)] + got_ref[:, pl.ds(size, size)].astype(jnp.float32)
-    sent_ref[:, pl.ds(0, size)] = passed.astype(jnp.bfloat16)
-    if extra:
-        ours = own_ref[:, pl.ds(2 * size, extra)].astype(jnp.float32)
-        theirs = got_ref[:, pl.ds(2 * size, extra)].astype(jnp.float32)
-        sent_ref[:, pl.ds(size, extra)] = (ours + theirs).astype(jnp.bfloat16)
-
-
-def first_sum(chunk, got, kept, own):
+    sent_ref[...] = passed.astype(jnp.bfloat16)
+    mark_ref[...] = jnp.zeros_like(mark_ref)
+
+
+MARK = jax.ShapeDtypeStruct((16, 128), jnp.bfloat16)
+
+
+def first_sum(chunk, got, kept, after):
     width = kept.shape[1]
     start, size = chunk
-    extra = got.shape[1] - 2 * size
     return pl.pallas_call(
         functools.partial(first_sum_kernel, start, size),
         in_specs=in_vmem(3),
-        out_specs=in_vmem(2),
+        out_specs=in_vmem(3),
         out_shape=[
-            jax.ShapeDtypeStruct((width, size + extra), jnp.bfloat16),
+            jax.ShapeDtypeStruct((width, size), jnp.bfloat16),
             jax.ShapeDtypeStruct((width, size), jnp.float32),
+            MARK,
         ],
         compiler_params=params(),
         name="first_sum",
-    )(got, kept, own)
-
-
-def second_sum_kernel(got_ref, kept_ref, own_ref, two_ref, three_ref, wg_ref):
+    )(got, kept, after)
+
+
+def second_sum_kernel(got_ref, kept_ref, after_ref, first_ref, second_ref, mark_ref):
     piece = kept_ref.shape[1] // 2
-    part = two_ref.shape[1] - piece
-    tail = pl.ds(2 * piece, part)
-    wg = own_ref[:, tail].astype(jnp.float32) + got_ref[:, tail].astype(jnp.float32)
-    wg_ref[...] = wg.astype(jnp.bfloat16)
-    for at, out in enumerate((two_ref, three_ref)):
+    for at, out in enumerate((first_ref, second_ref)):
         span = pl.ds(at * piece, piece)
-        out[:, pl.ds(0, piece)] = (kept_ref[:, span] + got_ref[:, span].astype(jnp.float32)).astype(jnp.bfloat16)
-        out[:, pl.ds(piece, part)] = wg.astype(jnp.bfloat16)
-
-
-def second_sum(got, kept, own):
+        out[...] = (kept_ref[:, span] + got_ref[:, span].astype(jnp.float32)).astype(out.dtype)
+    mark_ref[...] = jnp.zeros_like(mark_ref)
+
+
+def second_sum(got, kept, first_type, after):
     width, size = kept.shape
-    message = jax.ShapeDtypeStruct((width, got.shape[1] - size // 2), jnp.bfloat16)
     return pl.pallas_call(
         second_sum_kernel,
         in_specs=in_vmem(3),
         out_specs=in_vmem(3),
-        out_shape=[message] * 2 + [jax.ShapeDtypeStruct((width, got.shape[1] - size), jnp.bfloat16)],
+        out_shape=[jax.ShapeDtypeStruct((width, size // 2), kind) for kind in (first_type, jnp.bfloat16)] + [MARK],
         compiler_params=params(),
         name="second_sum",
-    )(got, kept, own)
-
-
-def last_sum_kernel(got_ref, kept_ref, wg_ref, zero_ref, one_ref):
-    piece = zero_ref.shape[1]
-    tail = pl.ds(piece, one_ref.shape[1] - piece)
-    zero_ref[...] = kept_ref[:, pl.ds(0, piece)] + got_ref[:, pl.ds(0, piece)].astype(jnp.float32)
-    span = pl.ds(piece, piece)
-    one_ref[:, pl.ds(0, piece)] = (kept_ref[:, span] + got_ref[:, span].astype(jnp.float32)).astype(jnp.bfloat16)
-    one_ref[:, tail] = wg_ref[...]
-
-
-def last_sum(got, kept, wg):
-    width, size = kept.shape
-    return pl.pallas_call(
-        last_sum_kernel,
+    )(got, kept, after)
+
+
+def add_kernel(a_ref, b_ref, after_ref, out_ref):
+    out_ref[...] = (a_ref[...].astype(jnp.float32) + b_ref[...].astype(jnp.float32)).astype(out_ref.dtype)
+
+
+def add(a, b, after):
+    return pl.pallas_call(
+        add_kernel,
         in_specs=in_vmem(3),
-        out_specs=in_vmem(2),
-        out_shape=[
-            jax.ShapeDtypeStruct((width, size // 2), jnp.float32),
-            jax.ShapeDtypeStruct((width, size // 2 + wg.shape[1]), jnp.bfloat16),
-        ],
-        compiler_params=params(),
-        name="last_sum",
-    )(got, kept, wg)
-
-
-def line_sum_kernel(three_ref, two_ref, one_ref, sent_one_ref, zero_ref, out_ref):
+        out_specs=in_vmem(1)[0],
+        out_shape=jax.ShapeDtypeStruct(a.shape, a.dtype),
+        compiler_params=params(),
+        name="add",
+    )(a, b, after)
+
+
+def line_sum_kernel(three_ref, two_ref, one_ref, zero_ref, wg_ref, got_wg_ref, out_ref):
     piece = zero_ref.shape[1]
     span, tail = pl.ds(0, piece), pl.ds(piece, out_ref.shape[1] - piece)
-    three, two, one = [ref[:, span].astype(jnp.float32) for ref in (three_ref, two_ref, one_ref)]
+    three, two, one = [ref[...].astype(jnp.float32) for ref in (three_ref, two_ref, one_ref)]
     out_ref[:, span] = ((zero_ref[...] + one) + (two + three)).astype(jnp.bfloat16)
-    three, two, one, own = [ref[:, tail].astype(jnp.float32) for ref in (three_ref, two_ref, one_ref, sent_one_ref)]
-    out_ref[:, tail] = ((own + one) + (two + three)).astype(jnp.bfloat16)
-
-
-def line_sum(three, two, one, sent_one, zero):
+    out_ref[:, tail] = (wg_ref[...].astype(jnp.float32) + got_wg_ref[...].astype(jnp.float32)).astype(jnp.bfloat16)
+
+
+def line_sum(three, two, one, zero, wg, got_wg):
+    width, piece = zero.shape
     return pl.pallas_call(
         line_sum_kernel,
-        in_specs=in_vmem(5),
+        in_specs=in_vmem(6),
         out_specs=in_vmem(1)[0],
-        out_shape=jax.ShapeDtypeStruct(two.shape, jnp.bfloat16),
+        out_shape=jax.ShapeDtypeStruct((width, piece + wg.shape[1]), jnp.bfloat16),
         compiler_params=params(),
         name="line_sum",
-    )(three, two, one, sent_one, zero)
+    )(three, two, one, zero, wg, got_wg)
 
 
 def finish_kernel(own_ref, got_ref, feat_ref, wg_ref):
@@ -390,20 +376,25 @@
     partial = aggregate(dense, [(0, 2, 3 * share, 0, share)], [beside_three], partial, jnp.bfloat16)
     other = send(partial, lay.plain(0, 1))
     chunk_a, chunk_b = (2 * share, 2 * share), (0, 2 * share)
-    act, back, sent_a = turn(chunk_a, partial, other, weight, cotangent, far_cot, dense)
+    act, back, sent_a, wg = turn(chunk_a, partial, other, weight, cotangent, far_cot, dense)
     got_a = send(sent_a, lay.along(True))
     sent_b, kept = rest_terms([chunk_b], back, dense)
     got_b = send(sent_b, lay.along(True))
-    passed_a, kept_a = first_sum(chunk_a, got_a, kept, sent_a)
+    got_w1 = send(wg, lay.in_class(2 * near))
+    passed_a, kept_a, mark_a = first_sum(chunk_a, got_a, kept, got_w1)
     back_a = send(passed_a, lay.along(False))
-    passed_b, kept_b = first_sum(chunk_b, got_b, kept, sent_b)
+    passed_b, kept_b, mark_b = first_sum(chunk_b, got_b, kept, mark_a)
     back_b = send(passed_b, lay.along(False))
-    sent_two, sent_three, wg = second_sum(back_a, kept_a, passed_a)
-    three = send(sent_three, lay.in_class(3 * near))
-    two = send(sent_two, lay.in_class(2 * near))
-    zero, sent_one = last_sum(back_b, kept_b, wg)
-    one = send(sent_one, lay.in_class(near))
-    ours = line_sum(three, two, one, sent_one, zero)
+    wg = add(wg, got_w1, mark_b)
+    got_w2 = send(wg, lay.in_class(near))
+    two, three, mark_c = second_sum(back_a, kept_a, jnp.bfloat16, back)
+    three = send(three, lay.in_class(3 * near))
+    two = send(two, lay.in_class(2 * near))
+    zero, one, mark_d = second_sum(back_b, kept_b, jnp.float32, mark_c)
+    one = send(one, lay.in_class(near))
+    wg = add(wg, got_w2, mark_c)
+    wg = add(wg, send(wg, lay.along(True)), mark_d)
+    ours = line_sum(three, two, one, zero, wg, send(wg, lay.along(False)))
     feat_grad, weight_grad = finish(ours, send(ours, lay.plain(1, 0)), share)
     return act, feat_grad, weight_grad
 

time: 56.1 us -> 55.3 us (0.986)
  waiting for transfers between devices: 21.3 us -> 15.6 us
  starting transfers between devices: 25.5 us -> 30.2 us
    ppermute x17 -> x21, waiting for transfers between devices: 21.3 us -> 15.6 us  [send(): return lax.ppermute(value, AXES, route)]
    ppermute x17 -> x21, starting transfers between devices: 25.5 us -> 30.2 us  [send(): return lax.ppermute(value, AXES, route)]
  transfers between devices with their start and end apart: 17 -> 21, of which waited for: 11 -> 12; matrix products, arithmetic and copies ran while one was open for 3% -> 3% of each run, Pallas kernels for 9% -> 9%
where the time goes in v6:
time: 55.3 us; the launch traced here: 55.1 us
  starting transfers between devices  30.2 us (55%)
  waiting for transfers between devices  15.6 us (28%)
  Pallas kernels  6.9 us (12%)
  other arithmetic  0.86 us (2%)
  between operations  0.79 us (1%)
  local copies, waits for them, and re-layouts  0.69 us (1%)
    ppermute x21, starting transfers between devices, send(): return lax.ppermute(value, AXES, route)  30.2 us
    ppermute x21, waiting for transfers between devices, send(): return lax.ppermute(value, AXES, route)  15.6 us
    pallas_call x1, Pallas kernels, dense_blocks(): pl.pallas_call(functools.partial(dense_kernel, blocks, near, halves), in_...  2.98 us
    pallas_call x2, Pallas kernels, aggregate(): pl.pallas_call(functools.partial(aggregate_kernel, spans, len(given) - le...  1.42 us
  transfers between devices with their start and end apart: 21, of which 12 were waited for; matrix products, arithmetic and copies ran while one was open for 3% of the time, Pallas kernels for 9%

profile of v6, /device:TPU:0, one launch (start us, length us, event | category | flops | bytes accessed | tf_op | source)
XLA Modules:
  0.0 55.1 jit_solution(16155767648256704595)
XLA Ops:
  0.6 4.1 %collective-permute-start.2 = (bf16[512,128]{1,0:T(8,128)(2,1)}, bf16[512,128]{1,0:T(8,128)(2,1)S(1)}, u32[]{:S(2)}, u32[]{:S(2)}) collective-permute-start(bf16[512,128]{1,0:T(8,128)(2,1)} %param.6), channel_id=1, source_target_pairs={{0,16},{1,19},{2,18},{3,17},{4,20},{5,23},{6,22},{7,21},{8,24},{9,... | collective-permute-start | bytes 393224 | tf_op jit(solution)/shard_map/ppermute | solution.py:343
  4.7 1.6 %collective-permute-start.3 = (bf16[512,128]{1,0:T(8,128)(2,1)}, bf16[512,128]{1,0:T(8,128)(2,1)S(1)}, u32[]{:S(2)}, u32[]{:S(2)}) collective-permute-start(bf16[512,128]{1,0:T(8,128)(2,1)} %param.6), channel_id=1, source_target_pairs={{0,8},{1,11},{2,10},{3,9},{4,12},{5,15},{6,14},{7,13},{8,0},{9,3},... | collective-permute-start | bytes 393224 | tf_op jit(solution)/shard_map/ppermute | solution.py:343
  6.3 1.5 %collective-permute-start.1 = (bf16[512,128]{1,0:T(8,128)(2,1)}, bf16[512,128]{1,0:T(8,128)(2,1)S(1)}, u32[]{:S(2)}, u32[]{:S(2)}) collective-permute-start(bf16[512,128]{1,0:T(8,128)(2,1)} %param.6), channel_id=1, source_target_pairs={{0,4},{1,7},{2,6},{3,5},{4,0},{5,3},{6,2},{7,1},{8,12},{9,15},{10,... | collective-permute-start | bytes 393224 | tf_op jit(solution)/shard_map/ppermute | solution.py:343
  7.8 1.6 %collective-permute-start = (bf16[512,128]{1,0:T(8,128)(2,1)}, bf16[512,128]{1,0:T(8,128)(2,1)S(1)}, u32[]{:S(2)}, u32[]{:S(2)}) collective-permute-start(bf16[512,128]{1,0:T(8,128)(2,1)} %param.6), channel_id=1, source_target_pairs={{0,0},{1,3},{2,2},{3,1},{4,4},{5,7},{6,6},{7,5},{8,8},{9,11},{10,1... | collective-permute-start | bytes 393224 | tf_op jit(solution)/shard_map/ppermute | solution.py:343
  9.4 1.7 %collective-permute-start.8 = (bf16[256,256]{1,0:T(8,128)(2,1)}, bf16[256,256]{1,0:T(8,128)(2,1)S(1)}, u32[]{:S(2)}, u32[]{:S(2)}) collective-permute-start(bf16[256,256]{1,0:T(8,128)(2,1)} %cot_ref.1), channel_id=1, source_target_pairs={{0,1},{1,0},{2,3},{3,2},{4,5},{5,4},{6,7},{7,6},{8,9},{9,8},{10,11... | collective-permute-start | bytes 393224 | tf_op jit(solution)/shard_map/ppermute | solution.py:343
  11.1 0.2 collective-permute-done.2
  11.4 0.2 collective-permute-done.3
  11.6 1.6 %collective-permute-start.4 = (bf16[1024,128]{1,0:T(8,128)(2,1)S(1)}, bf16[1024,128]{1,0:T(8,128)(2,1)S(1)}, u32[]{:S(2)}, u32[]{:S(2)}) collective-permute-start(bf16[1024,128]{1,0:T(8,128)(2,1)S(1)} %constant_dynamic-update-slice_fusion.refs_2_), channel_id=1, source_target_pairs={{0,4},{1,5},{2,6},{3,7},{4,0},{5,1},{6,2},{7,3},{8,12},{9,13},{10,... | collective-permute-start | bytes 786440 | tf_op jit(solution)/shard_map/ppermute | solution.py:343
  13.2 1.4 %collective-permute-start.5 = (bf16[512,128]{1,0:T(8,128)(2,1)S(1)}, bf16[512,128]{1,0:T(8,128)(2,1)S(1)}, u32[]{:S(2)}, u32[]{:S(2)}) collective-permute-start(bf16[512,128]{1,0:T(8,128)(2,1)S(1)} %collective-permute-done.2), channel_id=1, source_target_pairs={{0,8},{1,9},{2,10},{3,11},{4,12},{5,13},{6,14},{7,15},{8,0},{9,1},... | collective-permute-start | bytes 393224 | tf_op jit(solution)/shard_map/ppermute | solution.py:343
  14.6 0.8 %bitcast_select_fusion = s32[8,12]{1,0:T(8,128)S(1)} fusion(s32[1,1,8,12]{3,2,1,0:T(8,128)} %param.9, s32[]{:T(128)S(6)} %mul.14, s32[8]{0:T(128)} %bitcast.5), kind=kLoop, calls=%fused_computation.13 | loop fusion | flops 288 | bytes 804 | tf_op jit(solution)/shard_map/jit(_where)/select_n | solution.py:353
  15.4 2.8 %collective-permute-done.5.refs_4_ = bf16[512,128]{1,0:T(8,128)(2,1)S(1)} collective-permute-done((bf16[512,128]{1,0:T(8,128)(2,1)S(1)}, bf16[512,128]{1,0:T(8,128)(2,1)S(1)}, u32[]{:S(2)}, u32[]{:S(2)}) %collective-permute-start.5) | collective-permute-done | bytes 131104 | tf_op jit(solution)/shard_map/ppermute | solution.py:343
  18.2 0.5 collective-permute-start.6
  18.7 0.1 pad_add_fusion.table
  18.7 3.0 %dense_blocks.1.dense_ref = bf16[4,512,1024]{2,1,0:T(8,128)(2,1)S(1)} custom-call(s32[8,13]{1,0:T(8,128)S(1)} %pad_add_fusion.table, bf16[8,12,128,128]{3,2,1,0:T(8,128)(2,1)} %bitcast.4), custom_call_target="tpu_custom_call" | custom-call | tf_op jit(solution)/shard_map/dense_blocks/pallas_call | solution.py:82
  21.7 0.0 copy-start
  21.7 0.0 copy-start.1
  21.8 0.0 collective-permute-done.refs_0_
  21.8 0.0 collective-permute-done.4.refs_3_
  21.8 1.1 %aggregate.2.refs_0_ = f32[512,128]{1,0:T(8,128)S(1)} custom-call(bf16[4,512,1024]{2,1,0:T(8,128)(2,1)S(1)} %dense_blocks.1.dense_ref, bf16[512,128]{1,0:T(8,128)(2,1)S(1)} %collective-permute-done.refs_0_, bf16[512,128]{1,0:T(8,128)(2,1)S(1)} %collective-permute-done.1.refs_1_, bf16[1024,128]{1,0:T(8,128)(2,1)S(1)} %constant_dynamic-update-slice_fusion.refs_2_, ...), custom_call_target="tpu_custom_call" | custom-call | tf_op jit(solution)/shard_map/aggregate/pallas_call | solution.py:118
  22.9 0.2 collective-permute-done.6.refs_1_
  23.1 0.3 aggregate.3.own_ref
  23.5 2.2 %collective-permute-start.7 = (bf16[512,128]{1,0:T(8,128)(2,1)S(1)}, bf16[512,128]{1,0:T(8,128)(2,1)S(1)}, u32[]{:S(2)}, u32[]{:S(2)}) collective-permute-start(bf16[512,128]{1,0:T(8,128)(2,1)S(1)} %aggregate.3.own_ref), channel_id=1, source_target_pairs={{0,1},{1,0},{2,3},{3,2},{4,5},{5,4},{6,7},{7,6},{8,9},{9,8},{10,11... | collective-permute-start | bytes 393224 | tf_op jit(solution)/shard_map/ppermute | solution.py:343
  25.7 0.0 collective-permute-done.8.far_cot_ref
  25.7 2.9 %collective-permute-done.7.other_ref = bf16[512,128]{1,0:T(8,128)(2,1)S(1)} collective-permute-done((bf16[512,128]{1,0:T(8,128)(2,1)S(1)}, bf16[512,128]{1,0:T(8,128)(2,1)S(1)}, u32[]{:S(2)}, u32[]{:S(2)}) %collective-permute-start.7) | collective-permute-done | bytes 131104 | tf_op jit(solution)/shard_map/ppermute | solution.py:343
  28.7 0.9 %turn.1 = (bf16[256,256]{1,0:T(8,128)(2,1)S(1)}, bf16[128,512]{1,0:T(8,128)(2,1)S(1)}, bf16[128,1024]{1,0:T(8,128)(2,1)S(1)}, bf16[128,128]{1,0:T(8,128)(2,1)S(1)}) custom-call(bf16[512,128]{1,0:T(8,128)(2,1)S(1)} %aggregate.3.own_ref, bf16[512,128]{1,0:T(8,128)(2,1)S(1)} %collective-permute-done.7.other_ref, bf16[128,256]{1,0:T(8,128)(2,1)S(1)} %copy-done.1, ...), custom_call_target="tpu_custom_call" | custom-call | tf_op jit(solution)/shard_map/turn/pallas_call | solution.py:157
  29.5 0.1 collective-permute-start.9
  29.6 0.7 %rest_terms.1 = (bf16[128,1024]{1,0:T(8,128)(2,1)S(1)}, f32[2,128,1024]{2,1,0:T(8,128)S(1)}) custom-call(bf16[128,512]{1,0:T(8,128)(2,1)S(1)} %get-tuple-element.25.back_ref.after_ref, bf16[4,512,1024]{2,1,0:T(8,128)(2,1)S(1)} %dense_blocks.1.dense_ref), custom_call_target="tpu_custom_call" | custom-call | tf_op jit(solution)/shard_map/rest_terms/pallas_call | solution.py:185
  30.3 1.8 %collective-permute-start.14 = (bf16[128,1024]{1,0:T(8,128)(2,1)S(1)}, bf16[128,1024]{1,0:T(8,128)(2,1)S(1)}, u32[]{:S(2)}, u32[]{:S(2)}) collective-permute-start(bf16[128,1024]{1,0:T(8,128)(2,1)S(1)} %get-tuple-element.32), channel_id=1, source_target_pairs={{0,3},{1,5},{2,6},{3,0},{4,7},{5,1},{6,2},{7,4},{8,11},{9,13},{10,... | collective-permute-start | bytes 786440 | tf_op jit(solution)/shard_map/ppermute | solution.py:343
  32.1 2.2 %collective-permute-start.10 = (bf16[128,128]{1,0:T(8,128)(2,1)S(1)}, bf16[128,128]{1,0:T(8,128)(2,1)S(1)}, u32[]{:S(2)}, u32[]{:S(2)}) collective-permute-start(bf16[128,128]{1,0:T(8,128)(2,1)S(1)} %get-tuple-element.27.a_ref), channel_id=1, source_target_pairs={{0,16},{1,17},{2,18},{3,19},{4,20},{5,21},{6,22},{7,23},{8,24},{9,... | collective-permute-start | bytes 98312 | tf_op jit(solution)/shard_map/ppermute | solution.py:343
  34.2 2.6 %collective-permute-done.10.after_ref.b_ref = bf16[128,128]{1,0:T(8,128)(2,1)S(1)} collective-permute-done((bf16[128,128]{1,0:T(8,128)(2,1)S(1)}, bf16[128,128]{1,0:T(8,128)(2,1)S(1)}, u32[]{:S(2)}, u32[]{:S(2)}) %collective-permute-start.10) | collective-permute-done | bytes 32800 | tf_op jit(solution)/shard_map/ppermute | solution.py:343
  36.9 1.1 %collective-permute-start.11 = (bf16[128,512]{1,0:T(8,128)(2,1)S(1)}, bf16[128,512]{1,0:T(8,128)(2,1)S(1)}, u32[]{:S(2)}, u32[]{:S(2)}) collective-permute-start(bf16[128,512]{1,0:T(8,128)(2,1)S(1)} %get-tuple-element.28), channel_id=1, source_target_pairs={{0,4},{1,2},{2,1},{3,7},{4,0},{5,6},{6,5},{7,3},{8,12},{9,10},{10,... | collective-permute-start | bytes 393224 | tf_op jit(solution)/shard_map/ppermute | solution.py:343
  38.0 0.2 collective-permute-done.14.got_ref
  38.3 1.1 %collective-permute-start.15 = (bf16[128,512]{1,0:T(8,128)(2,1)S(1)}, bf16[128,512]{1,0:T(8,128)(2,1)S(1)}, u32[]{:S(2)}, u32[]{:S(2)}) collective-permute-start(bf16[128,512]{1,0:T(8,128)(2,1)S(1)} %get-tuple-element.34), channel_id=1, source_target_pairs={{0,4},{1,2},{2,1},{3,7},{4,0},{5,6},{6,5},{7,3},{8,12},{9,10},{10,... | collective-permute-start | bytes 393224 | tf_op jit(solution)/shard_map/ppermute | solution.py:343
  39.4 1.6 %collective-permute-start.17 = (bf16[128,128]{1,0:T(8,128)(2,1)S(1)}, bf16[128,128]{1,0:T(8,128)(2,1)S(1)}, u32[]{:S(2)}, u32[]{:S(2)}) collective-permute-start(bf16[128,128]{1,0:T(8,128)(2,1)S(1)} %add.31.a_ref), channel_id=1, source_target_pairs={{0,8},{1,9},{2,10},{3,11},{4,12},{5,13},{6,14},{7,15},{8,0},{9,1},... | collective-permute-start | bytes 98312 | tf_op jit(solution)/shard_map/ppermute | solution.py:343
  41.0 1.0 %collective-permute-done.11.got_ref = bf16[128,512]{1,0:T(8,128)(2,1)S(1)} collective-permute-done((bf16[128,512]{1,0:T(8,128)(2,1)S(1)}, bf16[128,512]{1,0:T(8,128)(2,1)S(1)}, u32[]{:S(2)}, u32[]{:S(2)}) %collective-permute-start.11) | collective-permute-done | bytes 131104 | tf_op jit(solution)/shard_map/ppermute | solution.py:343
  42.0 3.5 %collective-permute-start.12 = (bf16[128,256]{1,0:T(8,128)(2,1)S(1)}, bf16[128,256]{1,0:T(8,128)(2,1)S(1)}, u32[]{:S(2)}, u32[]{:S(2)}) collective-permute-start(bf16[128,256]{1,0:T(8,128)(2,1)S(1)} %get-tuple-element.30), channel_id=1, source_target_pairs={{0,24},{1,25},{2,26},{3,27},{4,28},{5,29},{6,30},{7,31},{8,16},{9,... | collective-permute-start | bytes 196616 | tf_op jit(solution)/shard_map/ppermute | solution.py:343
  45.5 0.1 collective-permute-start.18
  45.6 1.0 %collective-permute-start.16 = (bf16[128,256]{1,0:T(8,128)(2,1)S(1)}, bf16[128,256]{1,0:T(8,128)(2,1)S(1)}, u32[]{:S(2)}, u32[]{:S(2)}) collective-permute-start(bf16[128,256]{1,0:T(8,128)(2,1)S(1)} %get-tuple-element.37), channel_id=1, source_target_pairs={{0,8},{1,9},{2,10},{3,11},{4,12},{5,13},{6,14},{7,15},{8,0},{9,1},... | collective-permute-start | bytes 196616 | tf_op jit(solution)/shard_map/ppermute | solution.py:343
  46.7 2.3 %collective-permute-done.18.b_ref = bf16[128,128]{1,0:T(8,128)(2,1)S(1)} collective-permute-done((bf16[128,128]{1,0:T(8,128)(2,1)S(1)}, bf16[128,128]{1,0:T(8,128)(2,1)S(1)}, u32[]{:S(2)}, u32[]{:S(2)}) %collective-permute-start.18) | collective-permute-done | bytes 32800 | tf_op jit(solution)/shard_map/ppermute | solution.py:343
  48.9 1.2 %collective-permute-start.19 = (bf16[128,128]{1,0:T(8,128)(2,1)S(1)}, bf16[128,128]{1,0:T(8,128)(2,1)S(1)}, u32[]{:S(2)}, u32[]{:S(2)}) collective-permute-start(bf16[128,128]{1,0:T(8,128)(2,1)S(1)} %add.33.wg_ref), channel_id=1, source_target_pairs={{0,4},{1,2},{2,1},{3,7},{4,0},{5,6},{6,5},{7,3},{8,12},{9,10},{10,... | collective-permute-start | bytes 98312 | tf_op jit(solution)/shard_map/ppermute | solution.py:343
  50.2 0.0 collective-permute-done.12.three_ref
  50.2 2.3 %collective-permute-done.13.two_ref = bf16[128,256]{1,0:T(8,128)(2,1)S(1)} collective-permute-done((bf16[128,256]{1,0:T(8,128)(2,1)S(1)}, bf16[128,256]{1,0:T(8,128)(2,1)S(1)}, u32[]{:S(2)}, u32[]{:S(2)}) %collective-permute-start.13) | collective-permute-done | bytes 65568 | tf_op jit(solution)/shard_map/ppermute | solution.py:343
  52.4 0.5 collective-permute-done.19.got_wg_ref
  52.9 0.0 collective-permute-done.16.one_ref
  53.0 0.4 collective-permute-start.20
  53.4 0.7 %copy.10 = bf16[256,256]{1,0:T(8,128)(2,1)} copy(bf16[256,256]{1,0:T(8,128)(2,1)S(1)} %get-tuple-element.43) | data formatting | bytes 262144
  54.0 0.3 collective-permute-done.20.got_ref
  54.3 0.7 %finish.1 = (bf16[256,128]{1,0:T(8,128)(2,1)}, f32[128,256]{1,0:T(8,128)}) custom-call(bf16[128,384]{1,0:T(8,128)(2,1)S(1)} %line_sum.1.own_ref, bf16[128,384]{1,0:T(8,128)(2,1)S(1)} %collective-permute-done.20.got_ref), custom_call_target="tpu_custom_call" | custom-call | tf_op jit(solution)/shard_map/finish/pallas_call | solution.py:291
  (18 shorter events, 0.3 us)
Async XLA Ops:
  0.6 10.7 %collective-permute-start.2 = (bf16[512,128]{1,0:T(8,128)(2,1)}, bf16[512,128]{1,0:T(8,128)(2,1)S(1)}, u32[]{:S(2)}, u32[]{:S(2)}) collective-permute-start(bf16[512,128]{1,0:T(8,128)(2,1)} %param.6), channel_id=1, source_target_pairs={{0,16},{1,19},{2,18},{3,17},{4,20},{5,23},{6,22},{7,21},{8,24},{9,... | collective-permute-start | bytes 393224 | tf_op jit(solution)/shard_map/ppermute | solution.py:343
  4.7 6.8 %collective-permute-start.3 = (bf16[512,128]{1,0:T(8,128)(2,1)}, bf16[512,128]{1,0:T(8,128)(2,1)S(1)}, u32[]{:S(2)}, u32[]{:S(2)}) collective-permute-start(bf16[512,128]{1,0:T(8,128)(2,1)} %param.6), channel_id=1, source_target_pairs={{0,8},{1,11},{2,10},{3,9},{4,12},{5,15},{6,14},{7,13},{8,0},{9,3},... | collective-permute-start | bytes 393224 | tf_op jit(solution)/shard_map/ppermute | solution.py:343
  6.3 15.4 %collective-permute-start.1 = (bf16[512,128]{1,0:T(8,128)(2,1)}, bf16[512,128]{1,0:T(8,128)(2,1)S(1)}, u32[]{:S(2)}, u32[]{:S(2)}) collective-permute-start(bf16[512,128]{1,0:T(8,128)(2,1)} %param.6), channel_id=1, source_target_pairs={{0,4},{1,7},{2,6},{3,5},{4,0},{5,3},{6,2},{7,1},{8,12},{9,15},{10,... | collective-permute-start | bytes 393224 | tf_op jit(solution)/shard_map/ppermute | solution.py:343
  7.8 13.9 %collective-permute-start = (bf16[512,128]{1,0:T(8,128)(2,1)}, bf16[512,128]{1,0:T(8,128)(2,1)S(1)}, u32[]{:S(2)}, u32[]{:S(2)}) collective-permute-start(bf16[512,128]{1,0:T(8,128)(2,1)} %param.6), channel_id=1, source_target_pairs={{0,0},{1,3},{2,2},{3,1},{4,4},{5,7},{6,6},{7,5},{8,8},{9,11},{10,1... | collective-permute-start | bytes 393224 | tf_op jit(solution)/shard_map/ppermute | solution.py:343
  9.4 16.3 %collective-permute-start.8 = (bf16[256,256]{1,0:T(8,128)(2,1)}, bf16[256,256]{1,0:T(8,128)(2,1)S(1)}, u32[]{:S(2)}, u32[]{:S(2)}) collective-permute-start(bf16[256,256]{1,0:T(8,128)(2,1)} %cot_ref.1), channel_id=1, source_target_pairs={{0,1},{1,0},{2,3},{3,2},{4,5},{5,4},{6,7},{7,6},{8,9},{9,8},{10,11... | collective-permute-start | bytes 393224 | tf_op jit(solution)/shard_map/ppermute | solution.py:343
  11.6 10.2 %collective-permute-start.4 = (bf16[1024,128]{1,0:T(8,128)(2,1)S(1)}, bf16[1024,128]{1,0:T(8,128)(2,1)S(1)}, u32[]{:S(2)}, u32[]{:S(2)}) collective-permute-start(bf16[1024,128]{1,0:T(8,128)(2,1)S(1)} %constant_dynamic-update-slice_fusion.refs_2_), channel_id=1, source_target_pairs={{0,4},{1,5},{2,6},{3,7},{4,0},{5,1},{6,2},{7,3},{8,12},{9,13},{10,... | collective-permute-start | bytes 786440 | tf_op jit(solution)/shard_map/ppermute | solution.py:343
  13.2 5.0 %collective-permute-start.5 = (bf16[512,128]{1,0:T(8,128)(2,1)S(1)}, bf16[512,128]{1,0:T(8,128)(2,1)S(1)}, u32[]{:S(2)}, u32[]{:S(2)}) collective-permute-start(bf16[512,128]{1,0:T(8,128)(2,1)S(1)} %collective-permute-done.2), channel_id=1, source_target_pairs={{0,8},{1,9},{2,10},{3,11},{4,12},{5,13},{6,14},{7,15},{8,0},{9,1},... | collective-permute-start | bytes 393224 | tf_op jit(solution)/shard_map/ppermute | solution.py:343
  18.2 5.0 %collective-permute-start.6 = (bf16[512,128]{1,0:T(8,128)(2,1)S(1)}, bf16[512,128]{1,0:T(8,128)(2,1)S(1)}, u32[]{:S(2)}, u32[]{:S(2)}) collective-permute-start(bf16[512,128]{1,0:T(8,128)(2,1)S(1)} %collective-permute-done.5.refs_4_), channel_id=1, source_target_pairs={{0,4},{1,5},{2,6},{3,7},{4,0},{5,1},{6,2},{7,3},{8,12},{9,13},{10,... | collective-permute-start | bytes 393224 | tf_op jit(solution)/shard_map/ppermute | solution.py:343
  21.7 6.9 %copy-start = (bf16[256,256]{1,0:T(8,128)(2,1)S(1)}, bf16[256,256]{1,0:T(8,128)(2,1)}, u32[]{:S(2)}) copy-start(bf16[256,256]{1,0:T(8,128)(2,1)} %cot_ref.1) | copy-start | bytes 393220
  21.7 6.9 %copy-start.1 = (bf16[128,256]{1,0:T(8,128)(2,1)S(1)}, bf16[128,256]{1,0:T(8,128)(2,1)}, u32[]{:S(2)}) copy-start(bf16[128,256]{1,0:T(8,128)(2,1)} %weight_ref.1) | copy-start | bytes 196612
  23.5 5.2 %collective-permute-start.7 = (bf16[512,128]{1,0:T(8,128)(2,1)S(1)}, bf16[512,128]{1,0:T(8,128)(2,1)S(1)}, u32[]{:S(2)}, u32[]{:S(2)}) collective-permute-start(bf16[512,128]{1,0:T(8,128)(2,1)S(1)} %aggregate.3.own_ref), channel_id=1, source_target_pairs={{0,1},{1,0},{2,3},{3,2},{4,5},{5,4},{6,7},{7,6},{8,9},{9,8},{10,11... | collective-permute-start | bytes 393224 | tf_op jit(solution)/shard_map/ppermute | solution.py:343
  29.5 7.3 %collective-permute-start.9 = (bf16[128,1024]{1,0:T(8,128)(2,1)S(1)}, bf16[128,1024]{1,0:T(8,128)(2,1)S(1)}, u32[]{:S(2)}, u32[]{:S(2)}) collective-permute-start(bf16[128,1024]{1,0:T(8,128)(2,1)S(1)} %get-tuple-element.24), channel_id=1, source_target_pairs={{0,3},{1,5},{2,6},{3,0},{4,7},{5,1},{6,2},{7,4},{8,11},{9,13},{10,... | collective-permute-start | bytes 786440 | tf_op jit(solution)/shard_map/ppermute | solution.py:343
  30.3 7.9 %collective-permute-start.14 = (bf16[128,1024]{1,0:T(8,128)(2,1)S(1)}, bf16[128,1024]{1,0:T(8,128)(2,1)S(1)}, u32[]{:S(2)}, u32[]{:S(2)}) collective-permute-start(bf16[128,1024]{1,0:T(8,128)(2,1)S(1)} %get-tuple-element.32), channel_id=1, source_target_pairs={{0,3},{1,5},{2,6},{3,0},{4,7},{5,1},{6,2},{7,4},{8,11},{9,13},{10,... | collective-permute-start | bytes 786440 | tf_op jit(solution)/shard_map/ppermute | solution.py:343
  32.1 4.8 %collective-permute-start.10 = (bf16[128,128]{1,0:T(8,128)(2,1)S(1)}, bf16[128,128]{1,0:T(8,128)(2,1)S(1)}, u32[]{:S(2)}, u32[]{:S(2)}) collective-permute-start(bf16[128,128]{1,0:T(8,128)(2,1)S(1)} %get-tuple-element.27.a_ref), channel_id=1, source_target_pairs={{0,16},{1,17},{2,18},{3,19},{4,20},{5,21},{6,22},{7,23},{8,24},{9,... | collective-permute-start | bytes 98312 | tf_op jit(solution)/shard_map/ppermute | solution.py:343
  36.9 5.0 %collective-permute-start.11 = (bf16[128,512]{1,0:T(8,128)(2,1)S(1)}, bf16[128,512]{1,0:T(8,128)(2,1)S(1)}, u32[]{:S(2)}, u32[]{:S(2)}) collective-permute-start(bf16[128,512]{1,0:T(8,128)(2,1)S(1)} %get-tuple-element.28), channel_id=1, source_target_pairs={{0,4},{1,2},{2,1},{3,7},{4,0},{5,6},{6,5},{7,3},{8,12},{9,10},{10,... | collective-permute-start | bytes 393224 | tf_op jit(solution)/shard_map/ppermute | solution.py:343
  38.3 7.3 %collective-permute-start.15 = (bf16[128,512]{1,0:T(8,128)(2,1)S(1)}, bf16[128,512]{1,0:T(8,128)(2,1)S(1)}, u32[]{:S(2)}, u32[]{:S(2)}) collective-permute-start(bf16[128,512]{1,0:T(8,128)(2,1)S(1)} %get-tuple-element.34), channel_id=1, source_target_pairs={{0,4},{1,2},{2,1},{3,7},{4,0},{5,6},{6,5},{7,3},{8,12},{9,10},{10,... | collective-permute-start | bytes 393224 | tf_op jit(solution)/shard_map/ppermute | solution.py:343
  39.4 6.1 %collective-permute-start.17 = (bf16[128,128]{1,0:T(8,128)(2,1)S(1)}, bf16[128,128]{1,0:T(8,128)(2,1)S(1)}, u32[]{:S(2)}, u32[]{:S(2)}) collective-permute-start(bf16[128,128]{1,0:T(8,128)(2,1)S(1)} %add.31.a_ref), channel_id=1, source_target_pairs={{0,8},{1,9},{2,10},{3,11},{4,12},{5,13},{6,14},{7,15},{8,0},{9,1},... | collective-permute-start | bytes 98312 | tf_op jit(solution)/shard_map/ppermute | solution.py:343
  42.0 8.2 %collective-permute-start.12 = (bf16[128,256]{1,0:T(8,128)(2,1)S(1)}, bf16[128,256]{1,0:T(8,128)(2,1)S(1)}, u32[]{:S(2)}, u32[]{:S(2)}) collective-permute-start(bf16[128,256]{1,0:T(8,128)(2,1)S(1)} %get-tuple-element.30), channel_id=1, source_target_pairs={{0,24},{1,25},{2,26},{3,27},{4,28},{5,29},{6,30},{7,31},{8,16},{9,... | collective-permute-start | bytes 196616 | tf_op jit(solution)/shard_map/ppermute | solution.py:343
  45.5 6.9 %collective-permute-start.13 = (bf16[128,256]{1,0:T(8,128)(2,1)S(1)}, bf16[128,256]{1,0:T(8,128)(2,1)S(1)}, u32[]{:S(2)}, u32[]{:S(2)}) collective-permute-start(bf16[128,256]{1,0:T(8,128)(2,1)S(1)} %get-tuple-element.31), channel_id=1, source_target_pairs={{0,16},{1,17},{2,18},{3,19},{4,20},{5,21},{6,22},{7,23},{8,24},{9,... | collective-permute-start | bytes 196616 | tf_op jit(solution)/shard_map/ppermute | solution.py:343
  45.5 3.4 %collective-permute-start.18 = (bf16[128,128]{1,0:T(8,128)(2,1)S(1)}, bf16[128,128]{1,0:T(8,128)(2,1)S(1)}, u32[]{:S(2)}, u32[]{:S(2)}) collective-permute-start(bf16[128,128]{1,0:T(8,128)(2,1)S(1)} %add.32.a_ref), channel_id=1, source_target_pairs={{0,3},{1,5},{2,6},{3,0},{4,7},{5,1},{6,2},{7,4},{8,11},{9,13},{10,... | collective-permute-start | bytes 98312 | tf_op jit(solution)/shard_map/ppermute | solution.py:343
  45.6 7.3 %collective-permute-start.16 = (bf16[128,256]{1,0:T(8,128)(2,1)S(1)}, bf16[128,256]{1,0:T(8,128)(2,1)S(1)}, u32[]{:S(2)}, u32[]{:S(2)}) collective-permute-start(bf16[128,256]{1,0:T(8,128)(2,1)S(1)} %get-tuple-element.37), channel_id=1, source_target_pairs={{0,8},{1,9},{2,10},{3,11},{4,12},{5,13},{6,14},{7,15},{8,0},{9,1},... | collective-permute-start | bytes 196616 | tf_op jit(solution)/shard_map/ppermute | solution.py:343
  48.9 4.0 %collective-permute-start.19 = (bf16[128,128]{1,0:T(8,128)(2,1)S(1)}, bf16[128,128]{1,0:T(8,128)(2,1)S(1)}, u32[]{:S(2)}, u32[]{:S(2)}) collective-permute-start(bf16[128,128]{1,0:T(8,128)(2,1)S(1)} %add.33.wg_ref), channel_id=1, source_target_pairs={{0,4},{1,2},{2,1},{3,7},{4,0},{5,6},{6,5},{7,3},{8,12},{9,10},{10,... | collective-permute-start | bytes 98312 | tf_op jit(solution)/shard_map/ppermute | solution.py:343
  53.0 1.4 %collective-permute-start.20 = (bf16[128,384]{1,0:T(8,128)(2,1)S(1)}, bf16[128,384]{1,0:T(8,128)(2,1)S(1)}, u32[]{:S(2)}, u32[]{:S(2)}) collective-permute-start(bf16[128,384]{1,0:T(8,128)(2,1)S(1)} %line_sum.1.own_ref), channel_id=1, source_target_pairs={{0,2},{1,3},{2,0},{3,1},{4,6},{5,7},{6,4},{7,5},{8,10},{9,11},{10,... | collective-permute-start | bytes 294920 | tf_op jit(solution)/shard_map/ppermute | solution.py:343

commit v7 on v6

--- a/solution.py
+++ b/solution.py
@@ -381,9 +381,9 @@
     sent_b, kept = rest_terms([chunk_b], back, dense)
     got_b = send(sent_b, lay.along(True))
     got_w1 = send(wg, lay.in_class(2 * near))
-    passed_a, kept_a, mark_a = first_sum(chunk_a, got_a, kept, got_w1)
+    passed_a, kept_a, mark_a = first_sum(chunk_a, got_a, kept, back)
     back_a = send(passed_a, lay.along(False))
-    passed_b, kept_b, mark_b = first_sum(chunk_b, got_b, kept, mark_a)
+    passed_b, kept_b, mark_b = first_sum(chunk_b, got_b, kept, got_w1)
     back_b = send(passed_b, lay.along(False))
     wg = add(wg, got_w1, mark_b)
     got_w2 = send(wg, lay.in_class(near))

time: 55.3 us -> 54.7 us (0.989)
  waiting for transfers between devices: 15.6 us -> 13.7 us
  starting transfers between devices: 30.2 us -> 31 us
  Pallas kernels: 6.9 us -> 7.5 us
    ppermute x21, waiting for transfers between devices: 15.6 us -> 13.7 us  [send(): return lax.ppermute(value, AXES, route)]
    ppermute x21, starting transfers between devices: 30.2 us -> 31 us  [send(): return lax.ppermute(value, AXES, route)]
    pallas_call x2, Pallas kernels: 0.09 us -> 0.7 us  [first_sum(): pl.pallas_call(functools.partial(first_sum_kernel, start, size), in_specs...]
  transfers between devices with their start and end apart: 21 -> 21, of which waited for: 12 -> 11; matrix products, arithmetic and copies ran while one was open for 3% -> 3% of each run, Pallas kernels for 9% -> 11%
where the time goes in v7:
time: 54.7 us; the launch traced here: 54.4 us
  starting transfers between devices  31 us (57%)
  waiting for transfers between devices  13.7 us (25%)
  Pallas kernels  7.5 us (14%)
  other arithmetic  0.86 us (2%)
  between operations  0.77 us (1%)
  local copies, waits for them, and re-layouts  0.69 us (1%)
    ppermute x21, starting transfers between devices, send(): return lax.ppermute(value, AXES, route)  31 us
    ppermute x21, waiting for transfers between devices, send(): return lax.ppermute(value, AXES, route)  13.7 us
    pallas_call x1, Pallas kernels, dense_blocks(): pl.pallas_call(functools.partial(dense_kernel, blocks, near, halves), in_...  2.98 us
    pallas_call x2, Pallas kernels, aggregate(): pl.pallas_call(functools.partial(aggregate_kernel, spans, len(given) - le...  1.42 us
  transfers between devices with their start and end apart: 21, of which 11 were waited for; matrix products, arithmetic and copies ran while one was open for 3% of the time, Pallas kernels for 11%

profile of v7, /device:TPU:0, one launch (start us, length us, event | category | flops | bytes accessed | tf_op | source)
XLA Modules:
  0.0 54.4 jit_solution(7846008773980814953)
XLA Ops:
  0.6 4.1 %collective-permute-start.2 = (bf16[512,128]{1,0:T(8,128)(2,1)}, bf16[512,128]{1,0:T(8,128)(2,1)S(1)}, u32[]{:S(2)}, u32[]{:S(2)}) collective-permute-start(bf16[512,128]{1,0:T(8,128)(2,1)} %param.6), channel_id=1, source_target_pairs={{0,16},{1,19},{2,18},{3,17},{4,20},{5,23},{6,22},{7,21},{8,24},{9,... | collective-permute-start | bytes 393224 | tf_op jit(solution)/shard_map/ppermute | solution.py:343
  4.7 1.6 %collective-permute-start.3 = (bf16[512,128]{1,0:T(8,128)(2,1)}, bf16[512,128]{1,0:T(8,128)(2,1)S(1)}, u32[]{:S(2)}, u32[]{:S(2)}) collective-permute-start(bf16[512,128]{1,0:T(8,128)(2,1)} %param.6), channel_id=1, source_target_pairs={{0,8},{1,11},{2,10},{3,9},{4,12},{5,15},{6,14},{7,13},{8,0},{9,3},... | collective-permute-start | bytes 393224 | tf_op jit(solution)/shard_map/ppermute | solution.py:343
  6.3 1.5 %collective-permute-start.1 = (bf16[512,128]{1,0:T(8,128)(2,1)}, bf16[512,128]{1,0:T(8,128)(2,1)S(1)}, u32[]{:S(2)}, u32[]{:S(2)}) collective-permute-start(bf16[512,128]{1,0:T(8,128)(2,1)} %param.6), channel_id=1, source_target_pairs={{0,4},{1,7},{2,6},{3,5},{4,0},{5,3},{6,2},{7,1},{8,12},{9,15},{10,... | collective-permute-start | bytes 393224 | tf_op jit(solution)/shard_map/ppermute | solution.py:343
  7.8 1.6 %collective-permute-start = (bf16[512,128]{1,0:T(8,128)(2,1)}, bf16[512,128]{1,0:T(8,128)(2,1)S(1)}, u32[]{:S(2)}, u32[]{:S(2)}) collective-permute-start(bf16[512,128]{1,0:T(8,128)(2,1)} %param.6), channel_id=1, source_target_pairs={{0,0},{1,3},{2,2},{3,1},{4,4},{5,7},{6,6},{7,5},{8,8},{9,11},{10,1... | collective-permute-start | bytes 393224 | tf_op jit(solution)/shard_map/ppermute | solution.py:343
  9.4 1.7 %collective-permute-start.8 = (bf16[256,256]{1,0:T(8,128)(2,1)}, bf16[256,256]{1,0:T(8,128)(2,1)S(1)}, u32[]{:S(2)}, u32[]{:S(2)}) collective-permute-start(bf16[256,256]{1,0:T(8,128)(2,1)} %cot_ref.1), channel_id=1, source_target_pairs={{0,1},{1,0},{2,3},{3,2},{4,5},{5,4},{6,7},{7,6},{8,9},{9,8},{10,11... | collective-permute-start | bytes 393224 | tf_op jit(solution)/shard_map/ppermute | solution.py:343
  11.1 0.2 collective-permute-done.2
  11.4 0.2 collective-permute-done.3
  11.6 1.6 %collective-permute-start.4 = (bf16[1024,128]{1,0:T(8,128)(2,1)S(1)}, bf16[1024,128]{1,0:T(8,128)(2,1)S(1)}, u32[]{:S(2)}, u32[]{:S(2)}) collective-permute-start(bf16[1024,128]{1,0:T(8,128)(2,1)S(1)} %constant_dynamic-update-slice_fusion.refs_2_), channel_id=1, source_target_pairs={{0,4},{1,5},{2,6},{3,7},{4,0},{5,1},{6,2},{7,3},{8,12},{9,13},{10,... | collective-permute-start | bytes 786440 | tf_op jit(solution)/shard_map/ppermute | solution.py:343
  13.2 1.4 %collective-permute-start.5 = (bf16[512,128]{1,0:T(8,128)(2,1)S(1)}, bf16[512,128]{1,0:T(8,128)(2,1)S(1)}, u32[]{:S(2)}, u32[]{:S(2)}) collective-permute-start(bf16[512,128]{1,0:T(8,128)(2,1)S(1)} %collective-permute-done.2), channel_id=1, source_target_pairs={{0,8},{1,9},{2,10},{3,11},{4,12},{5,13},{6,14},{7,15},{8,0},{9,1},... | collective-permute-start | bytes 393224 | tf_op jit(solution)/shard_map/ppermute | solution.py:343
  14.6 0.8 %bitcast_select_fusion = s32[8,12]{1,0:T(8,128)S(1)} fusion(s32[1,1,8,12]{3,2,1,0:T(8,128)} %param.9, s32[]{:T(128)S(6)} %mul.14, s32[8]{0:T(128)} %bitcast.5), kind=kLoop, calls=%fused_computation.13 | loop fusion | flops 288 | bytes 804 | tf_op jit(solution)/shard_map/jit(_where)/select_n | solution.py:353
  15.4 2.8 %collective-permute-done.5.refs_4_ = bf16[512,128]{1,0:T(8,128)(2,1)S(1)} collective-permute-done((bf16[512,128]{1,0:T(8,128)(2,1)S(1)}, bf16[512,128]{1,0:T(8,128)(2,1)S(1)}, u32[]{:S(2)}, u32[]{:S(2)}) %collective-permute-start.5) | collective-permute-done | bytes 131104 | tf_op jit(solution)/shard_map/ppermute | solution.py:343
  18.2 0.5 collective-permute-start.6
  18.7 0.1 pad_add_fusion.table
  18.7 3.0 %dense_blocks.1.dense_ref = bf16[4,512,1024]{2,1,0:T(8,128)(2,1)S(1)} custom-call(s32[8,13]{1,0:T(8,128)S(1)} %pad_add_fusion.table, bf16[8,12,128,128]{3,2,1,0:T(8,128)(2,1)} %bitcast.4), custom_call_target="tpu_custom_call" | custom-call | tf_op jit(solution)/shard_map/dense_blocks/pallas_call | solution.py:82
  21.7 0.0 copy-start
  21.7 0.0 copy-start.1
  21.7 0.0 collective-permute-done.1.refs_1_
  21.8 0.0 collective-permute-done.refs_0_
  21.8 1.1 %aggregate.2.refs_0_ = f32[512,128]{1,0:T(8,128)S(1)} custom-call(bf16[4,512,1024]{2,1,0:T(8,128)(2,1)S(1)} %dense_blocks.1.dense_ref, bf16[512,128]{1,0:T(8,128)(2,1)S(1)} %collective-permute-done.refs_0_, bf16[512,128]{1,0:T(8,128)(2,1)S(1)} %collective-permute-done.1.refs_1_, bf16[1024,128]{1,0:T(8,128)(2,1)S(1)} %constant_dynamic-update-slice_fusion.refs_2_, ...), custom_call_target="tpu_custom_call" | custom-call | tf_op jit(solution)/shard_map/aggregate/pallas_call | solution.py:118
  22.9 0.2 collective-permute-done.6.refs_1_
  23.1 0.3 aggregate.3.own_ref
  23.5 2.2 %collective-permute-start.7 = (bf16[512,128]{1,0:T(8,128)(2,1)S(1)}, bf16[512,128]{1,0:T(8,128)(2,1)S(1)}, u32[]{:S(2)}, u32[]{:S(2)}) collective-permute-start(bf16[512,128]{1,0:T(8,128)(2,1)S(1)} %aggregate.3.own_ref), channel_id=1, source_target_pairs={{0,1},{1,0},{2,3},{3,2},{4,5},{5,4},{6,7},{7,6},{8,9},{9,8},{10,11... | collective-permute-start | bytes 393224 | tf_op jit(solution)/shard_map/ppermute | solution.py:343
  25.7 0.0 collective-permute-done.8.far_cot_ref
  25.7 2.9 %collective-permute-done.7.other_ref = bf16[512,128]{1,0:T(8,128)(2,1)S(1)} collective-permute-done((bf16[512,128]{1,0:T(8,128)(2,1)S(1)}, bf16[512,128]{1,0:T(8,128)(2,1)S(1)}, u32[]{:S(2)}, u32[]{:S(2)}) %collective-permute-start.7) | collective-permute-done | bytes 131104 | tf_op jit(solution)/shard_map/ppermute | solution.py:343
  28.7 0.9 %turn.1 = (bf16[256,256]{1,0:T(8,128)(2,1)S(1)}, bf16[128,512]{1,0:T(8,128)(2,1)S(1)}, bf16[128,1024]{1,0:T(8,128)(2,1)S(1)}, bf16[128,128]{1,0:T(8,128)(2,1)S(1)}) custom-call(bf16[512,128]{1,0:T(8,128)(2,1)S(1)} %aggregate.3.own_ref, bf16[512,128]{1,0:T(8,128)(2,1)S(1)} %collective-permute-done.7.other_ref, bf16[128,256]{1,0:T(8,128)(2,1)S(1)} %copy-done.1, ...), custom_call_target="tpu_custom_call" | custom-call | tf_op jit(solution)/shard_map/turn/pallas_call | solution.py:157
  29.5 0.1 collective-permute-start.9
  29.6 0.7 %rest_terms.1 = (bf16[128,1024]{1,0:T(8,128)(2,1)S(1)}, f32[2,128,1024]{2,1,0:T(8,128)S(1)}) custom-call(bf16[128,512]{1,0:T(8,128)(2,1)S(1)} %get-tuple-element.24.back_ref.after_ref, bf16[4,512,1024]{2,1,0:T(8,128)(2,1)S(1)} %dense_blocks.1.dense_ref), custom_call_target="tpu_custom_call" | custom-call | tf_op jit(solution)/shard_map/rest_terms/pallas_call | solution.py:185
  30.3 1.8 %collective-permute-start.13 = (bf16[128,1024]{1,0:T(8,128)(2,1)S(1)}, bf16[128,1024]{1,0:T(8,128)(2,1)S(1)}, u32[]{:S(2)}, u32[]{:S(2)}) collective-permute-start(bf16[128,1024]{1,0:T(8,128)(2,1)S(1)} %get-tuple-element.30), channel_id=1, source_target_pairs={{0,3},{1,5},{2,6},{3,0},{4,7},{5,1},{6,2},{7,4},{8,11},{9,13},{10,... | collective-permute-start | bytes 786440 | tf_op jit(solution)/shard_map/ppermute | solution.py:343
  32.1 2.2 %collective-permute-start.14 = (bf16[128,128]{1,0:T(8,128)(2,1)S(1)}, bf16[128,128]{1,0:T(8,128)(2,1)S(1)}, u32[]{:S(2)}, u32[]{:S(2)}) collective-permute-start(bf16[128,128]{1,0:T(8,128)(2,1)S(1)} %get-tuple-element.31.a_ref), channel_id=1, source_target_pairs={{0,16},{1,17},{2,18},{3,19},{4,20},{5,21},{6,22},{7,23},{8,24},{9,... | collective-permute-start | bytes 98312 | tf_op jit(solution)/shard_map/ppermute | solution.py:343
  34.2 1.2 %collective-permute-done.9.got_ref = bf16[128,1024]{1,0:T(8,128)(2,1)S(1)} collective-permute-done((bf16[128,1024]{1,0:T(8,128)(2,1)S(1)}, bf16[128,1024]{1,0:T(8,128)(2,1)S(1)}, u32[]{:S(2)}, u32[]{:S(2)}) %collective-permute-start.9) | collective-permute-done | bytes 262176 | tf_op jit(solution)/shard_map/ppermute | solution.py:343
  35.4 0.6 %first_sum.2 = (bf16[128,512]{1,0:T(8,128)(2,1)S(1)}, f32[128,512]{1,0:T(8,128)S(1)}, bf16[16,128]{1,0:T(8,128)(2,1)}) custom-call(bf16[128,1024]{1,0:T(8,128)(2,1)S(1)} %collective-permute-done.9.got_ref, f32[2,128,1024]{2,1,0:T(8,128)S(1)} %get-tuple-element.25.kept_ref, bf16[128,512]{1,0:T(8,128)(2,1)S(1)} %get-tuple-element.24.back_ref.after_ref), custom_call_target="tpu_custom_call" | custom-call | tf_op jit(solution)/shard_map/first_sum/pallas_call | solution.py:209
  36.0 1.0 %collective-permute-start.10 = (bf16[128,512]{1,0:T(8,128)(2,1)S(1)}, bf16[128,512]{1,0:T(8,128)(2,1)S(1)}, u32[]{:S(2)}, u32[]{:S(2)}) collective-permute-start(bf16[128,512]{1,0:T(8,128)(2,1)S(1)} %get-tuple-element.26), channel_id=1, source_target_pairs={{0,4},{1,2},{2,1},{3,7},{4,0},{5,6},{6,5},{7,3},{8,12},{9,10},{10,... | collective-permute-start | bytes 393224 | tf_op jit(solution)/shard_map/ppermute | solution.py:343
  37.1 0.0 collective-permute-done.14.after_ref.b_ref
  37.1 1.2 %collective-permute-done.13.got_ref = bf16[128,1024]{1,0:T(8,128)(2,1)S(1)} collective-permute-done((bf16[128,1024]{1,0:T(8,128)(2,1)S(1)}, bf16[128,1024]{1,0:T(8,128)(2,1)S(1)}, u32[]{:S(2)}, u32[]{:S(2)}) %collective-permute-start.13) | collective-permute-done | bytes 262176 | tf_op jit(solution)/shard_map/ppermute | solution.py:343
  38.2 0.1 first_sum.3
  38.3 1.1 %collective-permute-start.15 = (bf16[128,512]{1,0:T(8,128)(2,1)S(1)}, bf16[128,512]{1,0:T(8,128)(2,1)S(1)}, u32[]{:S(2)}, u32[]{:S(2)}) collective-permute-start(bf16[128,512]{1,0:T(8,128)(2,1)S(1)} %get-tuple-element.32), channel_id=1, source_target_pairs={{0,4},{1,2},{2,1},{3,7},{4,0},{5,6},{6,5},{7,3},{8,12},{9,10},{10,... | collective-permute-start | bytes 393224 | tf_op jit(solution)/shard_map/ppermute | solution.py:343
  39.4 1.7 %collective-permute-start.17 = (bf16[128,128]{1,0:T(8,128)(2,1)S(1)}, bf16[128,128]{1,0:T(8,128)(2,1)S(1)}, u32[]{:S(2)}, u32[]{:S(2)}) collective-permute-start(bf16[128,128]{1,0:T(8,128)(2,1)S(1)} %add.31.a_ref), channel_id=1, source_target_pairs={{0,8},{1,9},{2,10},{3,11},{4,12},{5,13},{6,14},{7,15},{8,0},{9,1},... | collective-permute-start | bytes 98312 | tf_op jit(solution)/shard_map/ppermute | solution.py:343
  41.1 3.4 %collective-permute-start.11 = (bf16[128,256]{1,0:T(8,128)(2,1)S(1)}, bf16[128,256]{1,0:T(8,128)(2,1)S(1)}, u32[]{:S(2)}, u32[]{:S(2)}) collective-permute-start(bf16[128,256]{1,0:T(8,128)(2,1)S(1)} %get-tuple-element.28), channel_id=1, source_target_pairs={{0,24},{1,25},{2,26},{3,27},{4,28},{5,29},{6,30},{7,31},{8,16},{9,... | collective-permute-start | bytes 196616 | tf_op jit(solution)/shard_map/ppermute | solution.py:343
  44.5 0.7 %collective-permute-start.18 = (bf16[128,128]{1,0:T(8,128)(2,1)S(1)}, bf16[128,128]{1,0:T(8,128)(2,1)S(1)}, u32[]{:S(2)}, u32[]{:S(2)}) collective-permute-start(bf16[128,128]{1,0:T(8,128)(2,1)S(1)} %add.32.a_ref), channel_id=1, source_target_pairs={{0,3},{1,5},{2,6},{3,0},{4,7},{5,1},{6,2},{7,4},{8,11},{9,13},{10,... | collective-permute-start | bytes 98312 | tf_op jit(solution)/shard_map/ppermute | solution.py:343
  45.2 0.8 %collective-permute-start.16 = (bf16[128,256]{1,0:T(8,128)(2,1)S(1)}, bf16[128,256]{1,0:T(8,128)(2,1)S(1)}, u32[]{:S(2)}, u32[]{:S(2)}) collective-permute-start(bf16[128,256]{1,0:T(8,128)(2,1)S(1)} %get-tuple-element.35), channel_id=1, source_target_pairs={{0,8},{1,9},{2,10},{3,11},{4,12},{5,13},{6,14},{7,15},{8,0},{9,1},... | collective-permute-start | bytes 196616 | tf_op jit(solution)/shard_map/ppermute | solution.py:343
  46.0 1.9 %collective-permute-done.18.b_ref = bf16[128,128]{1,0:T(8,128)(2,1)S(1)} collective-permute-done((bf16[128,128]{1,0:T(8,128)(2,1)S(1)}, bf16[128,128]{1,0:T(8,128)(2,1)S(1)}, u32[]{:S(2)}, u32[]{:S(2)}) %collective-permute-start.18) | collective-permute-done | bytes 32800 | tf_op jit(solution)/shard_map/ppermute | solution.py:343
  47.9 1.2 %collective-permute-start.19 = (bf16[128,128]{1,0:T(8,128)(2,1)S(1)}, bf16[128,128]{1,0:T(8,128)(2,1)S(1)}, u32[]{:S(2)}, u32[]{:S(2)}) collective-permute-start(bf16[128,128]{1,0:T(8,128)(2,1)S(1)} %add.33.wg_ref), channel_id=1, source_target_pairs={{0,4},{1,2},{2,1},{3,7},{4,0},{5,6},{6,5},{7,3},{8,12},{9,10},{10,... | collective-permute-start | bytes 98312 | tf_op jit(solution)/shard_map/ppermute | solution.py:343
  49.1 2.6 %collective-permute-done.12.two_ref = bf16[128,256]{1,0:T(8,128)(2,1)S(1)} collective-permute-done((bf16[128,256]{1,0:T(8,128)(2,1)S(1)}, bf16[128,256]{1,0:T(8,128)(2,1)S(1)}, u32[]{:S(2)}, u32[]{:S(2)}) %collective-permute-start.12) | collective-permute-done | bytes 65568 | tf_op jit(solution)/shard_map/ppermute | solution.py:343
  51.7 0.2 collective-permute-done.19.got_wg_ref
  51.9 0.8 %collective-permute-start.20 = (bf16[128,384]{1,0:T(8,128)(2,1)S(1)}, bf16[128,384]{1,0:T(8,128)(2,1)S(1)}, u32[]{:S(2)}, u32[]{:S(2)}) collective-permute-start(bf16[128,384]{1,0:T(8,128)(2,1)S(1)} %line_sum.1.own_ref), channel_id=1, source_target_pairs={{0,2},{1,3},{2,0},{3,1},{4,6},{5,7},{6,4},{7,5},{8,10},{9,11},{10,... | collective-permute-start | bytes 294920 | tf_op jit(solution)/shard_map/ppermute | solution.py:343
  52.8 0.7 %copy.10 = bf16[256,256]{1,0:T(8,128)(2,1)} copy(bf16[256,256]{1,0:T(8,128)(2,1)S(1)} %get-tuple-element.41) | data formatting | bytes 262144
  53.4 0.3 collective-permute-done.20.got_ref
  53.7 0.7 %finish.1 = (bf16[256,128]{1,0:T(8,128)(2,1)}, f32[128,256]{1,0:T(8,128)}) custom-call(bf16[128,384]{1,0:T(8,128)(2,1)S(1)} %line_sum.1.own_ref, bf16[128,384]{1,0:T(8,128)(2,1)S(1)} %collective-permute-done.20.got_ref), custom_call_target="tpu_custom_call" | custom-call | tf_op jit(solution)/shard_map/finish/pallas_call | solution.py:291
  (18 shorter events, 0.2 us)
Async XLA Ops:
  0.6 10.7 %collective-permute-start.2 = (bf16[512,128]{1,0:T(8,128)(2,1)}, bf16[512,128]{1,0:T(8,128)(2,1)S(1)}, u32[]{:S(2)}, u32[]{:S(2)}) collective-permute-start(bf16[512,128]{1,0:T(8,128)(2,1)} %param.6), channel_id=1, source_target_pairs={{0,16},{1,19},{2,18},{3,17},{4,20},{5,23},{6,22},{7,21},{8,24},{9,... | collective-permute-start | bytes 393224 | tf_op jit(solution)/shard_map/ppermute | solution.py:343
  4.7 6.8 %collective-permute-start.3 = (bf16[512,128]{1,0:T(8,128)(2,1)}, bf16[512,128]{1,0:T(8,128)(2,1)S(1)}, u32[]{:S(2)}, u32[]{:S(2)}) collective-permute-start(bf16[512,128]{1,0:T(8,128)(2,1)} %param.6), channel_id=1, source_target_pairs={{0,8},{1,11},{2,10},{3,9},{4,12},{5,15},{6,14},{7,13},{8,0},{9,3},... | collective-permute-start | bytes 393224 | tf_op jit(solution)/shard_map/ppermute | solution.py:343
  6.3 15.4 %collective-permute-start.1 = (bf16[512,128]{1,0:T(8,128)(2,1)}, bf16[512,128]{1,0:T(8,128)(2,1)S(1)}, u32[]{:S(2)}, u32[]{:S(2)}) collective-permute-start(bf16[512,128]{1,0:T(8,128)(2,1)} %param.6), channel_id=1, source_target_pairs={{0,4},{1,7},{2,6},{3,5},{4,0},{5,3},{6,2},{7,1},{8,12},{9,15},{10,... | collective-permute-start | bytes 393224 | tf_op jit(solution)/shard_map/ppermute | solution.py:343
  7.8 13.9 %collective-permute-start = (bf16[512,128]{1,0:T(8,128)(2,1)}, bf16[512,128]{1,0:T(8,128)(2,1)S(1)}, u32[]{:S(2)}, u32[]{:S(2)}) collective-permute-start(bf16[512,128]{1,0:T(8,128)(2,1)} %param.6), channel_id=1, source_target_pairs={{0,0},{1,3},{2,2},{3,1},{4,4},{5,7},{6,6},{7,5},{8,8},{9,11},{10,1... | collective-permute-start | bytes 393224 | tf_op jit(solution)/shard_map/ppermute | solution.py:343
  9.4 16.3 %collective-permute-start.8 = (bf16[256,256]{1,0:T(8,128)(2,1)}, bf16[256,256]{1,0:T(8,128)(2,1)S(1)}, u32[]{:S(2)}, u32[]{:S(2)}) collective-permute-start(bf16[256,256]{1,0:T(8,128)(2,1)} %cot_ref.1), channel_id=1, source_target_pairs={{0,1},{1,0},{2,3},{3,2},{4,5},{5,4},{6,7},{7,6},{8,9},{9,8},{10,11... | collective-permute-start | bytes 393224 | tf_op jit(solution)/shard_map/ppermute | solution.py:343
  11.6 10.2 %collective-permute-start.4 = (bf16[1024,128]{1,0:T(8,128)(2,1)S(1)}, bf16[1024,128]{1,0:T(8,128)(2,1)S(1)}, u32[]{:S(2)}, u32[]{:S(2)}) collective-permute-start(bf16[1024,128]{1,0:T(8,128)(2,1)S(1)} %constant_dynamic-update-slice_fusion.refs_2_), channel_id=1, source_target_pairs={{0,4},{1,5},{2,6},{3,7},{4,0},{5,1},{6,2},{7,3},{8,12},{9,13},{10,... | collective-permute-start | bytes 786440 | tf_op jit(solution)/shard_map/ppermute | solution.py:343
  13.2 5.0 %collective-permute-start.5 = (bf16[512,128]{1,0:T(8,128)(2,1)S(1)}, bf16[512,128]{1,0:T(8,128)(2,1)S(1)}, u32[]{:S(2)}, u32[]{:S(2)}) collective-permute-start(bf16[512,128]{1,0:T(8,128)(2,1)S(1)} %collective-permute-done.2), channel_id=1, source_target_pairs={{0,8},{1,9},{2,10},{3,11},{4,12},{5,13},{6,14},{7,15},{8,0},{9,1},... | collective-permute-start | bytes 393224 | tf_op jit(solution)/shard_map/ppermute | solution.py:343
  18.2 5.0 %collective-permute-start.6 = (bf16[512,128]{1,0:T(8,128)(2,1)S(1)}, bf16[512,128]{1,0:T(8,128)(2,1)S(1)}, u32[]{:S(2)}, u32[]{:S(2)}) collective-permute-start(bf16[512,128]{1,0:T(8,128)(2,1)S(1)} %collective-permute-done.5.refs_4_), channel_id=1, source_target_pairs={{0,4},{1,5},{2,6},{3,7},{4,0},{5,1},{6,2},{7,3},{8,12},{9,13},{10,... | collective-permute-start | bytes 393224 | tf_op jit(solution)/shard_map/ppermute | solution.py:343
  21.7 6.9 %copy-start = (bf16[256,256]{1,0:T(8,128)(2,1)S(1)}, bf16[256,256]{1,0:T(8,128)(2,1)}, u32[]{:S(2)}) copy-start(bf16[256,256]{1,0:T(8,128)(2,1)} %cot_ref.1) | copy-start | bytes 393220
  21.7 6.9 %copy-start.1 = (bf16[128,256]{1,0:T(8,128)(2,1)S(1)}, bf16[128,256]{1,0:T(8,128)(2,1)}, u32[]{:S(2)}) copy-start(bf16[128,256]{1,0:T(8,128)(2,1)} %weight_ref.1) | copy-start | bytes 196612
  23.5 5.2 %collective-permute-start.7 = (bf16[512,128]{1,0:T(8,128)(2,1)S(1)}, bf16[512,128]{1,0:T(8,128)(2,1)S(1)}, u32[]{:S(2)}, u32[]{:S(2)}) collective-permute-start(bf16[512,128]{1,0:T(8,128)(2,1)S(1)} %aggregate.3.own_ref), channel_id=1, source_target_pairs={{0,1},{1,0},{2,3},{3,2},{4,5},{5,4},{6,7},{7,6},{8,9},{9,8},{10,11... | collective-permute-start | bytes 393224 | tf_op jit(solution)/shard_map/ppermute | solution.py:343
  29.5 5.9 %collective-permute-start.9 = (bf16[128,1024]{1,0:T(8,128)(2,1)S(1)}, bf16[128,1024]{1,0:T(8,128)(2,1)S(1)}, u32[]{:S(2)}, u32[]{:S(2)}) collective-permute-start(bf16[128,1024]{1,0:T(8,128)(2,1)S(1)} %get-tuple-element.23), channel_id=1, source_target_pairs={{0,3},{1,5},{2,6},{3,0},{4,7},{5,1},{6,2},{7,4},{8,11},{9,13},{10,... | collective-permute-start | bytes 786440 | tf_op jit(solution)/shard_map/ppermute | solution.py:343
  30.3 7.9 %collective-permute-start.13 = (bf16[128,1024]{1,0:T(8,128)(2,1)S(1)}, bf16[128,1024]{1,0:T(8,128)(2,1)S(1)}, u32[]{:S(2)}, u32[]{:S(2)}) collective-permute-start(bf16[128,1024]{1,0:T(8,128)(2,1)S(1)} %get-tuple-element.30), channel_id=1, source_target_pairs={{0,3},{1,5},{2,6},{3,0},{4,7},{5,1},{6,2},{7,4},{8,11},{9,13},{10,... | collective-permute-start | bytes 786440 | tf_op jit(solution)/shard_map/ppermute | solution.py:343
  32.1 5.0 %collective-permute-start.14 = (bf16[128,128]{1,0:T(8,128)(2,1)S(1)}, bf16[128,128]{1,0:T(8,128)(2,1)S(1)}, u32[]{:S(2)}, u32[]{:S(2)}) collective-permute-start(bf16[128,128]{1,0:T(8,128)(2,1)S(1)} %get-tuple-element.31.a_ref), channel_id=1, source_target_pairs={{0,16},{1,17},{2,18},{3,19},{4,20},{5,21},{6,22},{7,23},{8,24},{9,... | collective-permute-start | bytes 98312 | tf_op jit(solution)/shard_map/ppermute | solution.py:343
  36.0 5.0 %collective-permute-start.10 = (bf16[128,512]{1,0:T(8,128)(2,1)S(1)}, bf16[128,512]{1,0:T(8,128)(2,1)S(1)}, u32[]{:S(2)}, u32[]{:S(2)}) collective-permute-start(bf16[128,512]{1,0:T(8,128)(2,1)S(1)} %get-tuple-element.26), channel_id=1, source_target_pairs={{0,4},{1,2},{2,1},{3,7},{4,0},{5,6},{6,5},{7,3},{8,12},{9,10},{10,... | collective-permute-start | bytes 393224 | tf_op jit(solution)/shard_map/ppermute | solution.py:343
  38.3 6.9 %collective-permute-start.15 = (bf16[128,512]{1,0:T(8,128)(2,1)S(1)}, bf16[128,512]{1,0:T(8,128)(2,1)S(1)}, u32[]{:S(2)}, u32[]{:S(2)}) collective-permute-start(bf16[128,512]{1,0:T(8,128)(2,1)S(1)} %get-tuple-element.32), channel_id=1, source_target_pairs={{0,4},{1,2},{2,1},{3,7},{4,0},{5,6},{6,5},{7,3},{8,12},{9,10},{10,... | collective-permute-start | bytes 393224 | tf_op jit(solution)/shard_map/ppermute | solution.py:343
  39.4 5.1 %collective-permute-start.17 = (bf16[128,128]{1,0:T(8,128)(2,1)S(1)}, bf16[128,128]{1,0:T(8,128)(2,1)S(1)}, u32[]{:S(2)}, u32[]{:S(2)}) collective-permute-start(bf16[128,128]{1,0:T(8,128)(2,1)S(1)} %add.31.a_ref), channel_id=1, source_target_pairs={{0,8},{1,9},{2,10},{3,11},{4,12},{5,13},{6,14},{7,15},{8,0},{9,1},... | collective-permute-start | bytes 98312 | tf_op jit(solution)/shard_map/ppermute | solution.py:343
  41.1 8.1 %collective-permute-start.11 = (bf16[128,256]{1,0:T(8,128)(2,1)S(1)}, bf16[128,256]{1,0:T(8,128)(2,1)S(1)}, u32[]{:S(2)}, u32[]{:S(2)}) collective-permute-start(bf16[128,256]{1,0:T(8,128)(2,1)S(1)} %get-tuple-element.28), channel_id=1, source_target_pairs={{0,24},{1,25},{2,26},{3,27},{4,28},{5,29},{6,30},{7,31},{8,16},{9,... | collective-permute-start | bytes 196616 | tf_op jit(solution)/shard_map/ppermute | solution.py:343
  44.5 7.3 %collective-permute-start.12 = (bf16[128,256]{1,0:T(8,128)(2,1)S(1)}, bf16[128,256]{1,0:T(8,128)(2,1)S(1)}, u32[]{:S(2)}, u32[]{:S(2)}) collective-permute-start(bf16[128,256]{1,0:T(8,128)(2,1)S(1)} %get-tuple-element.29), channel_id=1, source_target_pairs={{0,16},{1,17},{2,18},{3,19},{4,20},{5,21},{6,22},{7,23},{8,24},{9,... | collective-permute-start | bytes 196616 | tf_op jit(solution)/shard_map/ppermute | solution.py:343
  44.5 3.4 %collective-permute-start.18 = (bf16[128,128]{1,0:T(8,128)(2,1)S(1)}, bf16[128,128]{1,0:T(8,128)(2,1)S(1)}, u32[]{:S(2)}, u32[]{:S(2)}) collective-permute-start(bf16[128,128]{1,0:T(8,128)(2,1)S(1)} %add.32.a_ref), channel_id=1, source_target_pairs={{0,3},{1,5},{2,6},{3,0},{4,7},{5,1},{6,2},{7,4},{8,11},{9,13},{10,... | collective-permute-start | bytes 98312 | tf_op jit(solution)/shard_map/ppermute | solution.py:343
  45.2 6.7 %collective-permute-start.16 = (bf16[128,256]{1,0:T(8,128)(2,1)S(1)}, bf16[128,256]{1,0:T(8,128)(2,1)S(1)}, u32[]{:S(2)}, u32[]{:S(2)}) collective-permute-start(bf16[128,256]{1,0:T(8,128)(2,1)S(1)} %get-tuple-element.35), channel_id=1, source_target_pairs={{0,8},{1,9},{2,10},{3,11},{4,12},{5,13},{6,14},{7,15},{8,0},{9,1},... | collective-permute-start | bytes 196616 | tf_op jit(solution)/shard_map/ppermute | solution.py:343
  47.9 4.0 %collective-permute-start.19 = (bf16[128,128]{1,0:T(8,128)(2,1)S(1)}, bf16[128,128]{1,0:T(8,128)(2,1)S(1)}, u32[]{:S(2)}, u32[]{:S(2)}) collective-permute-start(bf16[128,128]{1,0:T(8,128)(2,1)S(1)} %add.33.wg_ref), channel_id=1, source_target_pairs={{0,4},{1,2},{2,1},{3,7},{4,0},{5,6},{6,5},{7,3},{8,12},{9,10},{10,... | collective-permute-start | bytes 98312 | tf_op jit(solution)/shard_map/ppermute | solution.py:343
  51.9 1.8 %collective-permute-start.20 = (bf16[128,384]{1,0:T(8,128)(2,1)S(1)}, bf16[128,384]{1,0:T(8,128)(2,1)S(1)}, u32[]{:S(2)}, u32[]{:S(2)}) collective-permute-start(bf16[128,384]{1,0:T(8,128)(2,1)S(1)} %line_sum.1.own_ref), channel_id=1, source_target_pairs={{0,2},{1,3},{2,0},{3,1},{4,6},{5,7},{6,4},{7,5},{8,10},{9,11},{10,... | collective-permute-start | bytes 294920 | tf_op jit(solution)/shard_map/ppermute | solution.py:343

commit v8 on v7

--- a/solution.py
+++ b/solution.py
@@ -126,7 +126,7 @@
 
 
 def turn_kernel(share, chunk, own_ref, other_ref, weight_ref, cot_ref, far_cot_ref, dense_ref,
-                act_ref, back_ref, sent_ref, wg_ref, g_ref, grad_ref):
+                act_ref, back_ref, sent_ref, g_ref, grad_ref):
     rows = own_ref.shape[0]
     weight = weight_ref[...]
     for half, cot in enumerate((cot_ref, far_cot_ref)):
@@ -145,9 +145,6 @@
     for second in range(2):
         term = dot(back, dense_ref[unit_at(2 + second), :, pl.ds(start, size)])
         sent_ref[:, pl.ds(second * size, size)] = term.astype(jnp.bfloat16)
-    part = wg_ref.shape[1]
-    columns = pl.ds(pl.multiple_of(lane_of_class() * part, part), part)
-    wg_ref[...] = tn_dot(g_ref[...], grad_ref[:, columns]).astype(jnp.bfloat16)
 
 
 def turn(chunk, own, other, weight, cot, far_cot, dense):
@@ -157,40 +154,44 @@
     return pl.pallas_call(
         functools.partial(turn_kernel, share, chunk),
         in_specs=in_vmem(6),
-        out_specs=in_vmem(4),
+        out_specs=in_vmem(5),
         out_shape=[
             pltpu.VMEM((share, hid), bf),
             jax.ShapeDtypeStruct((width, rows), bf),
             jax.ShapeDtypeStruct((width, 2 * chunk[1]), bf),
-            jax.ShapeDtypeStruct((width, hid // 2), bf),
+            jax.ShapeDtypeStruct((rows, width), bf),
+            jax.ShapeDtypeStruct((rows, hid), bf),
         ],
-        scratch_shapes=[pltpu.VMEM((rows, width), bf), pltpu.VMEM((rows, hid), bf)],
         compiler_params=params(),
         name="turn",
     )(own, other, weight, cot, far_cot, held_in_vmem(dense))
 
 
-def rest_kernel(chunks, back_ref, dense_ref, *refs):
+def rest_kernel(chunks, back_ref, dense_ref, g_ref, grad_ref, wg_ref, *refs):
     back = back_ref[...]
     for (start, size), sent in zip(chunks, refs[:-1]):
         for second in range(2):
             term = dot(back, dense_ref[unit_at(2 + second), :, pl.ds(start, size)])
             sent[:, pl.ds(second * size, size)] = term.astype(jnp.bfloat16)
+    part = wg_ref.shape[1]
+    columns = pl.ds(pl.multiple_of(lane_of_class() * part, part), part)
+    wg_ref[...] = tn_dot(g_ref[...], grad_ref[:, columns]).astype(jnp.bfloat16)
     for second in range(2):
         refs[-1][second] = dot(back, dense_ref[unit_at(second)])
 
 
-def rest_terms(chunks, back, dense):
+def rest_terms(chunks, back, dense, g, grad):
     width, span = back.shape[0], dense.shape[2]
     return pl.pallas_call(
         functools.partial(rest_kernel, chunks),
-        in_specs=in_vmem(2),
-        out_specs=in_vmem(len(chunks) + 1),
-        out_shape=[jax.ShapeDtypeStruct((width, 2 * size), jnp.bfloat16) for _, size in chunks]
+        in_specs=in_vmem(4),
+        out_specs=in_vmem(len(chunks) + 2),
+        out_shape=[jax.ShapeDtypeStruct((width, grad.shape[1] // 2), jnp.bfloat16)]
+        + [jax.ShapeDtypeStruct((width, 2 * size), jnp.bfloat16) for _, size in chunks]
         + [jax.ShapeDtypeStruct((2, width, span), jnp.float32)],
         compiler_params=params(),
         name="rest_terms",
-    )(back, held_in_vmem(dense))
+    )(back, held_in_vmem(dense), g, grad)
 
 
 def first_sum_kernel(start, size, got_ref, kept_ref, after_ref, sent_ref, total_ref, mark_ref):
@@ -376,9 +377,9 @@
     partial = aggregate(dense, [(0, 2, 3 * share, 0, share)], [beside_three], partial, jnp.bfloat16)
     other = send(partial, lay.plain(0, 1))
     chunk_a, chunk_b = (2 * share, 2 * share), (0, 2 * share)
-    act, back, sent_a, wg = turn(chunk_a, partial, other, weight, cotangent, far_cot, dense)
+    act, back, sent_a, g, grad = turn(chunk_a, partial, other, weight, cotangent, far_cot, dense)
     got_a = send(sent_a, lay.along(True))
-    sent_b, kept = rest_terms([chunk_b], back, dense)
+    wg, sent_b, kept = rest_terms([chunk_b], back, dense, g, grad)
     got_b = send(sent_b, lay.along(True))
     got_w1 = send(wg, lay.in_class(2 * near))
     passed_a, kept_a, mark_a = first_sum(chunk_a, got_a, kept, back)

time: 54.7 us -> 54.6 us (level)
  no operation moved by 1% of the time
where the time goes in v8:
time: 54.6 us; the launch traced here: 54.4 us
  starting transfers between devices  31.1 us (57%)
  waiting for transfers between devices  13.5 us (25%)
  Pallas kernels  7.48 us (14%)
  other arithmetic  0.86 us (2%)
  between operations  0.76 us (1%)
  local copies, waits for them, and re-layouts  0.69 us (1%)
    ppermute x21, starting transfers between devices, send(): return lax.ppermute(value, AXES, route)  31.1 us
    ppermute x21, waiting for transfers between devices, send(): return lax.ppermute(value, AXES, route)  13.5 us
    pallas_call x1, Pallas kernels, dense_blocks(): pl.pallas_call(functools.partial(dense_kernel, blocks, near, halves), in_...  2.98 us
    pallas_call x2, Pallas kernels, aggregate(): pl.pallas_call(functools.partial(aggregate_kernel, spans, len(given) - le...  1.42 us
  transfers between devices with their start and end apart: 21, of which 11 were waited for; matrix products, arithmetic and copies ran while one was open for 3% of the time, Pallas kernels for 11%

profile of v8, /device:TPU:0, one launch (start us, length us, event | category | flops | bytes accessed | tf_op | source)
XLA Modules:
  0.0 54.4 jit_solution(2065406897738785149)
XLA Ops:
  0.6 4.1 %collective-permute-start.2 = (bf16[512,128]{1,0:T(8,128)(2,1)}, bf16[512,128]{1,0:T(8,128)(2,1)S(1)}, u32[]{:S(2)}, u32[]{:S(2)}) collective-permute-start(bf16[512,128]{1,0:T(8,128)(2,1)} %param.6), channel_id=1, source_target_pairs={{0,16},{1,19},{2,18},{3,17},{4,20},{5,23},{6,22},{7,21},{8,24},{9,... | collective-permute-start | bytes 393224 | tf_op jit(solution)/shard_map/ppermute | solution.py:344
  4.7 1.6 %collective-permute-start.3 = (bf16[512,128]{1,0:T(8,128)(2,1)}, bf16[512,128]{1,0:T(8,128)(2,1)S(1)}, u32[]{:S(2)}, u32[]{:S(2)}) collective-permute-start(bf16[512,128]{1,0:T(8,128)(2,1)} %param.6), channel_id=1, source_target_pairs={{0,8},{1,11},{2,10},{3,9},{4,12},{5,15},{6,14},{7,13},{8,0},{9,3},... | collective-permute-start | bytes 393224 | tf_op jit(solution)/shard_map/ppermute | solution.py:344
  6.3 1.6 %collective-permute-start = (bf16[512,128]{1,0:T(8,128)(2,1)}, bf16[512,128]{1,0:T(8,128)(2,1)S(1)}, u32[]{:S(2)}, u32[]{:S(2)}) collective-permute-start(bf16[512,128]{1,0:T(8,128)(2,1)} %param.6), channel_id=1, source_target_pairs={{0,0},{1,3},{2,2},{3,1},{4,4},{5,7},{6,6},{7,5},{8,8},{9,11},{10,1... | collective-permute-start | bytes 393224 | tf_op jit(solution)/shard_map/ppermute | solution.py:344
  7.9 1.5 %collective-permute-start.1 = (bf16[512,128]{1,0:T(8,128)(2,1)}, bf16[512,128]{1,0:T(8,128)(2,1)S(1)}, u32[]{:S(2)}, u32[]{:S(2)}) collective-permute-start(bf16[512,128]{1,0:T(8,128)(2,1)} %param.6), channel_id=1, source_target_pairs={{0,4},{1,7},{2,6},{3,5},{4,0},{5,3},{6,2},{7,1},{8,12},{9,15},{10,... | collective-permute-start | bytes 393224 | tf_op jit(solution)/shard_map/ppermute | solution.py:344
  9.4 1.7 %collective-permute-start.8 = (bf16[256,256]{1,0:T(8,128)(2,1)}, bf16[256,256]{1,0:T(8,128)(2,1)S(1)}, u32[]{:S(2)}, u32[]{:S(2)}) collective-permute-start(bf16[256,256]{1,0:T(8,128)(2,1)} %cot_ref.1), channel_id=1, source_target_pairs={{0,1},{1,0},{2,3},{3,2},{4,5},{5,4},{6,7},{7,6},{8,9},{9,8},{10,11... | collective-permute-start | bytes 393224 | tf_op jit(solution)/shard_map/ppermute | solution.py:344
  11.1 0.2 collective-permute-done.2
  11.4 0.2 collective-permute-done.3
  11.6 1.6 %collective-permute-start.4 = (bf16[1024,128]{1,0:T(8,128)(2,1)S(1)}, bf16[1024,128]{1,0:T(8,128)(2,1)S(1)}, u32[]{:S(2)}, u32[]{:S(2)}) collective-permute-start(bf16[1024,128]{1,0:T(8,128)(2,1)S(1)} %constant_dynamic-update-slice_fusion.refs_2_), channel_id=1, source_target_pairs={{0,4},{1,5},{2,6},{3,7},{4,0},{5,1},{6,2},{7,3},{8,12},{9,13},{10,... | collective-permute-start | bytes 786440 | tf_op jit(solution)/shard_map/ppermute | solution.py:344
  13.2 1.4 %collective-permute-start.5 = (bf16[512,128]{1,0:T(8,128)(2,1)S(1)}, bf16[512,128]{1,0:T(8,128)(2,1)S(1)}, u32[]{:S(2)}, u32[]{:S(2)}) collective-permute-start(bf16[512,128]{1,0:T(8,128)(2,1)S(1)} %collective-permute-done.2), channel_id=1, source_target_pairs={{0,8},{1,9},{2,10},{3,11},{4,12},{5,13},{6,14},{7,15},{8,0},{9,1},... | collective-permute-start | bytes 393224 | tf_op jit(solution)/shard_map/ppermute | solution.py:344
  14.6 0.8 %bitcast_select_fusion = s32[8,12]{1,0:T(8,128)S(1)} fusion(s32[1,1,8,12]{3,2,1,0:T(8,128)} %param.9, s32[]{:T(128)S(6)} %mul.14, s32[8]{0:T(128)} %bitcast.5), kind=kLoop, calls=%fused_computation.13 | loop fusion | flops 288 | bytes 804 | tf_op jit(solution)/shard_map/jit(_where)/select_n | solution.py:354
  15.4 2.8 %collective-permute-done.5.refs_4_ = bf16[512,128]{1,0:T(8,128)(2,1)S(1)} collective-permute-done((bf16[512,128]{1,0:T(8,128)(2,1)S(1)}, bf16[512,128]{1,0:T(8,128)(2,1)S(1)}, u32[]{:S(2)}, u32[]{:S(2)}) %collective-permute-start.5) | collective-permute-done | bytes 131104 | tf_op jit(solution)/shard_map/ppermute | solution.py:344
  18.2 0.5 collective-permute-start.6
  18.7 0.1 pad_add_fusion.table
  18.7 3.0 %dense_blocks.1.dense_ref = bf16[4,512,1024]{2,1,0:T(8,128)(2,1)S(1)} custom-call(s32[8,13]{1,0:T(8,128)S(1)} %pad_add_fusion.table, bf16[8,12,128,128]{3,2,1,0:T(8,128)(2,1)} %bitcast.4), custom_call_target="tpu_custom_call" | custom-call | tf_op jit(solution)/shard_map/dense_blocks/pallas_call | solution.py:82
  21.7 0.0 copy-start
  21.7 0.0 copy-start.1
  21.8 0.0 collective-permute-done.4.refs_3_
  21.8 1.1 %aggregate.2.refs_0_ = f32[512,128]{1,0:T(8,128)S(1)} custom-call(bf16[4,512,1024]{2,1,0:T(8,128)(2,1)S(1)} %dense_blocks.1.dense_ref, bf16[512,128]{1,0:T(8,128)(2,1)S(1)} %collective-permute-done.refs_0_, bf16[512,128]{1,0:T(8,128)(2,1)S(1)} %collective-permute-done.1.refs_1_, bf16[1024,128]{1,0:T(8,128)(2,1)S(1)} %constant_dynamic-update-slice_fusion.refs_2_, ...), custom_call_target="tpu_custom_call" | custom-call | tf_op jit(solution)/shard_map/aggregate/pallas_call | solution.py:118
  22.9 0.2 collective-permute-done.6.refs_1_
  23.1 0.3 aggregate.3.own_ref
  23.5 2.2 %collective-permute-start.7 = (bf16[512,128]{1,0:T(8,128)(2,1)S(1)}, bf16[512,128]{1,0:T(8,128)(2,1)S(1)}, u32[]{:S(2)}, u32[]{:S(2)}) collective-permute-start(bf16[512,128]{1,0:T(8,128)(2,1)S(1)} %aggregate.3.own_ref), channel_id=1, source_target_pairs={{0,1},{1,0},{2,3},{3,2},{4,5},{5,4},{6,7},{7,6},{8,9},{9,8},{10,11... | collective-permute-start | bytes 393224 | tf_op jit(solution)/shard_map/ppermute | solution.py:344
  25.7 0.0 collective-permute-done.8.far_cot_ref
  25.7 2.9 %collective-permute-done.7.other_ref = bf16[512,128]{1,0:T(8,128)(2,1)S(1)} collective-permute-done((bf16[512,128]{1,0:T(8,128)(2,1)S(1)}, bf16[512,128]{1,0:T(8,128)(2,1)S(1)}, u32[]{:S(2)}, u32[]{:S(2)}) %collective-permute-start.7) | collective-permute-done | bytes 131104 | tf_op jit(solution)/shard_map/ppermute | solution.py:344
  28.7 0.9 %turn.1 = (bf16[256,256]{1,0:T(8,128)(2,1)S(1)}, bf16[128,512]{1,0:T(8,128)(2,1)S(1)}, bf16[128,1024]{1,0:T(8,128)(2,1)S(1)}, bf16[512,128]{1,0:T(8,128)(2,1)S(1)}, bf16[512,256]{1,0:T(8,128)(2,1)S(1)}) custom-call(bf16[512,128]{1,0:T(8,128)(2,1)S(1)} %aggregate.3.own_ref, bf16[512,128]{1,0:T(8,128)(2,1)S(1)} %collective-permute-done.7.other_ref, ...), custom_call_target="tpu_custom_call" | custom-call | tf_op jit(solution)/shard_map/turn/pallas_call | solution.py:154
  29.5 0.1 collective-permute-start.9
  29.6 0.7 %rest_terms.1 = (bf16[128,128]{1,0:T(8,128)(2,1)S(1)}, bf16[128,1024]{1,0:T(8,128)(2,1)S(1)}, f32[2,128,1024]{2,1,0:T(8,128)S(1)}) custom-call(bf16[128,512]{1,0:T(8,128)(2,1)S(1)} %get-tuple-element.26.back_ref.after_ref, bf16[4,512,1024]{2,1,0:T(8,128)(2,1)S(1)} %dense_blocks.1.dense_ref, bf16[512,128]{1,0:T(8,128)(2,1)S(1)} %get-tuple-element.27.g_ref, ...), custom_call_target="tpu_custom_call" | custom-call | tf_op jit(solution)/shard_map/rest_terms/pallas_call | solution.py:185
  30.3 1.8 %collective-permute-start.13 = (bf16[128,1024]{1,0:T(8,128)(2,1)S(1)}, bf16[128,1024]{1,0:T(8,128)(2,1)S(1)}, u32[]{:S(2)}, u32[]{:S(2)}) collective-permute-start(bf16[128,1024]{1,0:T(8,128)(2,1)S(1)} %get-tuple-element.34), channel_id=1, source_target_pairs={{0,3},{1,5},{2,6},{3,0},{4,7},{5,1},{6,2},{7,4},{8,11},{9,13},{10,... | collective-permute-start | bytes 786440 | tf_op jit(solution)/shard_map/ppermute | solution.py:344
  32.0 2.2 %collective-permute-start.14 = (bf16[128,128]{1,0:T(8,128)(2,1)S(1)}, bf16[128,128]{1,0:T(8,128)(2,1)S(1)}, u32[]{:S(2)}, u32[]{:S(2)}) collective-permute-start(bf16[128,128]{1,0:T(8,128)(2,1)S(1)} %get-tuple-element.35.a_ref), channel_id=1, source_target_pairs={{0,16},{1,17},{2,18},{3,19},{4,20},{5,21},{6,22},{7,23},{8,24},{9,... | collective-permute-start | bytes 98312 | tf_op jit(solution)/shard_map/ppermute | solution.py:344
  34.2 1.2 %collective-permute-done.9.got_ref = bf16[128,1024]{1,0:T(8,128)(2,1)S(1)} collective-permute-done((bf16[128,1024]{1,0:T(8,128)(2,1)S(1)}, bf16[128,1024]{1,0:T(8,128)(2,1)S(1)}, u32[]{:S(2)}, u32[]{:S(2)}) %collective-permute-start.9) | collective-permute-done | bytes 262176 | tf_op jit(solution)/shard_map/ppermute | solution.py:344
  35.4 0.6 %first_sum.2 = (bf16[128,512]{1,0:T(8,128)(2,1)S(1)}, f32[128,512]{1,0:T(8,128)S(1)}, bf16[16,128]{1,0:T(8,128)(2,1)}) custom-call(bf16[128,1024]{1,0:T(8,128)(2,1)S(1)} %collective-permute-done.9.got_ref, f32[2,128,1024]{2,1,0:T(8,128)S(1)} %get-tuple-element.29.kept_ref, bf16[128,512]{1,0:T(8,128)(2,1)S(1)} %get-tuple-element.26.back_ref.after_ref), custom_call_target="tpu_custom_call" | custom-call | tf_op jit(solution)/shard_map/first_sum/pallas_call | solution.py:210
  36.0 1.1 %collective-permute-start.10 = (bf16[128,512]{1,0:T(8,128)(2,1)S(1)}, bf16[128,512]{1,0:T(8,128)(2,1)S(1)}, u32[]{:S(2)}, u32[]{:S(2)}) collective-permute-start(bf16[128,512]{1,0:T(8,128)(2,1)S(1)} %get-tuple-element.30), channel_id=1, source_target_pairs={{0,4},{1,2},{2,1},{3,7},{4,0},{5,6},{6,5},{7,3},{8,12},{9,10},{10,... | collective-permute-start | bytes 393224 | tf_op jit(solution)/shard_map/ppermute | solution.py:344
  37.1 0.0 collective-permute-done.14.after_ref.b_ref
  37.1 1.1 %collective-permute-done.13.got_ref = bf16[128,1024]{1,0:T(8,128)(2,1)S(1)} collective-permute-done((bf16[128,1024]{1,0:T(8,128)(2,1)S(1)}, bf16[128,1024]{1,0:T(8,128)(2,1)S(1)}, u32[]{:S(2)}, u32[]{:S(2)}) %collective-permute-start.13) | collective-permute-done | bytes 262176 | tf_op jit(solution)/shard_map/ppermute | solution.py:344
  38.2 0.1 first_sum.3
  38.2 1.2 %collective-permute-start.15 = (bf16[128,512]{1,0:T(8,128)(2,1)S(1)}, bf16[128,512]{1,0:T(8,128)(2,1)S(1)}, u32[]{:S(2)}, u32[]{:S(2)}) collective-permute-start(bf16[128,512]{1,0:T(8,128)(2,1)S(1)} %get-tuple-element.36), channel_id=1, source_target_pairs={{0,4},{1,2},{2,1},{3,7},{4,0},{5,6},{6,5},{7,3},{8,12},{9,10},{10,... | collective-permute-start | bytes 393224 | tf_op jit(solution)/shard_map/ppermute | solution.py:344
  39.4 1.6 %collective-permute-start.17 = (bf16[128,128]{1,0:T(8,128)(2,1)S(1)}, bf16[128,128]{1,0:T(8,128)(2,1)S(1)}, u32[]{:S(2)}, u32[]{:S(2)}) collective-permute-start(bf16[128,128]{1,0:T(8,128)(2,1)S(1)} %add.31.a_ref), channel_id=1, source_target_pairs={{0,8},{1,9},{2,10},{3,11},{4,12},{5,13},{6,14},{7,15},{8,0},{9,1},... | collective-permute-start | bytes 98312 | tf_op jit(solution)/shard_map/ppermute | solution.py:344
  41.1 0.0 collective-permute-done.10.got_ref
  41.1 3.3 %collective-permute-start.11 = (bf16[128,256]{1,0:T(8,128)(2,1)S(1)}, bf16[128,256]{1,0:T(8,128)(2,1)S(1)}, u32[]{:S(2)}, u32[]{:S(2)}) collective-permute-start(bf16[128,256]{1,0:T(8,128)(2,1)S(1)} %get-tuple-element.32), channel_id=1, source_target_pairs={{0,24},{1,25},{2,26},{3,27},{4,28},{5,29},{6,30},{7,31},{8,16},{9,... | collective-permute-start | bytes 196616 | tf_op jit(solution)/shard_map/ppermute | solution.py:344
  44.4 0.7 %collective-permute-start.18 = (bf16[128,128]{1,0:T(8,128)(2,1)S(1)}, bf16[128,128]{1,0:T(8,128)(2,1)S(1)}, u32[]{:S(2)}, u32[]{:S(2)}) collective-permute-start(bf16[128,128]{1,0:T(8,128)(2,1)S(1)} %add.32.a_ref), channel_id=1, source_target_pairs={{0,3},{1,5},{2,6},{3,0},{4,7},{5,1},{6,2},{7,4},{8,11},{9,13},{10,... | collective-permute-start | bytes 98312 | tf_op jit(solution)/shard_map/ppermute | solution.py:344
  45.2 0.8 %collective-permute-start.16 = (bf16[128,256]{1,0:T(8,128)(2,1)S(1)}, bf16[128,256]{1,0:T(8,128)(2,1)S(1)}, u32[]{:S(2)}, u32[]{:S(2)}) collective-permute-start(bf16[128,256]{1,0:T(8,128)(2,1)S(1)} %get-tuple-element.39), channel_id=1, source_target_pairs={{0,8},{1,9},{2,10},{3,11},{4,12},{5,13},{6,14},{7,15},{8,0},{9,1},... | collective-permute-start | bytes 196616 | tf_op jit(solution)/shard_map/ppermute | solution.py:344
  46.0 1.9 %collective-permute-done.18.b_ref = bf16[128,128]{1,0:T(8,128)(2,1)S(1)} collective-permute-done((bf16[128,128]{1,0:T(8,128)(2,1)S(1)}, bf16[128,128]{1,0:T(8,128)(2,1)S(1)}, u32[]{:S(2)}, u32[]{:S(2)}) %collective-permute-start.18) | collective-permute-done | bytes 32800 | tf_op jit(solution)/shard_map/ppermute | solution.py:344
  47.9 1.3 %collective-permute-start.19 = (bf16[128,128]{1,0:T(8,128)(2,1)S(1)}, bf16[128,128]{1,0:T(8,128)(2,1)S(1)}, u32[]{:S(2)}, u32[]{:S(2)}) collective-permute-start(bf16[128,128]{1,0:T(8,128)(2,1)S(1)} %add.33.wg_ref), channel_id=1, source_target_pairs={{0,4},{1,2},{2,1},{3,7},{4,0},{5,6},{6,5},{7,3},{8,12},{9,10},{10,... | collective-permute-start | bytes 98312 | tf_op jit(solution)/shard_map/ppermute | solution.py:344
  49.1 2.6 %collective-permute-done.12.two_ref = bf16[128,256]{1,0:T(8,128)(2,1)S(1)} collective-permute-done((bf16[128,256]{1,0:T(8,128)(2,1)S(1)}, bf16[128,256]{1,0:T(8,128)(2,1)S(1)}, u32[]{:S(2)}, u32[]{:S(2)}) %collective-permute-start.12) | collective-permute-done | bytes 65568 | tf_op jit(solution)/shard_map/ppermute | solution.py:344
  51.8 0.1 collective-permute-done.19.got_wg_ref
  51.9 0.8 %collective-permute-start.20 = (bf16[128,384]{1,0:T(8,128)(2,1)S(1)}, bf16[128,384]{1,0:T(8,128)(2,1)S(1)}, u32[]{:S(2)}, u32[]{:S(2)}) collective-permute-start(bf16[128,384]{1,0:T(8,128)(2,1)S(1)} %line_sum.1.own_ref), channel_id=1, source_target_pairs={{0,2},{1,3},{2,0},{3,1},{4,6},{5,7},{6,4},{7,5},{8,10},{9,11},{10,... | collective-permute-start | bytes 294920 | tf_op jit(solution)/shard_map/ppermute | solution.py:344
  52.7 0.7 %copy.10 = bf16[256,256]{1,0:T(8,128)(2,1)} copy(bf16[256,256]{1,0:T(8,128)(2,1)S(1)} %get-tuple-element.45) | data formatting | bytes 262144
  53.4 0.3 collective-permute-done.20.got_ref
  53.7 0.7 %finish.1 = (bf16[256,128]{1,0:T(8,128)(2,1)}, f32[128,256]{1,0:T(8,128)}) custom-call(bf16[128,384]{1,0:T(8,128)(2,1)S(1)} %line_sum.1.own_ref, bf16[128,384]{1,0:T(8,128)(2,1)S(1)} %collective-permute-done.20.got_ref), custom_call_target="tpu_custom_call" | custom-call | tf_op jit(solution)/shard_map/finish/pallas_call | solution.py:292
  (18 shorter events, 0.2 us)
Async XLA Ops:
  0.6 10.7 %collective-permute-start.2 = (bf16[512,128]{1,0:T(8,128)(2,1)}, bf16[512,128]{1,0:T(8,128)(2,1)S(1)}, u32[]{:S(2)}, u32[]{:S(2)}) collective-permute-start(bf16[512,128]{1,0:T(8,128)(2,1)} %param.6), channel_id=1, source_target_pairs={{0,16},{1,19},{2,18},{3,17},{4,20},{5,23},{6,22},{7,21},{8,24},{9,... | collective-permute-start | bytes 393224 | tf_op jit(solution)/shard_map/ppermute | solution.py:344
  4.7 6.8 %collective-permute-start.3 = (bf16[512,128]{1,0:T(8,128)(2,1)}, bf16[512,128]{1,0:T(8,128)(2,1)S(1)}, u32[]{:S(2)}, u32[]{:S(2)}) collective-permute-start(bf16[512,128]{1,0:T(8,128)(2,1)} %param.6), channel_id=1, source_target_pairs={{0,8},{1,11},{2,10},{3,9},{4,12},{5,15},{6,14},{7,13},{8,0},{9,3},... | collective-permute-start | bytes 393224 | tf_op jit(solution)/shard_map/ppermute | solution.py:344
  6.3 15.4 %collective-permute-start = (bf16[512,128]{1,0:T(8,128)(2,1)}, bf16[512,128]{1,0:T(8,128)(2,1)S(1)}, u32[]{:S(2)}, u32[]{:S(2)}) collective-permute-start(bf16[512,128]{1,0:T(8,128)(2,1)} %param.6), channel_id=1, source_target_pairs={{0,0},{1,3},{2,2},{3,1},{4,4},{5,7},{6,6},{7,5},{8,8},{9,11},{10,1... | collective-permute-start | bytes 393224 | tf_op jit(solution)/shard_map/ppermute | solution.py:344
  7.9 13.9 %collective-permute-start.1 = (bf16[512,128]{1,0:T(8,128)(2,1)}, bf16[512,128]{1,0:T(8,128)(2,1)S(1)}, u32[]{:S(2)}, u32[]{:S(2)}) collective-permute-start(bf16[512,128]{1,0:T(8,128)(2,1)} %param.6), channel_id=1, source_target_pairs={{0,4},{1,7},{2,6},{3,5},{4,0},{5,3},{6,2},{7,1},{8,12},{9,15},{10,... | collective-permute-start | bytes 393224 | tf_op jit(solution)/shard_map/ppermute | solution.py:344
  9.4 16.3 %collective-permute-start.8 = (bf16[256,256]{1,0:T(8,128)(2,1)}, bf16[256,256]{1,0:T(8,128)(2,1)S(1)}, u32[]{:S(2)}, u32[]{:S(2)}) collective-permute-start(bf16[256,256]{1,0:T(8,128)(2,1)} %cot_ref.1), channel_id=1, source_target_pairs={{0,1},{1,0},{2,3},{3,2},{4,5},{5,4},{6,7},{7,6},{8,9},{9,8},{10,11... | collective-permute-start | bytes 393224 | tf_op jit(solution)/shard_map/ppermute | solution.py:344
  11.6 10.2 %collective-permute-start.4 = (bf16[1024,128]{1,0:T(8,128)(2,1)S(1)}, bf16[1024,128]{1,0:T(8,128)(2,1)S(1)}, u32[]{:S(2)}, u32[]{:S(2)}) collective-permute-start(bf16[1024,128]{1,0:T(8,128)(2,1)S(1)} %constant_dynamic-update-slice_fusion.refs_2_), channel_id=1, source_target_pairs={{0,4},{1,5},{2,6},{3,7},{4,0},{5,1},{6,2},{7,3},{8,12},{9,13},{10,... | collective-permute-start | bytes 786440 | tf_op jit(solution)/shard_map/ppermute | solution.py:344
  13.2 5.0 %collective-permute-start.5 = (bf16[512,128]{1,0:T(8,128)(2,1)S(1)}, bf16[512,128]{1,0:T(8,128)(2,1)S(1)}, u32[]{:S(2)}, u32[]{:S(2)}) collective-permute-start(bf16[512,128]{1,0:T(8,128)(2,1)S(1)} %collective-permute-done.2), channel_id=1, source_target_pairs={{0,8},{1,9},{2,10},{3,11},{4,12},{5,13},{6,14},{7,15},{8,0},{9,1},... | collective-permute-start | bytes 393224 | tf_op jit(solution)/shard_map/ppermute | solution.py:344
  18.2 5.0 %collective-permute-start.6 = (bf16[512,128]{1,0:T(8,128)(2,1)S(1)}, bf16[512,128]{1,0:T(8,128)(2,1)S(1)}, u32[]{:S(2)}, u32[]{:S(2)}) collective-permute-start(bf16[512,128]{1,0:T(8,128)(2,1)S(1)} %collective-permute-done.5.refs_4_), channel_id=1, source_target_pairs={{0,4},{1,5},{2,6},{3,7},{4,0},{5,1},{6,2},{7,3},{8,12},{9,13},{10,... | collective-permute-start | bytes 393224 | tf_op jit(solution)/shard_map/ppermute | solution.py:344
  21.7 6.9 %copy-start = (bf16[256,256]{1,0:T(8,128)(2,1)S(1)}, bf16[256,256]{1,0:T(8,128)(2,1)}, u32[]{:S(2)}) copy-start(bf16[256,256]{1,0:T(8,128)(2,1)} %cot_ref.1) | copy-start | bytes 393220
  21.7 6.9 %copy-start.1 = (bf16[128,256]{1,0:T(8,128)(2,1)S(1)}, bf16[128,256]{1,0:T(8,128)(2,1)}, u32[]{:S(2)}) copy-start(bf16[128,256]{1,0:T(8,128)(2,1)} %weight_ref.1) | copy-start | bytes 196612
  23.5 5.2 %collective-permute-start.7 = (bf16[512,128]{1,0:T(8,128)(2,1)S(1)}, bf16[512,128]{1,0:T(8,128)(2,1)S(1)}, u32[]{:S(2)}, u32[]{:S(2)}) collective-permute-start(bf16[512,128]{1,0:T(8,128)(2,1)S(1)} %aggregate.3.own_ref), channel_id=1, source_target_pairs={{0,1},{1,0},{2,3},{3,2},{4,5},{5,4},{6,7},{7,6},{8,9},{9,8},{10,11... | collective-permute-start | bytes 393224 | tf_op jit(solution)/shard_map/ppermute | solution.py:344
  29.5 5.9 %collective-permute-start.9 = (bf16[128,1024]{1,0:T(8,128)(2,1)S(1)}, bf16[128,1024]{1,0:T(8,128)(2,1)S(1)}, u32[]{:S(2)}, u32[]{:S(2)}) collective-permute-start(bf16[128,1024]{1,0:T(8,128)(2,1)S(1)} %get-tuple-element.25), channel_id=1, source_target_pairs={{0,3},{1,5},{2,6},{3,0},{4,7},{5,1},{6,2},{7,4},{8,11},{9,13},{10,... | collective-permute-start | bytes 786440 | tf_op jit(solution)/shard_map/ppermute | solution.py:344
  30.3 7.9 %collective-permute-start.13 = (bf16[128,1024]{1,0:T(8,128)(2,1)S(1)}, bf16[128,1024]{1,0:T(8,128)(2,1)S(1)}, u32[]{:S(2)}, u32[]{:S(2)}) collective-permute-start(bf16[128,1024]{1,0:T(8,128)(2,1)S(1)} %get-tuple-element.34), channel_id=1, source_target_pairs={{0,3},{1,5},{2,6},{3,0},{4,7},{5,1},{6,2},{7,4},{8,11},{9,13},{10,... | collective-permute-start | bytes 786440 | tf_op jit(solution)/shard_map/ppermute | solution.py:344
  32.0 5.1 %collective-permute-start.14 = (bf16[128,128]{1,0:T(8,128)(2,1)S(1)}, bf16[128,128]{1,0:T(8,128)(2,1)S(1)}, u32[]{:S(2)}, u32[]{:S(2)}) collective-permute-start(bf16[128,128]{1,0:T(8,128)(2,1)S(1)} %get-tuple-element.35.a_ref), channel_id=1, source_target_pairs={{0,16},{1,17},{2,18},{3,19},{4,20},{5,21},{6,22},{7,23},{8,24},{9,... | collective-permute-start | bytes 98312 | tf_op jit(solution)/shard_map/ppermute | solution.py:344
  36.0 5.1 %collective-permute-start.10 = (bf16[128,512]{1,0:T(8,128)(2,1)S(1)}, bf16[128,512]{1,0:T(8,128)(2,1)S(1)}, u32[]{:S(2)}, u32[]{:S(2)}) collective-permute-start(bf16[128,512]{1,0:T(8,128)(2,1)S(1)} %get-tuple-element.30), channel_id=1, source_target_pairs={{0,4},{1,2},{2,1},{3,7},{4,0},{5,6},{6,5},{7,3},{8,12},{9,10},{10,... | collective-permute-start | bytes 393224 | tf_op jit(solution)/shard_map/ppermute | solution.py:344
  38.2 6.9 %collective-permute-start.15 = (bf16[128,512]{1,0:T(8,128)(2,1)S(1)}, bf16[128,512]{1,0:T(8,128)(2,1)S(1)}, u32[]{:S(2)}, u32[]{:S(2)}) collective-permute-start(bf16[128,512]{1,0:T(8,128)(2,1)S(1)} %get-tuple-element.36), channel_id=1, source_target_pairs={{0,4},{1,2},{2,1},{3,7},{4,0},{5,6},{6,5},{7,3},{8,12},{9,10},{10,... | collective-permute-start | bytes 393224 | tf_op jit(solution)/shard_map/ppermute | solution.py:344
  39.4 5.0 %collective-permute-start.17 = (bf16[128,128]{1,0:T(8,128)(2,1)S(1)}, bf16[128,128]{1,0:T(8,128)(2,1)S(1)}, u32[]{:S(2)}, u32[]{:S(2)}) collective-permute-start(bf16[128,128]{1,0:T(8,128)(2,1)S(1)} %add.31.a_ref), channel_id=1, source_target_pairs={{0,8},{1,9},{2,10},{3,11},{4,12},{5,13},{6,14},{7,15},{8,0},{9,1},... | collective-permute-start | bytes 98312 | tf_op jit(solution)/shard_map/ppermute | solution.py:344
  41.1 8.0 %collective-permute-start.11 = (bf16[128,256]{1,0:T(8,128)(2,1)S(1)}, bf16[128,256]{1,0:T(8,128)(2,1)S(1)}, u32[]{:S(2)}, u32[]{:S(2)}) collective-permute-start(bf16[128,256]{1,0:T(8,128)(2,1)S(1)} %get-tuple-element.32), channel_id=1, source_target_pairs={{0,24},{1,25},{2,26},{3,27},{4,28},{5,29},{6,30},{7,31},{8,16},{9,... | collective-permute-start | bytes 196616 | tf_op jit(solution)/shard_map/ppermute | solution.py:344
  44.4 7.3 %collective-permute-start.12 = (bf16[128,256]{1,0:T(8,128)(2,1)S(1)}, bf16[128,256]{1,0:T(8,128)(2,1)S(1)}, u32[]{:S(2)}, u32[]{:S(2)}) collective-permute-start(bf16[128,256]{1,0:T(8,128)(2,1)S(1)} %get-tuple-element.33), channel_id=1, source_target_pairs={{0,16},{1,17},{2,18},{3,19},{4,20},{5,21},{6,22},{7,23},{8,24},{9,... | collective-permute-start | bytes 196616 | tf_op jit(solution)/shard_map/ppermute | solution.py:344
  44.4 3.4 %collective-permute-start.18 = (bf16[128,128]{1,0:T(8,128)(2,1)S(1)}, bf16[128,128]{1,0:T(8,128)(2,1)S(1)}, u32[]{:S(2)}, u32[]{:S(2)}) collective-permute-start(bf16[128,128]{1,0:T(8,128)(2,1)S(1)} %add.32.a_ref), channel_id=1, source_target_pairs={{0,3},{1,5},{2,6},{3,0},{4,7},{5,1},{6,2},{7,4},{8,11},{9,13},{10,... | collective-permute-start | bytes 98312 | tf_op jit(solution)/shard_map/ppermute | solution.py:344
  45.2 6.6 %collective-permute-start.16 = (bf16[128,256]{1,0:T(8,128)(2,1)S(1)}, bf16[128,256]{1,0:T(8,128)(2,1)S(1)}, u32[]{:S(2)}, u32[]{:S(2)}) collective-permute-start(bf16[128,256]{1,0:T(8,128)(2,1)S(1)} %get-tuple-element.39), channel_id=1, source_target_pairs={{0,8},{1,9},{2,10},{3,11},{4,12},{5,13},{6,14},{7,15},{8,0},{9,1},... | collective-permute-start | bytes 196616 | tf_op jit(solution)/shard_map/ppermute | solution.py:344
  47.9 4.0 %collective-permute-start.19 = (bf16[128,128]{1,0:T(8,128)(2,1)S(1)}, bf16[128,128]{1,0:T(8,128)(2,1)S(1)}, u32[]{:S(2)}, u32[]{:S(2)}) collective-permute-start(bf16[128,128]{1,0:T(8,128)(2,1)S(1)} %add.33.wg_ref), channel_id=1, source_target_pairs={{0,4},{1,2},{2,1},{3,7},{4,0},{5,6},{6,5},{7,3},{8,12},{9,10},{10,... | collective-permute-start | bytes 98312 | tf_op jit(solution)/shard_map/ppermute | solution.py:344
  51.9 1.8 %collective-permute-start.20 = (bf16[128,384]{1,0:T(8,128)(2,1)S(1)}, bf16[128,384]{1,0:T(8,128)(2,1)S(1)}, u32[]{:S(2)}, u32[]{:S(2)}) collective-permute-start(bf16[128,384]{1,0:T(8,128)(2,1)S(1)} %line_sum.1.own_ref), channel_id=1, source_target_pairs={{0,2},{1,3},{2,0},{3,1},{4,6},{5,7},{6,4},{7,5},{8,10},{9,11},{10,... | collective-permute-start | bytes 294920 | tf_op jit(solution)/shard_map/ppermute | solution.py:344

commit v9 on v8

--- a/solution.py
+++ b/solution.py
@@ -388,7 +388,7 @@
     back_b = send(passed_b, lay.along(False))
     wg = add(wg, got_w1, mark_b)
     got_w2 = send(wg, lay.in_class(near))
-    two, three, mark_c = second_sum(back_a, kept_a, jnp.bfloat16, back)
+    two, three, mark_c = second_sum(back_a, kept_a, jnp.bfloat16, mark_a)
     three = send(three, lay.in_class(3 * near))
     two = send(two, lay.in_class(2 * near))
     zero, one, mark_d = second_sum(back_b, kept_b, jnp.float32, mark_c)

time: 54.6 us -> 55.3 us (1.013)
  starting transfers between devices: 31.1 us -> 32 us
  Pallas kernels: 7.48 us -> 6.84 us
    ppermute x21, starting transfers between devices: 31.1 us -> 32 us  [send(): return lax.ppermute(value, AXES, route)]
    pallas_call x2, Pallas kernels: 0.7 us -> 0.09 us  [first_sum(): pl.pallas_call(functools.partial(first_sum_kernel, start, size), in_specs...]
  transfers between devices with their start and end apart: 21 -> 21, of which waited for: 11 -> 11; matrix products, arithmetic and copies ran while one was open for 3% -> 3% of each run, Pallas kernels for 11% -> 9%
where the time goes in v9:
time: 55.3 us; the launch traced here: 55.2 us
  starting transfers between devices  32 us (58%)
  waiting for transfers between devices  14 us (25%)
  Pallas kernels  6.84 us (12%)
  other arithmetic  0.86 us (2%)
  between operations  0.77 us (1%)
  local copies, waits for them, and re-layouts  0.69 us (1%)
    ppermute x21, starting transfers between devices, send(): return lax.ppermute(value, AXES, route)  32 us
    ppermute x21, waiting for transfers between devices, send(): return lax.ppermute(value, AXES, route)  14 us
    pallas_call x1, Pallas kernels, dense_blocks(): pl.pallas_call(functools.partial(dense_kernel, blocks, near, halves), in_...  2.98 us
    pallas_call x2, Pallas kernels, aggregate(): pl.pallas_call(functools.partial(aggregate_kernel, spans, len(given) - le...  1.42 us
  transfers between devices with their start and end apart: 21, of which 11 were waited for; matrix products, arithmetic and copies ran while one was open for 3% of the time, Pallas kernels for 9%

profile of v9, /device:TPU:0, one launch (start us, length us, event | category | flops | bytes accessed | tf_op | source)
XLA Modules:
  0.0 55.2 jit_solution(1910118147330677163)
XLA Ops:
  0.6 4.1 %collective-permute-start.2 = (bf16[512,128]{1,0:T(8,128)(2,1)}, bf16[512,128]{1,0:T(8,128)(2,1)S(1)}, u32[]{:S(2)}, u32[]{:S(2)}) collective-permute-start(bf16[512,128]{1,0:T(8,128)(2,1)} %param.6), channel_id=1, source_target_pairs={{0,16},{1,19},{2,18},{3,17},{4,20},{5,23},{6,22},{7,21},{8,24},{9,... | collective-permute-start | bytes 393224 | tf_op jit(solution)/shard_map/ppermute | solution.py:344
  4.7 1.6 %collective-permute-start.3 = (bf16[512,128]{1,0:T(8,128)(2,1)}, bf16[512,128]{1,0:T(8,128)(2,1)S(1)}, u32[]{:S(2)}, u32[]{:S(2)}) collective-permute-start(bf16[512,128]{1,0:T(8,128)(2,1)} %param.6), channel_id=1, source_target_pairs={{0,8},{1,11},{2,10},{3,9},{4,12},{5,15},{6,14},{7,13},{8,0},{9,3},... | collective-permute-start | bytes 393224 | tf_op jit(solution)/shard_map/ppermute | solution.py:344
  6.3 1.6 %collective-permute-start = (bf16[512,128]{1,0:T(8,128)(2,1)}, bf16[512,128]{1,0:T(8,128)(2,1)S(1)}, u32[]{:S(2)}, u32[]{:S(2)}) collective-permute-start(bf16[512,128]{1,0:T(8,128)(2,1)} %param.6), channel_id=1, source_target_pairs={{0,0},{1,3},{2,2},{3,1},{4,4},{5,7},{6,6},{7,5},{8,8},{9,11},{10,1... | collective-permute-start | bytes 393224 | tf_op jit(solution)/shard_map/ppermute | solution.py:344
  7.9 1.5 %collective-permute-start.1 = (bf16[512,128]{1,0:T(8,128)(2,1)}, bf16[512,128]{1,0:T(8,128)(2,1)S(1)}, u32[]{:S(2)}, u32[]{:S(2)}) collective-permute-start(bf16[512,128]{1,0:T(8,128)(2,1)} %param.6), channel_id=1, source_target_pairs={{0,4},{1,7},{2,6},{3,5},{4,0},{5,3},{6,2},{7,1},{8,12},{9,15},{10,... | collective-permute-start | bytes 393224 | tf_op jit(solution)/shard_map/ppermute | solution.py:344
  9.4 1.7 %collective-permute-start.8 = (bf16[256,256]{1,0:T(8,128)(2,1)}, bf16[256,256]{1,0:T(8,128)(2,1)S(1)}, u32[]{:S(2)}, u32[]{:S(2)}) collective-permute-start(bf16[256,256]{1,0:T(8,128)(2,1)} %cot_ref.1), channel_id=1, source_target_pairs={{0,1},{1,0},{2,3},{3,2},{4,5},{5,4},{6,7},{7,6},{8,9},{9,8},{10,11... | collective-permute-start | bytes 393224 | tf_op jit(solution)/shard_map/ppermute | solution.py:344
  11.1 0.2 collective-permute-done.2
  11.4 0.2 collective-permute-done.3
  11.6 1.6 %collective-permute-start.4 = (bf16[1024,128]{1,0:T(8,128)(2,1)S(1)}, bf16[1024,128]{1,0:T(8,128)(2,1)S(1)}, u32[]{:S(2)}, u32[]{:S(2)}) collective-permute-start(bf16[1024,128]{1,0:T(8,128)(2,1)S(1)} %constant_dynamic-update-slice_fusion.refs_2_), channel_id=1, source_target_pairs={{0,4},{1,5},{2,6},{3,7},{4,0},{5,1},{6,2},{7,3},{8,12},{9,13},{10,... | collective-permute-start | bytes 786440 | tf_op jit(solution)/shard_map/ppermute | solution.py:344
  13.2 1.4 %collective-permute-start.5 = (bf16[512,128]{1,0:T(8,128)(2,1)S(1)}, bf16[512,128]{1,0:T(8,128)(2,1)S(1)}, u32[]{:S(2)}, u32[]{:S(2)}) collective-permute-start(bf16[512,128]{1,0:T(8,128)(2,1)S(1)} %collective-permute-done.2), channel_id=1, source_target_pairs={{0,8},{1,9},{2,10},{3,11},{4,12},{5,13},{6,14},{7,15},{8,0},{9,1},... | collective-permute-start | bytes 393224 | tf_op jit(solution)/shard_map/ppermute | solution.py:344
  14.6 0.8 %bitcast_select_fusion = s32[8,12]{1,0:T(8,128)S(1)} fusion(s32[1,1,8,12]{3,2,1,0:T(8,128)} %param.9, s32[]{:T(128)S(6)} %mul.14, s32[8]{0:T(128)} %bitcast.5), kind=kLoop, calls=%fused_computation.13 | loop fusion | flops 288 | bytes 804 | tf_op jit(solution)/shard_map/jit(_where)/select_n | solution.py:354
  15.4 2.8 %collective-permute-done.5.refs_4_ = bf16[512,128]{1,0:T(8,128)(2,1)S(1)} collective-permute-done((bf16[512,128]{1,0:T(8,128)(2,1)S(1)}, bf16[512,128]{1,0:T(8,128)(2,1)S(1)}, u32[]{:S(2)}, u32[]{:S(2)}) %collective-permute-start.5) | collective-permute-done | bytes 131104 | tf_op jit(solution)/shard_map/ppermute | solution.py:344
  18.2 0.5 collective-permute-start.6
  18.7 0.1 pad_add_fusion.table
  18.7 3.0 %dense_blocks.1.dense_ref = bf16[4,512,1024]{2,1,0:T(8,128)(2,1)S(1)} custom-call(s32[8,13]{1,0:T(8,128)S(1)} %pad_add_fusion.table, bf16[8,12,128,128]{3,2,1,0:T(8,128)(2,1)} %bitcast.4), custom_call_target="tpu_custom_call" | custom-call | tf_op jit(solution)/shard_map/dense_blocks/pallas_call | solution.py:82
  21.7 0.0 copy-start
  21.7 0.0 copy-start.1
  21.7 0.0 collective-permute-done.refs_0_
  21.8 0.0 collective-permute-done.1.refs_1_
  21.8 0.0 collective-permute-done.4.refs_3_
  21.8 1.1 %aggregate.2.refs_0_ = f32[512,128]{1,0:T(8,128)S(1)} custom-call(bf16[4,512,1024]{2,1,0:T(8,128)(2,1)S(1)} %dense_blocks.1.dense_ref, bf16[512,128]{1,0:T(8,128)(2,1)S(1)} %collective-permute-done.refs_0_, bf16[512,128]{1,0:T(8,128)(2,1)S(1)} %collective-permute-done.1.refs_1_, bf16[1024,128]{1,0:T(8,128)(2,1)S(1)} %constant_dynamic-update-slice_fusion.refs_2_, ...), custom_call_target="tpu_custom_call" | custom-call | tf_op jit(solution)/shard_map/aggregate/pallas_call | solution.py:118
  22.9 0.2 collective-permute-done.6.refs_1_
  23.1 0.3 aggregate.3.own_ref
  23.5 2.2 %collective-permute-start.7 = (bf16[512,128]{1,0:T(8,128)(2,1)S(1)}, bf16[512,128]{1,0:T(8,128)(2,1)S(1)}, u32[]{:S(2)}, u32[]{:S(2)}) collective-permute-start(bf16[512,128]{1,0:T(8,128)(2,1)S(1)} %aggregate.3.own_ref), channel_id=1, source_target_pairs={{0,1},{1,0},{2,3},{3,2},{4,5},{5,4},{6,7},{7,6},{8,9},{9,8},{10,11... | collective-permute-start | bytes 393224 | tf_op jit(solution)/shard_map/ppermute | solution.py:344
  25.7 0.0 collective-permute-done.8.far_cot_ref
  25.7 2.9 %collective-permute-done.7.other_ref = bf16[512,128]{1,0:T(8,128)(2,1)S(1)} collective-permute-done((bf16[512,128]{1,0:T(8,128)(2,1)S(1)}, bf16[512,128]{1,0:T(8,128)(2,1)S(1)}, u32[]{:S(2)}, u32[]{:S(2)}) %collective-permute-start.7) | collective-permute-done | bytes 131104 | tf_op jit(solution)/shard_map/ppermute | solution.py:344
  28.7 0.9 %turn.1 = (bf16[256,256]{1,0:T(8,128)(2,1)S(1)}, bf16[128,512]{1,0:T(8,128)(2,1)S(1)}, bf16[128,1024]{1,0:T(8,128)(2,1)S(1)}, bf16[512,128]{1,0:T(8,128)(2,1)S(1)}, bf16[512,256]{1,0:T(8,128)(2,1)S(1)}) custom-call(bf16[512,128]{1,0:T(8,128)(2,1)S(1)} %aggregate.3.own_ref, bf16[512,128]{1,0:T(8,128)(2,1)S(1)} %collective-permute-done.7.other_ref, ...), custom_call_target="tpu_custom_call" | custom-call | tf_op jit(solution)/shard_map/turn/pallas_call | solution.py:154
  29.5 0.1 collective-permute-start.9
  29.6 0.6 %rest_terms.1 = (bf16[128,128]{1,0:T(8,128)(2,1)S(1)}, bf16[128,1024]{1,0:T(8,128)(2,1)S(1)}, f32[2,128,1024]{2,1,0:T(8,128)S(1)}) custom-call(bf16[128,512]{1,0:T(8,128)(2,1)S(1)} %get-tuple-element.27.back_ref.after_ref, bf16[4,512,1024]{2,1,0:T(8,128)(2,1)S(1)} %dense_blocks.1.dense_ref, bf16[512,128]{1,0:T(8,128)(2,1)S(1)} %get-tuple-element.28.g_ref, ...), custom_call_target="tpu_custom_call" | custom-call | tf_op jit(solution)/shard_map/rest_terms/pallas_call | solution.py:185
  30.2 1.8 %collective-permute-start.13 = (bf16[128,1024]{1,0:T(8,128)(2,1)S(1)}, bf16[128,1024]{1,0:T(8,128)(2,1)S(1)}, u32[]{:S(2)}, u32[]{:S(2)}) collective-permute-start(bf16[128,1024]{1,0:T(8,128)(2,1)S(1)} %get-tuple-element.36), channel_id=1, source_target_pairs={{0,3},{1,5},{2,6},{3,0},{4,7},{5,1},{6,2},{7,4},{8,11},{9,13},{10,... | collective-permute-start | bytes 786440 | tf_op jit(solution)/shard_map/ppermute | solution.py:344
  32.0 2.2 %collective-permute-start.14 = (bf16[128,128]{1,0:T(8,128)(2,1)S(1)}, bf16[128,128]{1,0:T(8,128)(2,1)S(1)}, u32[]{:S(2)}, u32[]{:S(2)}) collective-permute-start(bf16[128,128]{1,0:T(8,128)(2,1)S(1)} %get-tuple-element.37.a_ref), channel_id=1, source_target_pairs={{0,16},{1,17},{2,18},{3,19},{4,20},{5,21},{6,22},{7,23},{8,24},{9,... | collective-permute-start | bytes 98312 | tf_op jit(solution)/shard_map/ppermute | solution.py:344
  34.2 1.2 %collective-permute-done.9.got_ref = bf16[128,1024]{1,0:T(8,128)(2,1)S(1)} collective-permute-done((bf16[128,1024]{1,0:T(8,128)(2,1)S(1)}, bf16[128,1024]{1,0:T(8,128)(2,1)S(1)}, u32[]{:S(2)}, u32[]{:S(2)}) %collective-permute-start.9) | collective-permute-done | bytes 262176 | tf_op jit(solution)/shard_map/ppermute | solution.py:344
  35.4 1.3 %collective-permute-start.10 = (bf16[128,512]{1,0:T(8,128)(2,1)S(1)}, bf16[128,512]{1,0:T(8,128)(2,1)S(1)}, u32[]{:S(2)}, u32[]{:S(2)}) collective-permute-start(bf16[128,512]{1,0:T(8,128)(2,1)S(1)} %get-tuple-element.31), channel_id=1, source_target_pairs={{0,4},{1,2},{2,1},{3,7},{4,0},{5,6},{6,5},{7,3},{8,12},{9,10},{10,... | collective-permute-start | bytes 393224 | tf_op jit(solution)/shard_map/ppermute | solution.py:344
  36.7 0.1 collective-permute-done.14.after_ref.b_ref
  36.8 1.4 %collective-permute-done.13.got_ref = bf16[128,1024]{1,0:T(8,128)(2,1)S(1)} collective-permute-done((bf16[128,1024]{1,0:T(8,128)(2,1)S(1)}, bf16[128,1024]{1,0:T(8,128)(2,1)S(1)}, u32[]{:S(2)}, u32[]{:S(2)}) %collective-permute-start.13) | collective-permute-done | bytes 262176 | tf_op jit(solution)/shard_map/ppermute | solution.py:344
  38.2 1.3 %collective-permute-start.15 = (bf16[128,512]{1,0:T(8,128)(2,1)S(1)}, bf16[128,512]{1,0:T(8,128)(2,1)S(1)}, u32[]{:S(2)}, u32[]{:S(2)}) collective-permute-start(bf16[128,512]{1,0:T(8,128)(2,1)S(1)} %get-tuple-element.38), channel_id=1, source_target_pairs={{0,4},{1,2},{2,1},{3,7},{4,0},{5,6},{6,5},{7,3},{8,12},{9,10},{10,... | collective-permute-start | bytes 393224 | tf_op jit(solution)/shard_map/ppermute | solution.py:344
  39.5 1.6 %collective-permute-start.17 = (bf16[128,128]{1,0:T(8,128)(2,1)S(1)}, bf16[128,128]{1,0:T(8,128)(2,1)S(1)}, u32[]{:S(2)}, u32[]{:S(2)}) collective-permute-start(bf16[128,128]{1,0:T(8,128)(2,1)S(1)} %add.31.a_ref), channel_id=1, source_target_pairs={{0,8},{1,9},{2,10},{3,11},{4,12},{5,13},{6,14},{7,15},{8,0},{9,1},... | collective-permute-start | bytes 98312 | tf_op jit(solution)/shard_map/ppermute | solution.py:344
  41.1 0.0 collective-permute-done.10.got_ref
  41.1 2.8 %collective-permute-start.11 = (bf16[128,256]{1,0:T(8,128)(2,1)S(1)}, bf16[128,256]{1,0:T(8,128)(2,1)S(1)}, u32[]{:S(2)}, u32[]{:S(2)}) collective-permute-start(bf16[128,256]{1,0:T(8,128)(2,1)S(1)} %get-tuple-element.34), channel_id=1, source_target_pairs={{0,24},{1,25},{2,26},{3,27},{4,28},{5,29},{6,30},{7,31},{8,16},{9,... | collective-permute-start | bytes 196616 | tf_op jit(solution)/shard_map/ppermute | solution.py:344
  43.9 0.0 collective-permute-start.12
  43.9 0.7 %collective-permute-start.18 = (bf16[128,128]{1,0:T(8,128)(2,1)S(1)}, bf16[128,128]{1,0:T(8,128)(2,1)S(1)}, u32[]{:S(2)}, u32[]{:S(2)}) collective-permute-start(bf16[128,128]{1,0:T(8,128)(2,1)S(1)} %add.32.a_ref), channel_id=1, source_target_pairs={{0,3},{1,5},{2,6},{3,0},{4,7},{5,1},{6,2},{7,4},{8,11},{9,13},{10,... | collective-permute-start | bytes 98312 | tf_op jit(solution)/shard_map/ppermute | solution.py:344
  44.7 1.1 %collective-permute-start.16 = (bf16[128,256]{1,0:T(8,128)(2,1)S(1)}, bf16[128,256]{1,0:T(8,128)(2,1)S(1)}, u32[]{:S(2)}, u32[]{:S(2)}) collective-permute-start(bf16[128,256]{1,0:T(8,128)(2,1)S(1)} %get-tuple-element.41), channel_id=1, source_target_pairs={{0,8},{1,9},{2,10},{3,11},{4,12},{5,13},{6,14},{7,15},{8,0},{9,1},... | collective-permute-start | bytes 196616 | tf_op jit(solution)/shard_map/ppermute | solution.py:344
  45.8 1.5 %collective-permute-done.18.b_ref = bf16[128,128]{1,0:T(8,128)(2,1)S(1)} collective-permute-done((bf16[128,128]{1,0:T(8,128)(2,1)S(1)}, bf16[128,128]{1,0:T(8,128)(2,1)S(1)}, u32[]{:S(2)}, u32[]{:S(2)}) %collective-permute-start.18) | collective-permute-done | bytes 32800 | tf_op jit(solution)/shard_map/ppermute | solution.py:344
  47.3 1.2 %collective-permute-start.19 = (bf16[128,128]{1,0:T(8,128)(2,1)S(1)}, bf16[128,128]{1,0:T(8,128)(2,1)S(1)}, u32[]{:S(2)}, u32[]{:S(2)}) collective-permute-start(bf16[128,128]{1,0:T(8,128)(2,1)S(1)} %add.33.wg_ref), channel_id=1, source_target_pairs={{0,4},{1,2},{2,1},{3,7},{4,0},{5,6},{6,5},{7,3},{8,12},{9,10},{10,... | collective-permute-start | bytes 98312 | tf_op jit(solution)/shard_map/ppermute | solution.py:344
  48.6 3.1 %collective-permute-done.12.two_ref = bf16[128,256]{1,0:T(8,128)(2,1)S(1)} collective-permute-done((bf16[128,256]{1,0:T(8,128)(2,1)S(1)}, bf16[128,256]{1,0:T(8,128)(2,1)S(1)}, u32[]{:S(2)}, u32[]{:S(2)}) %collective-permute-start.12) | collective-permute-done | bytes 65568 | tf_op jit(solution)/shard_map/ppermute | solution.py:344
  51.7 1.8 %collective-permute-start.20 = (bf16[128,384]{1,0:T(8,128)(2,1)S(1)}, bf16[128,384]{1,0:T(8,128)(2,1)S(1)}, u32[]{:S(2)}, u32[]{:S(2)}) collective-permute-start(bf16[128,384]{1,0:T(8,128)(2,1)S(1)} %line_sum.1.own_ref), channel_id=1, source_target_pairs={{0,2},{1,3},{2,0},{3,1},{4,6},{5,7},{6,4},{7,5},{8,10},{9,11},{10,... | collective-permute-start | bytes 294920 | tf_op jit(solution)/shard_map/ppermute | solution.py:344
  53.5 0.7 %copy.10 = bf16[256,256]{1,0:T(8,128)(2,1)} copy(bf16[256,256]{1,0:T(8,128)(2,1)S(1)} %get-tuple-element.47) | data formatting | bytes 262144
  54.1 0.3 collective-permute-done.20.got_ref
  54.4 0.7 %finish.1 = (bf16[256,128]{1,0:T(8,128)(2,1)}, f32[128,256]{1,0:T(8,128)}) custom-call(bf16[128,384]{1,0:T(8,128)(2,1)S(1)} %line_sum.1.own_ref, bf16[128,384]{1,0:T(8,128)(2,1)S(1)} %collective-permute-done.20.got_ref), custom_call_target="tpu_custom_call" | custom-call | tf_op jit(solution)/shard_map/finish/pallas_call | solution.py:292
  (18 shorter events, 0.3 us)
Async XLA Ops:
  0.6 10.7 %collective-permute-start.2 = (bf16[512,128]{1,0:T(8,128)(2,1)}, bf16[512,128]{1,0:T(8,128)(2,1)S(1)}, u32[]{:S(2)}, u32[]{:S(2)}) collective-permute-start(bf16[512,128]{1,0:T(8,128)(2,1)} %param.6), channel_id=1, source_target_pairs={{0,16},{1,19},{2,18},{3,17},{4,20},{5,23},{6,22},{7,21},{8,24},{9,... | collective-permute-start | bytes 393224 | tf_op jit(solution)/shard_map/ppermute | solution.py:344
  4.7 6.8 %collective-permute-start.3 = (bf16[512,128]{1,0:T(8,128)(2,1)}, bf16[512,128]{1,0:T(8,128)(2,1)S(1)}, u32[]{:S(2)}, u32[]{:S(2)}) collective-permute-start(bf16[512,128]{1,0:T(8,128)(2,1)} %param.6), channel_id=1, source_target_pairs={{0,8},{1,11},{2,10},{3,9},{4,12},{5,15},{6,14},{7,13},{8,0},{9,3},... | collective-permute-start | bytes 393224 | tf_op jit(solution)/shard_map/ppermute | solution.py:344
  6.3 15.4 %collective-permute-start = (bf16[512,128]{1,0:T(8,128)(2,1)}, bf16[512,128]{1,0:T(8,128)(2,1)S(1)}, u32[]{:S(2)}, u32[]{:S(2)}) collective-permute-start(bf16[512,128]{1,0:T(8,128)(2,1)} %param.6), channel_id=1, source_target_pairs={{0,0},{1,3},{2,2},{3,1},{4,4},{5,7},{6,6},{7,5},{8,8},{9,11},{10,1... | collective-permute-start | bytes 393224 | tf_op jit(solution)/shard_map/ppermute | solution.py:344
  7.9 13.9 %collective-permute-start.1 = (bf16[512,128]{1,0:T(8,128)(2,1)}, bf16[512,128]{1,0:T(8,128)(2,1)S(1)}, u32[]{:S(2)}, u32[]{:S(2)}) collective-permute-start(bf16[512,128]{1,0:T(8,128)(2,1)} %param.6), channel_id=1, source_target_pairs={{0,4},{1,7},{2,6},{3,5},{4,0},{5,3},{6,2},{7,1},{8,12},{9,15},{10,... | collective-permute-start | bytes 393224 | tf_op jit(solution)/shard_map/ppermute | solution.py:344
  9.4 16.3 %collective-permute-start.8 = (bf16[256,256]{1,0:T(8,128)(2,1)}, bf16[256,256]{1,0:T(8,128)(2,1)S(1)}, u32[]{:S(2)}, u32[]{:S(2)}) collective-permute-start(bf16[256,256]{1,0:T(8,128)(2,1)} %cot_ref.1), channel_id=1, source_target_pairs={{0,1},{1,0},{2,3},{3,2},{4,5},{5,4},{6,7},{7,6},{8,9},{9,8},{10,11... | collective-permute-start | bytes 393224 | tf_op jit(solution)/shard_map/ppermute | solution.py:344
  11.6 10.2 %collective-permute-start.4 = (bf16[1024,128]{1,0:T(8,128)(2,1)S(1)}, bf16[1024,128]{1,0:T(8,128)(2,1)S(1)}, u32[]{:S(2)}, u32[]{:S(2)}) collective-permute-start(bf16[1024,128]{1,0:T(8,128)(2,1)S(1)} %constant_dynamic-update-slice_fusion.refs_2_), channel_id=1, source_target_pairs={{0,4},{1,5},{2,6},{3,7},{4,0},{5,1},{6,2},{7,3},{8,12},{9,13},{10,... | collective-permute-start | bytes 786440 | tf_op jit(solution)/shard_map/ppermute | solution.py:344
  13.2 5.0 %collective-permute-start.5 = (bf16[512,128]{1,0:T(8,128)(2,1)S(1)}, bf16[512,128]{1,0:T(8,128)(2,1)S(1)}, u32[]{:S(2)}, u32[]{:S(2)}) collective-permute-start(bf16[512,128]{1,0:T(8,128)(2,1)S(1)} %collective-permute-done.2), channel_id=1, source_target_pairs={{0,8},{1,9},{2,10},{3,11},{4,12},{5,13},{6,14},{7,15},{8,0},{9,1},... | collective-permute-start | bytes 393224 | tf_op jit(solution)/shard_map/ppermute | solution.py:344
  18.2 5.0 %collective-permute-start.6 = (bf16[512,128]{1,0:T(8,128)(2,1)S(1)}, bf16[512,128]{1,0:T(8,128)(2,1)S(1)}, u32[]{:S(2)}, u32[]{:S(2)}) collective-permute-start(bf16[512,128]{1,0:T(8,128)(2,1)S(1)} %collective-permute-done.5.refs_4_), channel_id=1, source_target_pairs={{0,4},{1,5},{2,6},{3,7},{4,0},{5,1},{6,2},{7,3},{8,12},{9,13},{10,... | collective-permute-start | bytes 393224 | tf_op jit(solution)/shard_map/ppermute | solution.py:344
  21.7 6.9 %copy-start = (bf16[256,256]{1,0:T(8,128)(2,1)S(1)}, bf16[256,256]{1,0:T(8,128)(2,1)}, u32[]{:S(2)}) copy-start(bf16[256,256]{1,0:T(8,128)(2,1)} %cot_ref.1) | copy-start | bytes 393220
  21.7 6.9 %copy-start.1 = (bf16[128,256]{1,0:T(8,128)(2,1)S(1)}, bf16[128,256]{1,0:T(8,128)(2,1)}, u32[]{:S(2)}) copy-start(bf16[128,256]{1,0:T(8,128)(2,1)} %weight_ref.1) | copy-start | bytes 196612
  23.5 5.2 %collective-permute-start.7 = (bf16[512,128]{1,0:T(8,128)(2,1)S(1)}, bf16[512,128]{1,0:T(8,128)(2,1)S(1)}, u32[]{:S(2)}, u32[]{:S(2)}) collective-permute-start(bf16[512,128]{1,0:T(8,128)(2,1)S(1)} %aggregate.3.own_ref), channel_id=1, source_target_pairs={{0,1},{1,0},{2,3},{3,2},{4,5},{5,4},{6,7},{7,6},{8,9},{9,8},{10,11... | collective-permute-start | bytes 393224 | tf_op jit(solution)/shard_map/ppermute | solution.py:344
  29.5 5.9 %collective-permute-start.9 = (bf16[128,1024]{1,0:T(8,128)(2,1)S(1)}, bf16[128,1024]{1,0:T(8,128)(2,1)S(1)}, u32[]{:S(2)}, u32[]{:S(2)}) collective-permute-start(bf16[128,1024]{1,0:T(8,128)(2,1)S(1)} %get-tuple-element.26), channel_id=1, source_target_pairs={{0,3},{1,5},{2,6},{3,0},{4,7},{5,1},{6,2},{7,4},{8,11},{9,13},{10,... | collective-permute-start | bytes 786440 | tf_op jit(solution)/shard_map/ppermute | solution.py:344
  30.2 8.0 %collective-permute-start.13 = (bf16[128,1024]{1,0:T(8,128)(2,1)S(1)}, bf16[128,1024]{1,0:T(8,128)(2,1)S(1)}, u32[]{:S(2)}, u32[]{:S(2)}) collective-permute-start(bf16[128,1024]{1,0:T(8,128)(2,1)S(1)} %get-tuple-element.36), channel_id=1, source_target_pairs={{0,3},{1,5},{2,6},{3,0},{4,7},{5,1},{6,2},{7,4},{8,11},{9,13},{10,... | collective-permute-start | bytes 786440 | tf_op jit(solution)/shard_map/ppermute | solution.py:344
  32.0 4.8 %collective-permute-start.14 = (bf16[128,128]{1,0:T(8,128)(2,1)S(1)}, bf16[128,128]{1,0:T(8,128)(2,1)S(1)}, u32[]{:S(2)}, u32[]{:S(2)}) collective-permute-start(bf16[128,128]{1,0:T(8,128)(2,1)S(1)} %get-tuple-element.37.a_ref), channel_id=1, source_target_pairs={{0,16},{1,17},{2,18},{3,19},{4,20},{5,21},{6,22},{7,23},{8,24},{9,... | collective-permute-start | bytes 98312 | tf_op jit(solution)/shard_map/ppermute | solution.py:344
  35.4 5.7 %collective-permute-start.10 = (bf16[128,512]{1,0:T(8,128)(2,1)S(1)}, bf16[128,512]{1,0:T(8,128)(2,1)S(1)}, u32[]{:S(2)}, u32[]{:S(2)}) collective-permute-start(bf16[128,512]{1,0:T(8,128)(2,1)S(1)} %get-tuple-element.31), channel_id=1, source_target_pairs={{0,4},{1,2},{2,1},{3,7},{4,0},{5,6},{6,5},{7,3},{8,12},{9,10},{10,... | collective-permute-start | bytes 393224 | tf_op jit(solution)/shard_map/ppermute | solution.py:344
  38.2 6.4 %collective-permute-start.15 = (bf16[128,512]{1,0:T(8,128)(2,1)S(1)}, bf16[128,512]{1,0:T(8,128)(2,1)S(1)}, u32[]{:S(2)}, u32[]{:S(2)}) collective-permute-start(bf16[128,512]{1,0:T(8,128)(2,1)S(1)} %get-tuple-element.38), channel_id=1, source_target_pairs={{0,4},{1,2},{2,1},{3,7},{4,0},{5,6},{6,5},{7,3},{8,12},{9,10},{10,... | collective-permute-start | bytes 393224 | tf_op jit(solution)/shard_map/ppermute | solution.py:344
  39.5 4.4 %collective-permute-start.17 = (bf16[128,128]{1,0:T(8,128)(2,1)S(1)}, bf16[128,128]{1,0:T(8,128)(2,1)S(1)}, u32[]{:S(2)}, u32[]{:S(2)}) collective-permute-start(bf16[128,128]{1,0:T(8,128)(2,1)S(1)} %add.31.a_ref), channel_id=1, source_target_pairs={{0,8},{1,9},{2,10},{3,11},{4,12},{5,13},{6,14},{7,15},{8,0},{9,1},... | collective-permute-start | bytes 98312 | tf_op jit(solution)/shard_map/ppermute | solution.py:344
  41.1 7.5 %collective-permute-start.11 = (bf16[128,256]{1,0:T(8,128)(2,1)S(1)}, bf16[128,256]{1,0:T(8,128)(2,1)S(1)}, u32[]{:S(2)}, u32[]{:S(2)}) collective-permute-start(bf16[128,256]{1,0:T(8,128)(2,1)S(1)} %get-tuple-element.34), channel_id=1, source_target_pairs={{0,24},{1,25},{2,26},{3,27},{4,28},{5,29},{6,30},{7,31},{8,16},{9,... | collective-permute-start | bytes 196616 | tf_op jit(solution)/shard_map/ppermute | solution.py:344
  43.9 7.7 %collective-permute-start.12 = (bf16[128,256]{1,0:T(8,128)(2,1)S(1)}, bf16[128,256]{1,0:T(8,128)(2,1)S(1)}, u32[]{:S(2)}, u32[]{:S(2)}) collective-permute-start(bf16[128,256]{1,0:T(8,128)(2,1)S(1)} %get-tuple-element.35), channel_id=1, source_target_pairs={{0,16},{1,17},{2,18},{3,19},{4,20},{5,21},{6,22},{7,23},{8,24},{9,... | collective-permute-start | bytes 196616 | tf_op jit(solution)/shard_map/ppermute | solution.py:344
  43.9 3.4 %collective-permute-start.18 = (bf16[128,128]{1,0:T(8,128)(2,1)S(1)}, bf16[128,128]{1,0:T(8,128)(2,1)S(1)}, u32[]{:S(2)}, u32[]{:S(2)}) collective-permute-start(bf16[128,128]{1,0:T(8,128)(2,1)S(1)} %add.32.a_ref), channel_id=1, source_target_pairs={{0,3},{1,5},{2,6},{3,0},{4,7},{5,1},{6,2},{7,4},{8,11},{9,13},{10,... | collective-permute-start | bytes 98312 | tf_op jit(solution)/shard_map/ppermute | solution.py:344
  44.7 7.0 %collective-permute-start.16 = (bf16[128,256]{1,0:T(8,128)(2,1)S(1)}, bf16[128,256]{1,0:T(8,128)(2,1)S(1)}, u32[]{:S(2)}, u32[]{:S(2)}) collective-permute-start(bf16[128,256]{1,0:T(8,128)(2,1)S(1)} %get-tuple-element.41), channel_id=1, source_target_pairs={{0,8},{1,9},{2,10},{3,11},{4,12},{5,13},{6,14},{7,15},{8,0},{9,1},... | collective-permute-start | bytes 196616 | tf_op jit(solution)/shard_map/ppermute | solution.py:344
  47.3 4.3 %collective-permute-start.19 = (bf16[128,128]{1,0:T(8,128)(2,1)S(1)}, bf16[128,128]{1,0:T(8,128)(2,1)S(1)}, u32[]{:S(2)}, u32[]{:S(2)}) collective-permute-start(bf16[128,128]{1,0:T(8,128)(2,1)S(1)} %add.33.wg_ref), channel_id=1, source_target_pairs={{0,4},{1,2},{2,1},{3,7},{4,0},{5,6},{6,5},{7,3},{8,12},{9,10},{10,... | collective-permute-start | bytes 98312 | tf_op jit(solution)/shard_map/ppermute | solution.py:344
  51.7 2.7 %collective-permute-start.20 = (bf16[128,384]{1,0:T(8,128)(2,1)S(1)}, bf16[128,384]{1,0:T(8,128)(2,1)S(1)}, u32[]{:S(2)}, u32[]{:S(2)}) collective-permute-start(bf16[128,384]{1,0:T(8,128)(2,1)S(1)} %line_sum.1.own_ref), channel_id=1, source_target_pairs={{0,2},{1,3},{2,0},{3,1},{4,6},{5,7},{6,4},{7,5},{8,10},{9,11},{10,... | collective-permute-start | bytes 294920 | tf_op jit(solution)/shard_map/ppermute | solution.py:344
